TPU v7x, 512 devices: a whole 4x4x16 slice. The times are simulated.
512 devices in a mesh: hid: 32 (over z, y_lo), wid: 16 (over y_hi, x, core).
Axes of the slice: x: 4, y: 4 (y_hi: 2, y_lo: 2; y = y_hi * 2 + y_lo), z: 16, core: 2. Of those that a mesh axis runs over, the one named last changes fastest.
Arguments:
- inputs: bfloat16 [512, 6144], P('hid', 'wid'), may hold values from -420 to 420
- cotangent: bfloat16 [512, 6144], P('hid', 'wid'), may hold values from -6 to 6
- norm_gain: float32 [6144], P('wid'), may hold values from 0.5 to 1.5
- qkv_weight: bfloat16 [6144, 3, 4096], P('wid', None, 'hid'), may hold values from -0.078125 to 0.078125
- out_weight: bfloat16 [4096, 6144], P('hid', 'wid'), may hold values from -0.375 to 0.375
- up_weight: bfloat16 [6144, 16384], P('wid', 'hid'), may hold values from -0.078125 to 0.078125
- down_weight: bfloat16 [16384, 6144], P('hid', 'wid'), may hold values from -0.046875 to 0.046875
- query_gain: float32 [128], replicated, may hold values from 0.5 to 1.5
- key_gain: float32 [128], replicated, may hold values from 0.5 to 1.5
Outputs:
- input_grad: bfloat16 [512, 6144], P('hid', 'wid')
- qkv_grad: bfloat16 [6144, 3, 4096], P('wid', None, 'hid')
- out_grad: bfloat16 [4096, 6144], P('hid', 'wid')
- up_grad: bfloat16 [6144, 16384], P('wid', 'hid')
- down_grad: bfloat16 [16384, 6144], P('hid', 'wid')
All inputs are finite; a program needn't handle non-finite values.
Results may differ from a plain program's by a relative error of at most 0.011.
Values may be sent and summed in bfloat16 or wider, within the bound.
No kernel may reach another device: no remote copies, remote signals or barrier semaphores. Data moves between devices by JAX's collectives and lax.ppermute only.
A program may use at most 64 MiB of HBM per device.

v0:
```python
import math

import jax
import jax.numpy as jnp
from jax import lax
from jax.sharding import PartitionSpec as P

HEAD_DIM = 128
PATCHES = 256


EPSILON = 1e-06


def combined_all(value, axis, join):
    pieces = jax.tree.map(lambda part: lax.all_gather(part, axis), value)
    head = jax.tree.map(lambda part: part[0], pieces)
    tail = jax.tree.map(lambda part: part[1:], pieces)
    subtotal, _ = lax.scan(lambda subtotal, share: (join(subtotal, share), None), head, tail)
    return subtotal


def product(form, left_arr, right_arr):
    return jnp.einsum(form, left_arr, right_arr, preferred_element_type=jnp.float32)


def head_norm(values, gain):
    centre = jnp.mean(values, axis=-1, keepdims=True)
    centred = values - centre
    inverse = lax.rsqrt(jnp.mean(centred * centred, axis=-1, keepdims=True) + EPSILON)
    unit_rows = centred * inverse
    return (unit_rows, inverse, unit_rows * gain)


def head_norm_back(upstream, unit_rows, inverse, gain):
    scaled = upstream * gain
    return inverse * (
        scaled
        - jnp.mean(scaled, axis=-1, keepdims=True)
        - unit_rows * jnp.mean(scaled * unit_rows, axis=-1, keepdims=True)
    )


def gelu_pair(pre_act, upstream):
    hidden, pullback = jax.vjp(jax.nn.gelu, pre_act)
    return (hidden.astype(jnp.bfloat16), pullback(upstream)[0].astype(jnp.bfloat16))


def merge_moments(first_part, second_part):
    first_count, first_mean, first_square = first_part
    second_count, second_mean, second_square = second_part
    joint_count = first_count + second_count
    offset = second_mean - first_mean
    return (
        joint_count,
        first_mean + offset * (second_count / joint_count),
        first_square + second_square + offset * offset * (first_count * second_count / joint_count),
    )


def attention_pair(qkv_rows, att_grad, query_gain, key_gain):
    tok_count = qkv_rows.shape[0]
    head_width = qkv_rows.shape[2]
    head_count = head_width // HEAD_DIM
    image_count = tok_count // PATCHES
    score_scale = 1.0 / math.sqrt(HEAD_DIM)

    def per_image(values):
        return values.reshape(image_count, PATCHES, head_count, HEAD_DIM)

    query_unit, query_inverse, query_normed = head_norm(per_image(qkv_rows[:, 0]), query_gain)
    key_unit, key_inverse, key_normed = head_norm(per_image(qkv_rows[:, 1]), key_gain)
    query_normed = query_normed.astype(jnp.bfloat16)
    key_normed = key_normed.astype(jnp.bfloat16)
    value_rows = per_image(qkv_rows[:, 2]).astype(jnp.bfloat16)
    scores = product("ipha,iqha->ihpq", query_normed, key_normed) * score_scale
    exponent = jnp.exp(scores)
    probs = exponent / jnp.sum(exponent, axis=-1, keepdims=True)
    probs_low = probs.astype(jnp.bfloat16)
    attended = (
        product("ihpq,iqha->ipha", probs_low, value_rows)
        .astype(jnp.bfloat16)
        .reshape(tok_count, head_width)
    )
    grad_rows = per_image(att_grad)
    probs_grad = product("ipha,iqha->ihpq", grad_rows, value_rows)
    value_grad = product("ihpq,ipha->iqha", probs_low, grad_rows)
    score_grad = (
        probs * (probs_grad - jnp.sum(probs * probs_grad, axis=-1, keepdims=True)) * score_scale
    ).astype(jnp.bfloat16)
    qn_grad = product("ihpq,iqha->ipha", score_grad, key_normed)
    kn_grad = product("ihpq,ipha->iqha", score_grad, query_normed)
    query_grad = head_norm_back(qn_grad, query_unit, query_inverse, query_gain)
    key_grad = head_norm_back(kn_grad, key_unit, key_inverse, key_gain)
    qkv_back = jnp.stack(
        [
            query_grad.reshape(tok_count, head_width),
            key_grad.reshape(tok_count, head_width),
            value_grad.reshape(tok_count, head_width),
        ],
        axis=1,
    ).astype(jnp.bfloat16)
    return (attended, qkv_back)


def local(
    inputs,
    cotangent,
    norm_gain,
    qkv_weight,
    out_weight,
    up_weight,
    down_weight,
    query_gain,
    key_gain,
):
    input_rows = inputs.astype(jnp.float32)
    row_centre = jnp.mean(input_rows, axis=-1)
    row_deviation = input_rows - row_centre[:, None]
    row_square = jnp.sum(row_deviation * row_deviation, axis=-1)
    width_count = jnp.full((1,), float(input_rows.shape[1]), jnp.float32)
    total_count, mean_all, square_all = combined_all(
        (width_count, row_centre, row_square), "wid", merge_moments
    )
    inverse = lax.rsqrt(square_all / total_count + EPSILON)[:, None]
    unit_rows = (input_rows - mean_all[:, None]) * inverse
    normed = (unit_rows * norm_gain).astype(jnp.bfloat16)
    normed_all, grad_all = (
        lax.all_gather(normed, "hid", axis=0, tiled=True),
        lax.all_gather(cotangent, "hid", axis=0, tiled=True),
    )
    pre_part = product("td,df->tf", normed_all, up_weight)
    qkv_part = product("td,dch->tch", normed_all, qkv_weight)
    hidden_part = product("td,fd->tf", grad_all, down_weight)
    att_part = product("td,hd->th", grad_all, out_weight)
    pre_act, qkv_rows, hidden_grad, att_sum = lax.psum(
        (pre_part, qkv_part, hidden_part, att_part), "wid"
    )
    hidden, pre_grad = gelu_pair(pre_act, hidden_grad)
    att_grad = att_sum.astype(jnp.bfloat16)
    attended, qkv_back = attention_pair(qkv_rows, att_grad, query_gain, key_gain)
    qkv_grad = product("td,tch->dch", normed_all, qkv_back).astype(jnp.bfloat16)
    out_grad = product("th,td->hd", attended, grad_all).astype(jnp.bfloat16)
    up_grad = product("td,tf->df", normed_all, pre_grad).astype(jnp.bfloat16)
    down_grad = product("tf,td->fd", hidden, grad_all).astype(jnp.bfloat16)
    normed_grad = lax.psum_scatter(
        product("tf,df->td", pre_grad, up_weight), "hid", scatter_dimension=0, tiled=True
    ) + lax.psum_scatter(
        product("tch,dch->td", qkv_back, qkv_weight), "hid", scatter_dimension=0, tiled=True
    )
    unit_grad = normed_grad * norm_gain
    grad_total, grad_project = lax.psum(
        (jnp.sum(unit_grad, axis=-1), jnp.sum(unit_grad * unit_rows, axis=-1)), "wid"
    )
    input_grad = (
        inverse
        * (
            unit_grad
            - (grad_total / total_count)[:, None]
            - unit_rows * (grad_project / total_count)[:, None]
        )
    ).astype(jnp.bfloat16)
    return (input_grad, qkv_grad, out_grad, up_grad, down_grad)


def solution(mesh):
    placed = (
        P("hid", "wid"),
        P("hid", "wid"),
        P("wid"),
        P("wid", None, "hid"),
        P("hid", "wid"),
        P("wid", "hid"),
        P("hid", "wid"),
        P(),
        P(),
    )
    return jax.shard_map(
        local,
        mesh=mesh,
        in_specs=placed,
        out_specs=(
            P("hid", "wid"),
            P("wid", None, "hid"),
            P("hid", "wid"),
            P("wid", "hid"),
            P("hid", "wid"),
        ),
        check_vma=False,
    )
```

profile of v0, /device:TPU:1, one launch (start us, length us, event | category | flops | bytes accessed | tf_op | source)
XLA Modules:
  0.0 634.7 jit_solution(3816883910043703335)
XLA Ops:
  7.2 0.9 convert_reduce_fusion
  8.1 1.3 dynamic-slice
  10.4 58.1 %all_gather.23 = bf16[512,384]{1,0:T(8,128)(2,1)S(1)} all-gather(bf16[16,384]{1,0:T(8,128)(2,1)S(1)} %copy-done.18), channel_id=1, replica_groups=mesh['hid'=32,'wid'=16] {'hid'}, dimensions={0}, use_global_device_ids=true | all-gather | bytes 405504 | tf_op jit(solution)/shard_map/all_gather | solution.py:130
  69.0 0.8 dynamic-update-slice
  69.8 76.6 %all-reduce.10 = (bf16[512,128]{1,0:T(8,128)(2,1)S(1)}, f32[16]{0:T(128)}, f32[256]{0:T(256)S(1)}, f32[256]{0:T(256)S(1)}) all-reduce(f32[512,128]{1,0:T(8,128)S(1)} %fusion.74, f32[16]{0:T(128)S(1)} %dynamic-update-slice, f32[256]{0:T(256)S(1)} %get-tuple-element.84, ...), channel_id=1, replica_groups=mesh['hid'=32,'wid'=16] {'wid'}, use_global_device_ids=true, to_apply=%region_13.14 | all-reduce | flops 66064 | bytes 397440 | tf_op jit(solution)/shard_map/psum | solution.py:136
  146.5 0.7 slice_bitcast_fusion
  147.4 63.4 %while.14 = (s32[]{:T(128)}, f32[1]{0:T(128)}, f32[16]{0:T(128)S(1)}, f32[16]{0:T(128)S(1)}, f32[15,1]{0,1:T(1,128)S(1)}, /*index=5*/f32[15,16]{1,0:T(8,128)S(1)}, f32[15,16]{1,0:T(8,128)S(1)}, s32[]{:T(128)}) while((s32[]{:T(128)}, f32[1]{0:T(128)}, f32[16]{0:T(128)S(1)}, f32[16]{0:T(128)S(1)}, f32[15,1]{0,1:T(1,128)S(1)}, ...), condition=%wide.region_3.4_spmd, body=%wide.region_2.3_spmd.sunk | while | flops 118 | bytes 549 | solution.py:19
  147.4 0.6 constant_dynamic-slice_fusion.4
  151.6 0.6 constant_dynamic-slice_fusion.4
  155.8 0.6 constant_dynamic-slice_fusion.4
  160.1 0.6 constant_dynamic-slice_fusion.4
  164.3 0.6 constant_dynamic-slice_fusion.4
  168.5 0.6 constant_dynamic-slice_fusion.4
  172.8 0.6 constant_dynamic-slice_fusion.4
  177.0 0.6 constant_dynamic-slice_fusion.4
  181.2 0.6 constant_dynamic-slice_fusion.4
  185.4 0.6 constant_dynamic-slice_fusion.4
  189.7 0.6 constant_dynamic-slice_fusion.4
  193.9 0.6 constant_dynamic-slice_fusion.4
  198.1 0.6 constant_dynamic-slice_fusion.4
  202.4 0.6 constant_dynamic-slice_fusion.4
  206.6 0.6 constant_dynamic-slice_fusion.4
  211.4 0.6 copy-done.23
  212.1 46.9 %all_gather.24 = bf16[512,384]{1,0:T(8,128)(2,1)S(1)} all-gather(bf16[16,384]{1,0:T(8,128)(2,1)S(1)} %fusion.47), channel_id=1, replica_groups=mesh['hid'=32,'wid'=16] {'hid'}, dimensions={0}, use_global_device_ids=true | all-gather | bytes 405504 | tf_op jit(solution)/shard_map/all_gather | solution.py:129
  259.0 1.3 fusion.33
  260.3 1.4 fusion.73
  261.7 1.5 fusion.72
  263.2 174.1 %all-reduce.9.cloned.1.call-done = (f32[512,3,128]{2,0,1:T(8,128)}, f32[512,512]{1,0:T(8,128)}, f32[512,512]{1,0:T(8,128)}) async-done(((f32[512,3,128]{2,0,1:T(8,128)}, f32[512,512]{1,0:T(8,128)}, f32[512,512]{1,0:T(8,128)}), (f32[512,3,128]{2,0,1:T(8,128)}, f32[512,512]{1,0:T(8,128)}, f32[512,512]{1,0:T(8,128)})) %all-reduce.9.cloned.1.call-update) | async-done | bytes 2883600 | tf_op jit(solution)/shard_map/psum | solution.py:136
  437.3 1.2 slice_reduce_fusion
  438.5 1.3 multiply_reduce_fusion.3
  442.0 0.8 copy.38
  443.0 2.0 fusion.65
  445.0 1.6 fusion.66
  447.1 1.0 multiply_convert_fusion.3
  448.2 0.8 copy.32
  448.9 0.7 broadcast_multiply_fusion
  449.6 1.0 multiply_convert_fusion.2
  450.6 0.8 copy.35
  451.4 2.0 fusion.23
  453.9 1.3 convolution_add_fusion
  455.6 0.9 convolution_convert_fusion.5
  456.6 1.1 convolution_convert_fusion.2
  457.7 1.1 convolution_convert_fusion.1
  458.9 1.3 convolution_convert_fusion
  460.2 107.3 %reduce-scatter.2.cloned.1.call-done = f32[16,384]{1,0:T(8,128)} async-done(((f32[512,384]{1,0:T(8,128)}), f32[16,384]{1,0:T(8,128)}) %reduce-scatter.2.cloned.1.call-update) | async-done | bytes 24592 | tf_op jit(solution)/shard_map/reduce_scatter | solution.py:146
  567.5 1.0 multiply_reduce_fusion.5
  568.5 58.1 %all-reduce.3 = (f32[16]{0:T(128)S(1)}, f32[16]{0:T(128)S(1)}) all-reduce(f32[16]{0:T(128)S(1)} %get-tuple-element.54, f32[16]{0:T(128)S(1)} %get-tuple-element.53), channel_id=1, replica_groups=mesh['hid'=32,'wid'=16] {'wid'}, use_global_device_ids=true, to_apply=%region_23.24 | all-reduce | flops 32 | bytes 256 | tf_op jit(solution)/shard_map/psum | solution.py:152
  627.2 0.7 fusion.51
  (111 shorter events, 6.6 us)
Async XLA Ops:
  7.2 253.1 %copy-start = (bf16[384,512]{1,0:T(8,128)(2,1)S(1)}, bf16[384,512]{1,0:T(8,128)(2,1)}, u32[]{:S(2)}) copy-start(bf16[384,512]{1,0:T(8,128)(2,1)} %param.16) | copy-start | bytes 1179652
  7.2 430.1 %all-reduce.9.cloned.1.call-start = ((), (), s32[]{:S(2)}) async-start(), calls=%async_computation.2 | async-start | bytes 5767168 | tf_op jit(solution)/shard_map/psum | solution.py:136
  7.2 2.9 copy-start.4
  8.1 2.2 copy-start.18
  10.4 58.1 %copy-start.15 = (bf16[128,384]{1,0:T(8,128)(2,1)S(1)}, bf16[128,384]{1,0:T(8,128)(2,1)}, u32[]{:S(2)}) copy-start(bf16[128,384]{1,0:T(8,128)(2,1)} %param.15) | copy-start | bytes 294916
  147.2 64.8 %copy-start.16 = (f32[384]{0:T(512)S(1)}, f32[384]{0:T(512)}, u32[]{:S(2)}) copy-start(f32[384]{0:T(512)} %param.13) | copy-start | bytes 4612
  147.4 111.6 %copy-start.5 = (bf16[384,3,128]{2,0,1:T(8,128)(2,1)S(1)}, bf16[384,3,128]{2,0,1:T(8,128)(2,1)}, u32[]{:S(2)}) copy-start(bf16[384,3,128]{2,0,1:T(8,128)(2,1)} %param.14) | copy-start | bytes 884740
  211.4 0.6 copy-start.23
  260.3 1.4 copy-start.3
  263.2 304.3 %reduce-scatter.2.cloned.1.call-start = ((), (), s32[]{:S(2)}) async-start(), calls=%async_computation.1 | async-start | bytes 811008 | tf_op jit(solution)/shard_map/reduce_scatter | solution.py:146
  437.3 2.5 copy-start.1
  438.5 6.5 %copy-start.19 = (f32[2,256]{1,0:T(2,128)}, f32[2,256]{1,0:T(2,128)S(1)}, u32[]{:S(2)}) copy-start(f32[2,256]{1,0:T(2,128)S(1)} %div.78) | copy-start | bytes 6148
  439.9 5.1 copy-start.21
  440.1 4.8 copy-start.20
  440.2 4.8 copy-start.22
  440.6 1.2 copy-start.7
  440.6 0.7 copy-start.25
  440.6 0.7 copy-start.26
  446.5 4.8 copy-start.2
  451.4 2.0 copy-start.6
  451.4 2.0 copy-start.8
  451.4 2.0 copy-start.10
  451.4 2.0 copy-start.12
  455.6 0.9 copy-start.9
  455.6 1.0 copy-start.11
  455.6 1.0 copy-start.13
  458.9 108.6 %copy-start.17 = (f32[384]{0:T(512)S(1)}, f32[384]{0:T(512)}, u32[]{:S(2)}) copy-start(f32[384]{0:T(512)} %param.13) | copy-start | bytes 4612
  458.9 108.6 %copy-start.24 = (f32[16]{0:T(128)S(1)}, f32[16]{0:T(128)}, u32[]{:S(2)}) copy-start(f32[16]{0:T(128)} %copy-done.23) | copy-start | bytes 196
  567.5 59.7 %copy-start.14 = (f32[16,384]{1,0:T(8,128)S(1)}, f32[16,384]{1,0:T(8,128)}, u32[]{:S(2)}) copy-start(f32[16,384]{1,0:T(8,128)} %reduce-scatter.2.cloned.1.call-done) | copy-start | bytes 73732
Sparse Core Ops, SparseCore 0:
  263.3 173.9 all-reduce.8
  455.4 112.0 reduce-scatter.1
where the time goes:
time: 636 us; the launch traced here: 635 us
  waiting for transfers between devices  281 us (44%)
  blocking collectives  240 us (38%)
  loops' own time  54.4 us (9%)
  local copies, waits for them, and re-layouts  16.3 us (3%)
  matrix products  15.2 us (2%)
  between operations  15.1 us (2%)
  other arithmetic  12.5 us (2%)
    psum x1, waiting for transfers between devices, local(): lax.psum((pre_part, qkv_part, hidden_part, att_part), 'wid')  174 us
    reduce_scatter x1, waiting for transfers between devices, local(): lax.psum_scatter(product('tf,df->td', pre_grad, up_weight), 'hid', scatte...  107 us
    psum x1, blocking collectives, local(): lax.psum((pre_part, qkv_part, hidden_part, att_part), 'wid')  76.6 us
    psum x1, blocking collectives, local(): lax.psum((jnp.sum(unit_grad, axis=-1), jnp.sum(unit_grad * unit_rows, axi...  58.1 us
    all_gather x1, blocking collectives, local(): lax.all_gather(cotangent, 'hid', axis=0, tiled=True)  58.1 us
    another operation x1, loops' own time, combined_all(): lax.scan(lambda subtotal, share: (join(subtotal, share), None), head, tail)  54.4 us
    all_gather x1, blocking collectives, local(): lax.all_gather(normed, 'hid', axis=0, tiled=True)  46.9 us
    dot_general x15, matrix products, product(): jnp.einsum(form, left_arr, right_arr, preferred_element_type=jnp.float32)  14.9 us
  transfers between devices with their start and end apart: 2, of which 2 were waited for; matrix products, arithmetic and copies ran while one was open for 1% of the time, Pallas kernels for 0%

commit v1 on v0

v1 whole, which is shorter than its diff:
```python
import math

import jax
import jax.numpy as jnp
from jax import lax
from jax.sharding import PartitionSpec as P

HEAD_DIM = 128
PATCHES = 256
EPSILON = 1e-06
F32 = jnp.float32
BF16 = jnp.bfloat16


def product(form, left_arr, right_arr):
    return jnp.einsum(form, left_arr, right_arr, preferred_element_type=F32)


def exact(form, left_arr, right_arr):
    return jnp.einsum(
        form, left_arr, right_arr, preferred_element_type=F32, precision=lax.Precision.HIGHEST
    )


def pieces(value, count):
    out = []
    for _ in range(count):
        piece = lax.reduce_precision(value, 8, 7)
        out.append(piece.astype(BF16))
        value = value - piece
    return out


def head_norm(values, gain):
    centre = jnp.mean(values, axis=-1, keepdims=True)
    centred = values - centre
    inverse = lax.rsqrt(jnp.mean(centred * centred, axis=-1, keepdims=True) + EPSILON)
    unit_rows = centred * inverse
    return (unit_rows, inverse, unit_rows * gain)


def head_norm_back(upstream, unit_rows, inverse, gain):
    scaled = upstream * gain
    return inverse * (
        scaled
        - jnp.mean(scaled, axis=-1, keepdims=True)
        - unit_rows * jnp.mean(scaled * unit_rows, axis=-1, keepdims=True)
    )


def gelu_pair(pre_act, upstream):
    hidden, pullback = jax.vjp(jax.nn.gelu, pre_act)
    return (hidden.astype(BF16), pullback(upstream)[0].astype(BF16))


def attention_pair(qkv_rows, att_grad, query_gain, key_gain):
    tok_count = qkv_rows.shape[0]
    head_width = qkv_rows.shape[2]
    head_count = head_width // HEAD_DIM
    image_count = tok_count // PATCHES
    score_scale = 1.0 / math.sqrt(HEAD_DIM)

    def per_image(values):
        return values.reshape(image_count, PATCHES, head_count, HEAD_DIM)

    query_unit, query_inverse, query_normed = head_norm(per_image(qkv_rows[:, 0]), query_gain)
    key_unit, key_inverse, key_normed = head_norm(per_image(qkv_rows[:, 1]), key_gain)
    query_normed = query_normed.astype(BF16)
    key_normed = key_normed.astype(BF16)
    value_rows = per_image(qkv_rows[:, 2]).astype(BF16)
    scores = product("ipha,iqha->ihpq", query_normed, key_normed) * score_scale
    exponent = jnp.exp(scores)
    probs = exponent / jnp.sum(exponent, axis=-1, keepdims=True)
    probs_low = probs.astype(BF16)
    attended = (
        product("ihpq,iqha->ipha", probs_low, value_rows).astype(BF16).reshape(tok_count, head_width)
    )
    grad_rows = per_image(att_grad)
    probs_grad = product("ipha,iqha->ihpq", grad_rows, value_rows)
    value_grad = product("ihpq,ipha->iqha", probs_low, grad_rows)
    score_grad = (
        probs * (probs_grad - jnp.sum(probs * probs_grad, axis=-1, keepdims=True)) * score_scale
    ).astype(BF16)
    qn_grad = product("ihpq,iqha->ipha", score_grad, key_normed)
    kn_grad = product("ihpq,ipha->iqha", score_grad, query_normed)
    query_grad = head_norm_back(qn_grad, query_unit, query_inverse, query_gain)
    key_grad = head_norm_back(kn_grad, key_unit, key_inverse, key_gain)
    qkv_back = jnp.concatenate(
        [
            query_grad.reshape(tok_count, head_width),
            key_grad.reshape(tok_count, head_width),
            value_grad.reshape(tok_count, head_width),
        ],
        axis=1,
    ).astype(BF16)
    return (attended, qkv_back)


def to_all(block, axis, count):
    rows, columns = block.shape
    spread = jnp.broadcast_to(block[None], (count, rows, columns)).reshape(count * rows, columns)
    return lax.all_to_all(spread, axis, 0, 0, tiled=True)


def local(
    hid_count,
    wid_count,
    inputs,
    cotangent,
    norm_gain,
    qkv_weight,
    out_weight,
    up_weight,
    down_weight,
    query_gain,
    key_gain,
):
    width = inputs.shape[1]
    tokens = inputs.shape[0] * hid_count
    total = float(width * wid_count)
    own = tokens // wid_count
    hidden_size = up_weight.shape[1]
    head_size = out_weight.shape[0]
    flat_qkv = qkv_weight.reshape(width, 3 * head_size)

    pre_sums = exact("d,df->f", norm_gain, up_weight.astype(F32))
    qkv_sums = exact("d,df->f", norm_gain, flat_qkv.astype(F32))
    column_sums = jnp.concatenate([pre_sums, qkv_sums])
    sum_rows = jnp.concatenate([p.reshape(-1, 128) for p in pieces(column_sums, 3)])
    sum_rows = jnp.pad(sum_rows, ((0, own - sum_rows.shape[0]), (0, 0)))

    both = to_all(jnp.concatenate([inputs, cotangent], axis=1), "hid", hid_count)
    rows, grad_all = both[:, :width].astype(F32), both[:, width:]
    part_mean = jnp.mean(rows, axis=-1, keepdims=True)
    deviation = rows - part_mean
    part_square = jnp.sum(deviation * deviation, axis=-1, keepdims=True)
    centred = (deviation * norm_gain).astype(BF16)
    stats = jnp.concatenate(pieces(part_mean, 3) + pieces(part_square, 3), axis=1)
    stats = jnp.pad(stats, ((0, 0), (0, 128 - stats.shape[1])))
    sent = jnp.concatenate(
        [
            product("td,df->tf", centred, up_weight).astype(BF16),
            product("td,df->tf", centred, flat_qkv).astype(BF16),
            product("td,fd->tf", grad_all, down_weight).astype(BF16),
            product("td,fd->tf", grad_all, out_weight).astype(BF16),
            stats,
            jnp.tile(sum_rows, (wid_count, 1)),
        ],
        axis=1,
    )
    got = lax.all_to_all(sent, "wid", 0, 0, tiled=True).reshape(wid_count, own, -1)
    edge = 2 * hidden_size + 4 * head_size
    sums = jnp.sum(got[:, :, :edge].astype(F32), axis=0)
    stats = got[:, :, edge : edge + 128].astype(F32)
    means = stats[:, :, 0] + stats[:, :, 1] + stats[:, :, 2]
    squares = stats[:, :, 3] + stats[:, :, 4] + stats[:, :, 5]
    sum_rows = got[:, :, edge + 128 :].astype(F32)
    lines = column_sums.shape[0] // 128
    all_sums = (
        sum_rows[:, :lines] + sum_rows[:, lines : 2 * lines] + sum_rows[:, 2 * lines : 3 * lines]
    ).reshape(wid_count, -1)
    mean = jnp.mean(means, axis=0)
    offset = means - mean
    variance = (jnp.sum(squares, axis=0) + float(width) * jnp.sum(offset * offset, axis=0)) / total
    inverse = lax.rsqrt(variance + EPSILON)
    normal = hidden_size + 3 * head_size
    normal_rows = inverse[:, None] * (sums[:, :normal] + exact("wt,wf->tf", offset, all_sums))
    pre_act = normal_rows[:, :hidden_size]
    hidden_grad = sums[:, normal : normal + hidden_size]
    total_sums = jnp.sum(all_sums, axis=0)
    hidden, pre_grad = gelu_pair(pre_act, hidden_grad)
    back = pre_grad.astype(F32)
    grad_sum = jnp.sum(back * total_sums[:hidden_size], axis=-1)
    grad_project = jnp.sum(back * pre_act, axis=-1)
    stats = jnp.stack(
        pieces(mean, 3) + pieces(inverse, 3) + pieces(grad_sum, 3) + pieces(grad_project, 3), axis=1
    )
    stats = jnp.pad(stats, ((0, 0), (0, 128 - stats.shape[1])))
    block = jnp.concatenate(
        [
            hidden,
            pre_grad,
            normal_rows[:, hidden_size:].astype(BF16),
            sums[:, normal + hidden_size :].astype(BF16),
            stats,
        ],
        axis=1,
    )
    shared = to_all(block, "wid", wid_count)
    hidden = shared[:, :hidden_size]
    pre_grad = shared[:, hidden_size : 2 * hidden_size]
    qkv_rows = shared[:, 2 * hidden_size : 2 * hidden_size + 3 * head_size].astype(F32)
    att_grad = shared[:, 2 * hidden_size + 3 * head_size : edge]
    stats = shared[:, edge:].astype(F32)
    mean, inverse, grad_sum, grad_project = (
        stats[:, i : i + 1] + stats[:, i + 1 : i + 2] + stats[:, i + 2 : i + 3] for i in (0, 3, 6, 9)
    )
    attended, qkv_back = attention_pair(
        qkv_rows.reshape(tokens, 3, head_size), att_grad, query_gain, key_gain
    )
    back = qkv_back.astype(F32)
    grad_sum = grad_sum + jnp.sum(back * total_sums[hidden_size:], axis=-1, keepdims=True)
    grad_project = grad_project + jnp.sum(back * qkv_rows, axis=-1, keepdims=True)
    unit_rows = (rows - mean) * inverse
    normed = (unit_rows * norm_gain).astype(BF16)
    unit_grad = norm_gain * (
        product("tf,df->td", pre_grad, up_weight) + product("tf,df->td", qkv_back, flat_qkv)
    )
    part = inverse * (unit_grad - grad_sum / total - unit_rows * (grad_project / total))
    parts = lax.all_to_all(part.astype(BF16), "hid", 0, 0, tiled=True)
    qkv_grad = product("td,tf->df", normed, qkv_back).astype(BF16)
    out_grad = product("th,td->hd", attended, grad_all).astype(BF16)
    up_grad = product("td,tf->df", normed, pre_grad).astype(BF16)
    down_grad = product("tf,td->fd", hidden, grad_all).astype(BF16)
    input_grad = jnp.sum(parts.reshape(hid_count, -1, width).astype(F32), axis=0).astype(BF16)
    return (input_grad, qkv_grad.reshape(qkv_weight.shape), out_grad, up_grad, down_grad)


def solution(mesh):
    hid_count, wid_count = mesh.shape["hid"], mesh.shape["wid"]

    def body(*args):
        return local(hid_count, wid_count, *args)

    return jax.shard_map(
        body,
        mesh=mesh,
        in_specs=(
            P("hid", "wid"),
            P("hid", "wid"),
            P("wid"),
            P("wid", None, "hid"),
            P("hid", "wid"),
            P("wid", "hid"),
            P("hid", "wid"),
            P(),
            P(),
        ),
        out_specs=(
            P("hid", "wid"),
            P("wid", None, "hid"),
            P("hid", "wid"),
            P("wid", "hid"),
            P("hid", "wid"),
        ),
        check_vma=False,
    )
```

time: 636 us -> 192 us (0.30)
  blocking collectives: 240 us -> 33.7 us
  waiting for transfers between devices: 281 us -> 81.7 us
  loops' own time: 54.4 us -> 0 us
  starting transfers between devices: 0.08 us -> 25.4 us
  between operations: 15.1 us -> 1.32 us
    psum x1 -> x0, waiting for transfers between devices: 174 us -> none  [local(): lax.psum((pre_part, qkv_part, hidden_part, att_part), 'wid')]
    psum x2 -> x0, blocking collectives: 135 us -> none  [the longest x1 76.6 us: local(): lax.psum((pre_part, qkv_part, hidden_part, att_part), 'wid')]
    reduce_scatter x1 -> x0, waiting for transfers between devices: 107 us -> none  [local(): lax.psum_scatter(product('tf,df->td', pre_grad, up_weight), 'hid', scatte...]
    all_gather x2 -> x0, blocking collectives: 105 us -> none  [the longest x1 58.1 us: local(): lax.all_gather(cotangent, 'hid', axis=0, tiled=True)]
    all_to_all x0 -> x3, waiting for transfers between devices: none -> 81.7 us  [the longest x2 66.4 us: to_all(): return lax.all_to_all(spread, axis, 0, 0, tiled=True)]
    another operation x1 -> x0, loops' own time: 54.4 us -> none  [combined_all(): lax.scan(lambda subtotal, share: (join(subtotal, share), None), head, tail)]
    all_to_all x0 -> x1, blocking collectives: none -> 33.7 us  [local(): lax.all_to_all(sent, 'wid', 0, 0, tiled=True).reshape(wid_count, own, -1)]
    all_to_all x0 -> x3, starting transfers between devices: none -> 25.4 us  [the longest x2 21.3 us: to_all(): return lax.all_to_all(spread, axis, 0, 0, tiled=True)]
  transfers between devices with their start and end apart: 2 -> 3, of which waited for: 2 -> 3; matrix products, arithmetic and copies ran while one was open for 1% -> 6% of each run, Pallas kernels for 0% -> 0%
where the time goes in v1:
time: 192 us; the launch traced here: 190 us
  waiting for transfers between devices  81.7 us (43%)
  blocking collectives  33.7 us (18%)
  starting transfers between devices  25.4 us (13%)
  matrix products  20.1 us (10%)
  local copies, waits for them, and re-layouts  15.3 us (8%)
  other arithmetic  12.3 us (6%)
    all_to_all x2, waiting for transfers between devices, to_all(): return lax.all_to_all(spread, axis, 0, 0, tiled=True)  66.4 us
    all_to_all x1, blocking collectives, local(): lax.all_to_all(sent, 'wid', 0, 0, tiled=True).reshape(wid_count, own, -1)  33.7 us
    all_to_all x2, starting transfers between devices, to_all(): return lax.all_to_all(spread, axis, 0, 0, tiled=True)  21.3 us
    dot_general x15, matrix products, product(): return jnp.einsum(form, left_arr, right_arr, preferred_element_type=F32)  18.6 us
    all_to_all x1, waiting for transfers between devices, local(): parts = lax.all_to_all(part.astype(BF16), 'hid', 0, 0, tiled=True)  15.3 us
    unnamed x66, local copies, waits for them, and re-layouts  4.83 us
    all_to_all x1, starting transfers between devices, local(): parts = lax.all_to_all(part.astype(BF16), 'hid', 0, 0, tiled=True)  4.01 us
  transfers between devices with their start and end apart: 3, of which 3 were waited for; matrix products, arithmetic and copies ran while one was open for 6% of the time, Pallas kernels for 0%

profile of v1, /device:TPU:1, one launch (start us, length us, event | category | flops | bytes accessed | tf_op | source)
XLA Modules:
  0.0 189.8 jit_solution(2998571305763040320)
XLA Ops:
  0.7 0.8 pad_maximum_fusion.1
  1.5 0.9 broadcast_in_dim.8
  2.4 17.0 %all-to-all-start = ((bf16[32,16,768]{2,1,0:T(8,128)(2,1)}), bf16[32,16,768]{2,1,0:T(8,128)(2,1)S(1)}, u32[]{:S(2)}, u32[]{:S(2)}) async-start(bf16[32,16,768]{2,1,0:T(8,128)(2,1)} %broadcast_in_dim.8), calls=%async_computation | async-start | bytes 1572864 | tf_op jit(solution)/shard_map/all_to_all | solution.py:102
  19.7 0.4 convolution_reduce_fusion
  20.1 0.3 fusion.114
  20.4 41.9 %all-to-all-done = bf16[32,16,768]{2,1,0:T(8,128)(2,1)S(1)} async-done(((bf16[32,16,768]{2,1,0:T(8,128)(2,1)}), bf16[32,16,768]{2,1,0:T(8,128)(2,1)S(1)}, u32[]{:S(2)}, u32[]{:S(2)}) %all-to-all-start) | async-done | bytes 786464 | tf_op jit(solution)/shard_map/all_to_all | solution.py:102
  62.8 0.5 convolution_convert_fusion.4
  63.3 0.5 convolution_convert_fusion.1
  64.1 0.5 convolution_convert_fusion
  64.6 0.3 convolution_convert_fusion.8
  65.1 33.7 %all_to_all.33 = bf16[16,32,1792]{2,1,0:T(8,128)(2,1)S(1)} all-to-all(bf16[16,32,1792]{2,1,0:T(8,128)(2,1)S(1)} %broadcast_dynamic-update-slice_fusion), channel_id=1, replica_groups=mesh['hid'=32,'wid'=16] {'wid'}, dimensions={0} | all-to-all | bytes 3670016 | tf_op jit(solution)/shard_map/all_to_all | solution.py:151
  98.9 0.8 fusion.107
  99.6 1.3 copy.234
  101.1 1.0 fusion.105
  102.4 0.3 fusion.17
  103.2 1.3 broadcast_in_dim.9
  104.5 4.3 %all-to-all-start.2 = ((bf16[16,32,1664]{2,1,0:T(8,128)(2,1)}), bf16[16,32,1664]{2,1,0:T(8,128)(2,1)S(1)}, u32[]{:S(2)}, u32[]{:S(2)}) async-start(bf16[16,32,1664]{2,1,0:T(8,128)(2,1)} %broadcast_in_dim.9), calls=%async_computation.2 | async-start | bytes 3407872 | tf_op jit(solution)/shard_map/all_to_all | solution.py:102
  108.8 24.5 %all-to-all-done.2 = bf16[16,32,1664]{2,1,0:T(8,128)(2,1)S(1)} async-done(((bf16[16,32,1664]{2,1,0:T(8,128)(2,1)}), bf16[16,32,1664]{2,1,0:T(8,128)(2,1)S(1)}, u32[]{:S(2)}, u32[]{:S(2)}) %all-to-all-start.2) | async-done | bytes 1703968 | tf_op jit(solution)/shard_map/all_to_all | solution.py:102
  133.3 1.0 slice_convert_fusion
  134.3 0.5 copy-done.1
  134.8 1.4 copy.200
  136.4 2.4 %fusion.34 = f32[512,384]{1,0:T(8,128)} fusion(bf16[384,512]{1,0:T(8,128)(2,1)S(1)} %copy-done, bf16[512,1664]{1,0:T(8,128)(2,1)} %bitcast.135), kind=kOutput, calls=%fused_computation.55 | convolution fusion | flops 201326592 | bytes 1703936 | tf_op jit(solution)/shard_map/tf,df->td/dot_general | solution.py:16
  139.7 0.5 fusion.45
  140.2 0.9 fusion.15
  141.1 1.2 fusion.102
  142.3 1.9 multiply_convert_fusion.1
  144.2 1.0 copy.208
  145.2 1.8 copy.212
  147.1 3.3 %fusion.103 = (f32[2,256]{1,0:T(2,128)}, f32[2,256]{1,0:T(2,128)}, f32[2,256,1,128]{1,3,0,2:T(8,128)}) fusion(f32[2,256]{1,0:T(2,128)S(1)} %rsqrt.50, f32[2,256,1,128]{1,3,0,2:T(8,128)} %copy.212, f32[2,256]{1,0:T(2,128)S(1)} %div.76, f32[128]{0:T(128)} %param.17, f32[2,256,256]{1,2,0:T(8,128)} %copy-done.3, f32[2,256,256]{1,2,0:T(8,128)} %copy-done.11, ...), kind=kOutput, calls=%fused_computation.212 | convolution fusion | flops 34864896 | bytes 1848320 | tf_op jit(solution)/shard_map/ihpq,ipha->iqha/dot_general | solution.py:16
  150.4 0.7 broadcast_multiply_fusion
  151.1 0.7 broadcast_multiply_fusion.1
  151.8 1.1 multiply_convert_fusion
  153.0 1.1 copy.216
  154.1 0.3 fusion.26
  154.4 0.3 copy-done.16
  154.9 0.9 copy.219
  155.8 2.2 %fusion.43 = (f32[512]{0:T(512)S(1)}, f32[512]{0:T(512)S(1)}, f32[512]{0:T(512)S(1)}, f32[512]{0:T(512)S(1)}) fusion(f32[512,128]{1,0:T(8,128)S(1)} %get-tuple-element.59, f32[512,1]{1,0:T(8,128)S(1)} %copy.218, f32[512,1]{1,0:T(8,128)} %copy.219), kind=kLoop, calls=%fused_computation.74 | loop fusion | flops 6144 | bytes 36864 | tf_op jit(solution)/shard_map/add | solution.py:196
  158.0 1.3 fusion.5
  159.3 4.0 %all-to-all-start.3 = ((bf16[32,16,384]{2,1,0:T(8,128)(2,1)}), bf16[32,16,384]{2,1,0:T(8,128)(2,1)S(1)}, u32[]{:S(2)}, u32[]{:S(2)}) async-start(bf16[32,16,384]{2,1,0:T(8,128)(2,1)} %bitcast.165), calls=%async_computation.3 | async-start | bytes 786432 | tf_op jit(solution)/shard_map/all_to_all | solution.py:210
  163.3 1.9 %fusion.16 = bf16[2,256,1,128]{1,3,0,2:T(8,128)(2,1)} fusion(bf16[2,256,128]{2,1,0:T(8,128)(2,1)S(1)} %bitcast.146, f32[2,256,256]{1,2,0:T(8,128)} %copy-done.3), kind=kOutput, calls=%fused_computation.34 | convolution fusion | flops 33751040 | bytes 786432 | tf_op jit(solution)/shard_map/ihpq,iqha->ipha/dot_general | solution.py:16
  165.2 1.0 copy.222
  166.3 2.3 %convolution_convert_fusion.5 = bf16[384,384]{0,1:T(8,128)(2,1)} fusion(f32[512]{0:T(512)S(1)} %get-tuple-element.40, f32[512]{0:T(512)S(1)} %get-tuple-element.39, f32[384]{0:T(512)S(1)} %copy-done.22, bf16[512,768]{1,0:T(8,128)(2,1)S(1)} %bitcast.125, bf16[512,128]{1,0:T(8,128)(2,1)} %bitcast.163, bf16[512,128]{1,0:T(8,128)(2,1)} %bitcast.160, ...), kind=kOutput, calls=%fused_computation.18 | convolution fusion | flops 153305088 | bytes 1087488 | tf_op jit(solution)/shard_map/td,tf->df/dot_general | solution.py:16
  168.5 1.8 copy.223
  170.4 0.9 convolution_convert_fusion.9
  171.3 1.2 convolution_convert_fusion.2
  172.5 1.3 convolution_convert_fusion.3
  173.8 15.3 %all-to-all-done.3 = bf16[32,16,384]{2,1,0:T(8,128)(2,1)S(1)} async-done(((bf16[32,16,384]{2,1,0:T(8,128)(2,1)}), bf16[32,16,384]{2,1,0:T(8,128)(2,1)S(1)}, u32[]{:S(2)}, u32[]{:S(2)}) %all-to-all-start.3) | async-done | bytes 393248 | tf_op jit(solution)/shard_map/all_to_all | solution.py:210
  189.2 0.7 reduce_sum.231
  (109 shorter events, 3.4 us)
Async XLA Ops:
  0.6 19.5 %copy-start = (bf16[384,512]{1,0:T(8,128)(2,1)S(1)}, bf16[384,512]{1,0:T(8,128)(2,1)}, u32[]{:S(2)}) copy-start(bf16[384,512]{1,0:T(8,128)(2,1)} %param.14) | copy-start | bytes 1179652
  0.6 18.8 %copy-start.19 = (bf16[384,3,128]{2,0,1:T(8,128)(2,1)S(1)}, bf16[384,3,128]{2,0,1:T(8,128)(2,1)}, u32[]{:S(2)}) copy-start(bf16[384,3,128]{2,0,1:T(8,128)(2,1)} %param.12) | copy-start | bytes 884740
  0.7 19.0 %copy-start.21 = (f32[384]{0:T(512)S(1)}, f32[384]{0:T(512)}, u32[]{:S(2)}) copy-start(f32[384]{0:T(512)} %param.11) | copy-start | bytes 4612
  2.4 60.0 %all-to-all-start = ((bf16[32,16,768]{2,1,0:T(8,128)(2,1)}), bf16[32,16,768]{2,1,0:T(8,128)(2,1)S(1)}, u32[]{:S(2)}, u32[]{:S(2)}) async-start(bf16[32,16,768]{2,1,0:T(8,128)(2,1)} %broadcast_in_dim.8), calls=%async_computation | async-start | bytes 1572864 | tf_op jit(solution)/shard_map/all_to_all | solution.py:102
  19.7 44.1 %copy-start.4 = (bf16[384,3,128]{0,2,1:T(8,128)(2,1)}, bf16[384,3,128]{0,2,1:T(8,128)(2,1)S(1)}, u32[]{:S(2)}) copy-start(bf16[384,3,128]{0,2,1:T(8,128)(2,1)S(1)} %copy.190) | copy-start | bytes 884740
  62.8 1.3 copy-start.18
  63.2 1.3 copy-start.23
  104.5 28.8 %all-to-all-start.2 = ((bf16[16,32,1664]{2,1,0:T(8,128)(2,1)}), bf16[16,32,1664]{2,1,0:T(8,128)(2,1)S(1)}, u32[]{:S(2)}, u32[]{:S(2)}) async-start(bf16[16,32,1664]{2,1,0:T(8,128)(2,1)} %broadcast_in_dim.9), calls=%async_computation.2 | async-start | bytes 3407872 | tf_op jit(solution)/shard_map/all_to_all | solution.py:102
  133.3 1.4 copy-start.1
  136.4 3.3 %copy-start.24 = (f32[128]{0:T(128)S(1)}, f32[128]{0:T(128)}, u32[]{:S(2)}) copy-start(f32[128]{0:T(128)} %param.17) | copy-start | bytes 1540
  136.4 3.3 %copy-start.25 = (f32[128]{0:T(128)S(1)}, f32[128]{0:T(128)}, u32[]{:S(2)}) copy-start(f32[128]{0:T(128)} %param.16) | copy-start | bytes 1540
  138.9 0.7 copy-start.6
  139.1 2.0 %copy-start.8 = (f32[512,1,128]{2,0,1:T(8,128)}, f32[512,1,128]{2,0,1:T(8,128)S(1)}, u32[]{:S(2)}) copy-start(f32[512,1,128]{2,0,1:T(8,128)S(1)} %copy.201) | copy-start | bytes 786436
  139.3 3.0 %copy-start.20 = (f32[2,256]{1,0:T(2,128)}, f32[2,256]{1,0:T(2,128)S(1)}, u32[]{:S(2)}) copy-start(f32[2,256]{1,0:T(2,128)S(1)} %rsqrt.48) | copy-start | bytes 6148
  139.4 1.7 copy-start.9
  139.7 2.6 %copy-start.11 = (f32[2,256,256]{1,2,0:T(8,128)}, f32[2,256,256]{1,2,0:T(8,128)S(1)}, u32[]{:S(2)}) copy-start(f32[2,256,256]{1,2,0:T(8,128)S(1)} %fusion.115) | copy-start | bytes 1572868
  140.2 2.1 %copy-start.3 = (f32[2,256,256]{1,2,0:T(8,128)}, f32[2,256,256]{1,2,0:T(8,128)S(1)}, u32[]{:S(2)}) copy-start(f32[2,256,256]{1,2,0:T(8,128)S(1)} %fusion.45) | copy-start | bytes 1572868
  142.3 11.8 %copy-start.2 = (bf16[16,32,1664]{2,1,0:T(8,128)(2,1)S(1)}, bf16[16,32,1664]{2,1,0:T(8,128)(2,1)}, u32[]{:S(2)}) copy-start(bf16[16,32,1664]{2,1,0:T(8,128)(2,1)} %copy-done.1) | copy-start | bytes 5111812
  145.2 12.7 %copy-start.12 = (bf16[2,256,1,128]{3,1,0,2:T(8,128)(2,1)}, bf16[2,256,1,128]{3,1,0,2:T(8,128)(2,1)S(1)}, u32[]{:S(2)}) copy-start(bf16[2,256,1,128]{3,1,0,2:T(8,128)(2,1)S(1)} %copy.208) | copy-start | bytes 393220
  153.0 1.4 copy-start.14
  154.1 0.7 copy-start.16
  155.7 2.2 %copy-start.5 = (bf16[384,3,128]{0,2,1:T(8,128)(2,1)S(1)}, bf16[384,3,128]{0,2,1:T(8,128)(2,1)}, u32[]{:S(2)}) copy-start(bf16[384,3,128]{0,2,1:T(8,128)(2,1)} %copy-done.4) | copy-start | bytes 884740
  155.7 2.2 %copy-start.10 = (f32[512,384]{1,0:T(8,128)S(1)}, f32[512,384]{1,0:T(8,128)}, u32[]{:S(2)}) copy-start(f32[512,384]{1,0:T(8,128)} %fusion.34) | copy-start | bytes 2359300
  155.7 2.2 %copy-start.15 = (bf16[2,256,1,128]{3,1,0,2:T(8,128)(2,1)S(1)}, bf16[2,256,1,128]{3,1,0,2:T(8,128)(2,1)}, u32[]{:S(2)}) copy-start(bf16[2,256,1,128]{3,1,0,2:T(8,128)(2,1)} %copy-done.14) | copy-start | bytes 393220
  155.7 2.2 %copy-start.17 = (bf16[2,256,1,128]{3,1,0,2:T(8,128)(2,1)S(1)}, bf16[2,256,1,128]{3,1,0,2:T(8,128)(2,1)}, u32[]{:S(2)}) copy-start(bf16[2,256,1,128]{3,1,0,2:T(8,128)(2,1)} %copy-done.16) | copy-start | bytes 393220
  155.7 2.2 %copy-start.22 = (f32[384]{0:T(512)S(1)}, f32[384]{0:T(512)}, u32[]{:S(2)}) copy-start(f32[384]{0:T(512)} %param.11) | copy-start | bytes 4612
  158.0 5.3 %copy-start.7 = (bf16[512,1,128]{2,0,1:T(8,128)(2,1)S(1)}, bf16[512,1,128]{2,0,1:T(8,128)(2,1)}, u32[]{:S(2)}) copy-start(bf16[512,1,128]{2,0,1:T(8,128)(2,1)} %copy-done.6) | copy-start | bytes 393220
  159.3 7.0 %copy-start.13 = (bf16[2,256,1,128]{3,1,0,2:T(8,128)(2,1)S(1)}, bf16[2,256,1,128]{3,1,0,2:T(8,128)(2,1)}, u32[]{:S(2)}) copy-start(bf16[2,256,1,128]{3,1,0,2:T(8,128)(2,1)} %copy-done.12) | copy-start | bytes 393220
  159.3 29.9 %all-to-all-start.3 = ((bf16[32,16,384]{2,1,0:T(8,128)(2,1)}), bf16[32,16,384]{2,1,0:T(8,128)(2,1)S(1)}, u32[]{:S(2)}, u32[]{:S(2)}) async-start(bf16[32,16,384]{2,1,0:T(8,128)(2,1)} %bitcast.165), calls=%async_computation.3 | async-start | bytes 786432 | tf_op jit(solution)/shard_map/all_to_all | solution.py:210

commit v2 on v1

--- a/solution.py
+++ b/solution.py
@@ -3,11 +3,14 @@
 import jax
 import jax.numpy as jnp
 from jax import lax
+from jax.sharding import Mesh
 from jax.sharding import PartitionSpec as P
 
 HEAD_DIM = 128
 PATCHES = 256
 EPSILON = 1e-06
+Z_COUNT = 16
+CHIPS = 8
 F32 = jnp.float32
 BF16 = jnp.bfloat16
 
@@ -103,8 +106,6 @@
 
 
 def local(
-    hid_count,
-    wid_count,
     inputs,
     cotangent,
     norm_gain,
@@ -116,52 +117,93 @@
     key_gain,
 ):
     width = inputs.shape[1]
-    tokens = inputs.shape[0] * hid_count
-    total = float(width * wid_count)
-    own = tokens // wid_count
+    block = inputs.shape[0]
+    total = float(width * CHIPS * 2)
+    image = block * Z_COUNT
+    own = image // CHIPS
+    half = image // 2
     hidden_size = up_weight.shape[1]
     head_size = out_weight.shape[0]
+    core = lax.axis_index("core")
+    swap = [(0, 1), (1, 0)]
     flat_qkv = qkv_weight.reshape(width, 3 * head_size)
 
-    pre_sums = exact("d,df->f", norm_gain, up_weight.astype(F32))
-    qkv_sums = exact("d,df->f", norm_gain, flat_qkv.astype(F32))
-    column_sums = jnp.concatenate([pre_sums, qkv_sums])
-    sum_rows = jnp.concatenate([p.reshape(-1, 128) for p in pieces(column_sums, 3)])
+    both = to_all(jnp.concatenate([inputs, cotangent], axis=1), "z", Z_COUNT)
+    own_weights = (norm_gain, up_weight, flat_qkv, down_weight, out_weight)
+    other_weights = tuple(lax.ppermute(w, "core", swap) for w in own_weights)
+
+    def column_sums(weights):
+        gain, up, qkv = weights[:3]
+        return jnp.concatenate(
+            [exact("d,df->f", gain, up.astype(F32)), exact("d,df->f", gain, qkv.astype(F32))]
+        )
+
+    sums = column_sums(own_weights) + column_sums(other_weights)
+    lines = sums.shape[0] // 128
+    sum_rows = jnp.concatenate([p.reshape(-1, 128) for p in pieces(sums, 3)])
     sum_rows = jnp.pad(sum_rows, ((0, own - sum_rows.shape[0]), (0, 0)))
 
-    both = to_all(jnp.concatenate([inputs, cotangent], axis=1), "hid", hid_count)
-    rows, grad_all = both[:, :width].astype(F32), both[:, width:]
-    part_mean = jnp.mean(rows, axis=-1, keepdims=True)
-    deviation = rows - part_mean
-    part_square = jnp.sum(deviation * deviation, axis=-1, keepdims=True)
-    centred = (deviation * norm_gain).astype(BF16)
+    low, high = both[:half], both[half:]
+    pair = lax.all_to_all(
+        jnp.concatenate([low, high, low, high]), ("y_lo", "core"), 0, 0, tiled=True
+    ).reshape(2, 2, half, 2 * width)
+    pair = jnp.swapaxes(pair, 0, 1).reshape(2, image, 2 * width)
+    mine = lax.dynamic_index_in_dim(pair, core, 0, keepdims=False)
+    other = lax.dynamic_index_in_dim(pair, 1 - core, 0, keepdims=False)
+    rest = jnp.where(core == 0, high, low)
+    rest_moved = lax.ppermute(rest, "y_lo", swap)
+    y_lo = lax.axis_index("y_lo")
+    rest = jnp.concatenate(
+        [jnp.where(y_lo == 0, rest, rest_moved), jnp.where(y_lo == 0, rest_moved, rest)]
+    )
+
+    mine_rows, other_rows = mine[:, :width].astype(F32), other[:, :width].astype(F32)
+    mine_grad, other_grad = mine[:, width:], other[:, width:]
+    part_mean = (
+        jnp.sum(mine_rows, axis=-1, keepdims=True) + jnp.sum(other_rows, axis=-1, keepdims=True)
+    ) / float(2 * width)
+    part_square = 0.0
+    centred = []
+    for rows, weights in ((mine_rows, own_weights), (other_rows, other_weights)):
+        deviation = rows - part_mean
+        part_square += jnp.sum(deviation * deviation, axis=-1, keepdims=True)
+        centred.append((deviation * weights[0]).astype(BF16))
     stats = jnp.concatenate(pieces(part_mean, 3) + pieces(part_square, 3), axis=1)
     stats = jnp.pad(stats, ((0, 0), (0, 128 - stats.shape[1])))
+    up_pair, qkv_pair, down_pair, out_pair = zip(own_weights[1:], other_weights[1:])
+
+    def paired(form, left_pair, right_pair):
+        return (
+            product(form, left_pair[0], right_pair[0]) + product(form, left_pair[1], right_pair[1])
+        ).astype(BF16)
+
+    grads = (mine_grad, other_grad)
     sent = jnp.concatenate(
         [
-            product("td,df->tf", centred, up_weight).astype(BF16),
-            product("td,df->tf", centred, flat_qkv).astype(BF16),
-            product("td,fd->tf", grad_all, down_weight).astype(BF16),
-            product("td,fd->tf", grad_all, out_weight).astype(BF16),
+            paired("td,df->tf", centred, up_pair),
+            paired("td,df->tf", centred, qkv_pair),
+            paired("td,fd->tf", grads, down_pair),
+            paired("td,fd->tf", grads, out_pair),
             stats,
-            jnp.tile(sum_rows, (wid_count, 1)),
+            jnp.tile(sum_rows, (CHIPS, 1)),
         ],
         axis=1,
     )
-    got = lax.all_to_all(sent, "wid", 0, 0, tiled=True).reshape(wid_count, own, -1)
+    got = lax.all_to_all(sent, ("y_hi", "x"), 0, 0, tiled=True).reshape(CHIPS, own, -1)
     edge = 2 * hidden_size + 4 * head_size
     sums = jnp.sum(got[:, :, :edge].astype(F32), axis=0)
     stats = got[:, :, edge : edge + 128].astype(F32)
     means = stats[:, :, 0] + stats[:, :, 1] + stats[:, :, 2]
     squares = stats[:, :, 3] + stats[:, :, 4] + stats[:, :, 5]
     sum_rows = got[:, :, edge + 128 :].astype(F32)
-    lines = column_sums.shape[0] // 128
     all_sums = (
         sum_rows[:, :lines] + sum_rows[:, lines : 2 * lines] + sum_rows[:, 2 * lines : 3 * lines]
-    ).reshape(wid_count, -1)
+    ).reshape(CHIPS, -1)
     mean = jnp.mean(means, axis=0)
     offset = means - mean
-    variance = (jnp.sum(squares, axis=0) + float(width) * jnp.sum(offset * offset, axis=0)) / total
+    variance = (
+        jnp.sum(squares, axis=0) + float(2 * width) * jnp.sum(offset * offset, axis=0)
+    ) / total
     inverse = lax.rsqrt(variance + EPSILON)
     normal = hidden_size + 3 * head_size
     normal_rows = inverse[:, None] * (sums[:, :normal] + exact("wt,wf->tf", offset, all_sums))
@@ -186,62 +228,84 @@
         ],
         axis=1,
     )
-    shared = to_all(block, "wid", wid_count)
-    hidden = shared[:, :hidden_size]
-    pre_grad = shared[:, hidden_size : 2 * hidden_size]
-    qkv_rows = shared[:, 2 * hidden_size : 2 * hidden_size + 3 * head_size].astype(F32)
-    att_grad = shared[:, 2 * hidden_size + 3 * head_size : edge]
-    stats = shared[:, edge:].astype(F32)
-    mean, inverse, grad_sum, grad_project = (
-        stats[:, i : i + 1] + stats[:, i + 1 : i + 2] + stats[:, i + 2 : i + 3] for i in (0, 3, 6, 9)
-    )
+    shared = to_all(block, ("y_hi", "x"), CHIPS)
+    shared_other = lax.ppermute(shared, "core", swap)
+
+    def unpack(shared):
+        stats = shared[:, edge:].astype(F32)
+        return (
+            shared[:, :hidden_size],
+            shared[:, hidden_size : 2 * hidden_size],
+            shared[:, 2 * hidden_size : 2 * hidden_size + 3 * head_size].astype(F32),
+            shared[:, 2 * hidden_size + 3 * head_size : edge],
+            *(
+                stats[:, i : i + 1] + stats[:, i + 1 : i + 2] + stats[:, i + 2 : i + 3]
+                for i in (0, 3, 6, 9)
+            ),
+        )
+
+    hidden, pre_grad, qkv_rows, att_grad, mean, inverse, grad_sum, grad_project = unpack(shared)
     attended, qkv_back = attention_pair(
-        qkv_rows.reshape(tokens, 3, head_size), att_grad, query_gain, key_gain
-    )
+        qkv_rows.reshape(image, 3, head_size), att_grad, query_gain, key_gain
+    )
+    attention = jnp.concatenate([attended, qkv_back], axis=1)
+    attention_other = lax.ppermute(attention, "core", swap)
     back = qkv_back.astype(F32)
     grad_sum = grad_sum + jnp.sum(back * total_sums[hidden_size:], axis=-1, keepdims=True)
     grad_project = grad_project + jnp.sum(back * qkv_rows, axis=-1, keepdims=True)
-    unit_rows = (rows - mean) * inverse
-    normed = (unit_rows * norm_gain).astype(BF16)
-    unit_grad = norm_gain * (
-        product("tf,df->td", pre_grad, up_weight) + product("tf,df->td", qkv_back, flat_qkv)
-    )
-    part = inverse * (unit_grad - grad_sum / total - unit_rows * (grad_project / total))
-    parts = lax.all_to_all(part.astype(BF16), "hid", 0, 0, tiled=True)
-    qkv_grad = product("td,tf->df", normed, qkv_back).astype(BF16)
-    out_grad = product("th,td->hd", attended, grad_all).astype(BF16)
-    up_grad = product("td,tf->df", normed, pre_grad).astype(BF16)
-    down_grad = product("tf,td->fd", hidden, grad_all).astype(BF16)
-    input_grad = jnp.sum(parts.reshape(hid_count, -1, width).astype(F32), axis=0).astype(BF16)
+    parts = []
+    for rows, weights in ((mine_rows, own_weights), (other_rows, other_weights)):
+        gain, up, qkv = weights[:3]
+        unit_rows = (rows - mean) * inverse
+        unit_grad = gain * (product("tf,df->td", pre_grad, up) + product("tf,df->td", qkv_back, qkv))
+        part = inverse * (unit_grad - grad_sum / total - unit_rows * (grad_project / total))
+        parts.append(part.astype(BF16).reshape(2, half, width))
+    first = jnp.where(core == 0, parts[0], parts[1])
+    second = jnp.where(core == 0, parts[1], parts[0])
+    parts = jnp.stack([first, second], axis=1).reshape(4 * half, width)
+    parts = lax.all_to_all(parts, ("y_lo", "core"), 0, 0, tiled=True).reshape(2, image, width)
+    parts = jnp.sum(parts.astype(F32), axis=0).astype(BF16)
+    parts = lax.all_to_all(parts, "z", 0, 0, tiled=True).reshape(Z_COUNT, -1, width)
+    input_grad = jnp.sum(parts.astype(F32), axis=0).astype(BF16)
+
+    hidden_other, pre_grad_other, _, _, mean_other, inverse_other, _, _ = unpack(shared_other)
+    attended_other, back_other = attention_other[:, :head_size], attention_other[:, head_size:]
+    normed = ((mine_rows - mean) * inverse * norm_gain).astype(BF16)
+    normed_other = (
+        (rest[:, :width].astype(F32) - mean_other) * inverse_other * norm_gain
+    ).astype(BF16)
+    normed = jnp.concatenate([normed, normed_other])
+    grad_all = jnp.concatenate([mine_grad, rest[:, width:]])
+    qkv_grad = product("td,tf->df", normed, jnp.concatenate([qkv_back, back_other])).astype(BF16)
+    out_grad = product("th,td->hd", jnp.concatenate([attended, attended_other]), grad_all).astype(BF16)
+    up_grad = product("td,tf->df", normed, jnp.concatenate([pre_grad, pre_grad_other])).astype(BF16)
+    down_grad = product("tf,td->fd", jnp.concatenate([hidden, hidden_other]), grad_all).astype(BF16)
     return (input_grad, qkv_grad.reshape(qkv_weight.shape), out_grad, up_grad, down_grad)
 
 
 def solution(mesh):
-    hid_count, wid_count = mesh.shape["hid"], mesh.shape["wid"]
-
-    def body(*args):
-        return local(hid_count, wid_count, *args)
-
+    mesh = Mesh(mesh.devices.reshape(Z_COUNT, 2, 2, 4, 2), ("z", "y_lo", "y_hi", "x", "core"))
+    hid, wid = ("z", "y_lo"), ("y_hi", "x", "core")
     return jax.shard_map(
-        body,
+        local,
         mesh=mesh,
         in_specs=(
-            P("hid", "wid"),
-            P("hid", "wid"),
-            P("wid"),
-            P("wid", None, "hid"),
-            P("hid", "wid"),
-            P("wid", "hid"),
-            P("hid", "wid"),
+            P(hid, wid),
+            P(hid, wid),
+            P(wid),
+            P(wid, None, hid),
+            P(hid, wid),
+            P(wid, hid),
+            P(hid, wid),
             P(),
             P(),
         ),
         out_specs=(
-            P("hid", "wid"),
-            P("wid", None, "hid"),
-            P("hid", "wid"),
-            P("wid", "hid"),
-            P("hid", "wid"),
+            P(hid, wid),
+            P(wid, None, hid),
+            P(hid, wid),
+            P(wid, hid),
+            P(hid, wid),
         ),
         check_vma=False,
     )

time: 192 us -> 168 us (0.88)
  the two profiles are of different devices: /device:TPU:1 before, /device:TPU:16 now
where the time goes in v2:
time: 168 us; the launch traced here: 167 us
  waiting for transfers between devices  62 us (37%)
  starting transfers between devices  59.4 us (35%)
  matrix products  17.6 us (10%)
  local copies, waits for them, and re-layouts  15.2 us (9%)
  other arithmetic  11.5 us (7%)
    all_to_all x2, starting transfers between devices, to_all(): return lax.all_to_all(spread, axis, 0, 0, tiled=True)  21.6 us
    dot_general x22, matrix products, product(): return jnp.einsum(form, left_arr, right_arr, preferred_element_type=F32)  16 us
    all_to_all x1, waiting for transfers between devices, local(): lax.all_to_all(sent, ('y_hi', 'x'), 0, 0, tiled=True)  12.6 us
    all_to_all x2, waiting for transfers between devices, to_all(): return lax.all_to_all(spread, axis, 0, 0, tiled=True)  12.6 us
    ppermute x1, waiting for transfers between devices, local(): rest_moved = lax.ppermute(rest, 'y_lo', swap)  12 us
    ppermute x5, starting transfers between devices, local(): other_weights = tuple((lax.ppermute(w, 'core', swap) for w in own_weights))  10.6 us
    all_to_all x1, waiting for transfers between devices, local(): lax.all_to_all(jnp.concatenate([low, high, low, high]), ('y_lo', 'core'),...  10.5 us
    all_to_all x1, waiting for transfers between devices, local(): lax.all_to_all(parts, 'z', 0, 0, tiled=True).reshape(Z_COUNT, -1, width)  9.77 us
  transfers between devices with their start and end apart: 14, of which 6 were waited for; matrix products, arithmetic and copies ran while one was open for 18% of the time, Pallas kernels for 0%

profile of v2, /device:TPU:16, one launch (start us, length us, event | category | flops | bytes accessed | tf_op | source)
XLA Modules:
  0.0 167.1 jit_solution(8699268113385194216)
XLA Ops:
  0.7 0.8 pad_maximum_fusion.8
  1.5 0.8 broadcast_in_dim.8
  2.2 15.2 %all-to-all-start = ((bf16[16,16,768]{2,1,0:T(8,128)(2,1)}), bf16[16,16,768]{2,1,0:T(8,128)(2,1)S(1)}, u32[]{:S(2)}, u32[]{:S(2)}) async-start(bf16[16,16,768]{2,1,0:T(8,128)(2,1)} %broadcast_in_dim.8), calls=%async_computation | async-start | bytes 786432 | tf_op jit(solution)/shard_map/all_to_all | solution.py:105
  17.4 1.9 %collective-permute-start = (f32[384]{0:T(512)S(1)}, f32[384]{0:T(512)S(1)}, u32[]{:S(2)}, u32[]{:S(2)}) collective-permute-start(f32[384]{0:T(512)S(1)} %copy-done.16), channel_id=1, source_target_pairs={{0,1},{1,0},{2,3},{3,2},{4,5},{5,4},{6,7},{7,6},{8,9},{9,8},{10,11... | collective-permute-start | bytes 4616 | tf_op jit(solution)/shard_map/ppermute | solution.py:133
  19.4 2.4 %collective-permute-start.4 = (bf16[128,384]{1,0:T(8,128)(2,1)}, bf16[128,384]{1,0:T(8,128)(2,1)}, u32[]{:S(2)}, u32[]{:S(2)}) collective-permute-start(bf16[128,384]{1,0:T(8,128)(2,1)} %param.13), channel_id=1, source_target_pairs={{0,1},{1,0},{2,3},{3,2},{4,5},{5,4},{6,7},{7,6},{8,9},{9,8},{10,11... | collective-permute-start | bytes 294920 | tf_op jit(solution)/shard_map/ppermute | solution.py:133
  22.0 1.9 %collective-permute-start.2 = (bf16[384,384]{0,1:T(8,128)(2,1)S(1)}, bf16[384,384]{0,1:T(8,128)(2,1)S(1)}, u32[]{:S(2)}, u32[]{:S(2)}) collective-permute-start(bf16[384,384]{0,1:T(8,128)(2,1)S(1)} %bitcast.217), channel_id=1, source_target_pairs={{0,1},{1,0},{2,3},{3,2},{4,5},{5,4},{6,7},{7,6},{8,9},{9,8},{10,11... | collective-permute-start | bytes 884744 | tf_op jit(solution)/shard_map/ppermute | solution.py:133
  23.9 2.4 %collective-permute-start.3 = (bf16[512,384]{1,0:T(8,128)(2,1)}, bf16[512,384]{1,0:T(8,128)(2,1)}, u32[]{:S(2)}, u32[]{:S(2)}) collective-permute-start(bf16[512,384]{1,0:T(8,128)(2,1)} %param.15), channel_id=1, source_target_pairs={{0,1},{1,0},{2,3},{3,2},{4,5},{5,4},{6,7},{7,6},{8,9},{9,8},{10,11... | collective-permute-start | bytes 1179656 | tf_op jit(solution)/shard_map/ppermute | solution.py:133
  26.4 1.9 %collective-permute-start.1 = (bf16[384,512]{1,0:T(8,128)(2,1)S(1)}, bf16[384,512]{1,0:T(8,128)(2,1)S(1)}, u32[]{:S(2)}, u32[]{:S(2)}) collective-permute-start(bf16[384,512]{1,0:T(8,128)(2,1)S(1)} %copy-done), channel_id=1, source_target_pairs={{0,1},{1,0},{2,3},{3,2},{4,5},{5,4},{6,7},{7,6},{8,9},{9,8},{10,11... | collective-permute-start | bytes 1179656 | tf_op jit(solution)/shard_map/ppermute | solution.py:133
  28.6 12.6 %all-to-all-done = bf16[16,16,768]{2,1,0:T(8,128)(2,1)S(1)} async-done(((bf16[16,16,768]{2,1,0:T(8,128)(2,1)}), bf16[16,16,768]{2,1,0:T(8,128)(2,1)S(1)}, u32[]{:S(2)}, u32[]{:S(2)}) %all-to-all-start) | async-done | bytes 393248 | tf_op jit(solution)/shard_map/all_to_all | solution.py:105
  41.2 0.9 pad_maximum_fusion
  42.1 3.5 %all-to-all-start.1 = ((bf16[4,128,768]{2,1,0:T(8,128)(2,1)}), bf16[4,128,768]{2,1,0:T(8,128)(2,1)S(1)}, u32[]{:S(2)}, u32[]{:S(2)}) async-start(bf16[4,128,768]{2,1,0:T(8,128)(2,1)} %bitcast.1), calls=%async_computation.1 | async-start | bytes 1572864 | tf_op jit(solution)/shard_map/all_to_all | solution.py:147
  46.8 10.5 %all-to-all-done.1 = bf16[4,128,768]{2,1,0:T(8,128)(2,1)S(1)} async-done(((bf16[4,128,768]{2,1,0:T(8,128)(2,1)}), bf16[4,128,768]{2,1,0:T(8,128)(2,1)S(1)}, u32[]{:S(2)}, u32[]{:S(2)}) %all-to-all-start.1) | async-done | bytes 786464 | tf_op jit(solution)/shard_map/all_to_all | solution.py:147
  57.4 1.8 %fusion.143 = f32[256,128]{1,0:T(8,128)} fusion(bf16[128,384]{1,0:T(8,128)(2,1)} %param.13, bf16[256,768]{1,0:T(8,128)(2,1)S(1)} %get-tuple-element.70), kind=kOutput, calls=%fused_computation.273 | convolution fusion | flops 25165824 | bytes 425984 | tf_op jit(solution)/shard_map/td,fd->tf/dot_general | solution.py:19
  60.3 1.0 fusion.12
  61.7 0.7 constant_dynamic-update-slice_fusion.4
  63.4 1.3 fusion.145
  64.7 1.4 fusion.1
  66.1 0.7 constant_dynamic-update-slice_fusion.2
  66.8 1.1 fusion.17
  69.9 7.3 %all-to-all-start.2 = ((bf16[8,32,1792]{2,1,0:T(8,128)(2,1)}), bf16[8,32,1792]{2,1,0:T(8,128)(2,1)S(1)}, u32[]{:S(2)}, u32[]{:S(2)}) async-start(bf16[8,32,1792]{2,1,0:T(8,128)(2,1)} %broadcast_dynamic-update-slice_fusion), calls=%async_computation.2 | async-start | bytes 1835008 | tf_op jit(solution)/shard_map/all_to_all | solution.py:192
  77.2 12.6 %all-to-all-done.2 = bf16[8,32,1792]{2,1,0:T(8,128)(2,1)S(1)} async-done(((bf16[8,32,1792]{2,1,0:T(8,128)(2,1)}), bf16[8,32,1792]{2,1,0:T(8,128)(2,1)S(1)}, u32[]{:S(2)}, u32[]{:S(2)}) %all-to-all-start.2) | async-done | bytes 917536 | tf_op jit(solution)/shard_map/all_to_all | solution.py:192
  90.5 1.0 copy.164
  92.5 1.0 broadcast_in_dim.9
  93.5 6.4 %all-to-all-start.3 = ((bf16[8,32,1664]{2,1,0:T(8,128)(2,1)}), bf16[8,32,1664]{2,1,0:T(8,128)(2,1)S(1)}, u32[]{:S(2)}, u32[]{:S(2)}) async-start(bf16[8,32,1664]{2,1,0:T(8,128)(2,1)} %broadcast_in_dim.9), calls=%async_computation.3 | async-start | bytes 1703936 | tf_op jit(solution)/shard_map/all_to_all | solution.py:105
  100.0 2.5 %collective-permute-start.5 = (bf16[128,768]{1,0:T(8,128)(2,1)S(1)}, bf16[128,768]{1,0:T(8,128)(2,1)S(1)}, u32[]{:S(2)}, u32[]{:S(2)}) collective-permute-start(bf16[128,768]{1,0:T(8,128)(2,1)S(1)} %bitcast.226), channel_id=1, source_target_pairs={{0,16},{16,0},{1,17},{17,1},{2,18},{18,2},{3,19},{19,3},{4,20},{20... | collective-permute-start | bytes 589832 | tf_op jit(solution)/shard_map/ppermute | solution.py:154
  102.5 12.0 %collective-permute-done.5 = bf16[128,768]{1,0:T(8,128)(2,1)S(1)} collective-permute-done((bf16[128,768]{1,0:T(8,128)(2,1)S(1)}, bf16[128,768]{1,0:T(8,128)(2,1)S(1)}, u32[]{:S(2)}, u32[]{:S(2)}) %collective-permute-start.5) | collective-permute-done | bytes 196640 | tf_op jit(solution)/shard_map/ppermute | solution.py:154
  114.5 0.8 broadcast_select_fusion
  117.0 0.8 fusion.18
  117.9 0.8 fusion.19
  118.9 1.1 fusion.148
  120.0 1.9 %collective-permute-start.6 = (bf16[256,1664]{1,0:T(8,128)(2,1)S(1)}, bf16[256,1664]{1,0:T(8,128)(2,1)}, u32[]{:S(2)}, u32[]{:S(2)}) collective-permute-start(bf16[256,1664]{1,0:T(8,128)(2,1)S(1)} %bitcast.211), channel_id=1, source_target_pairs={{0,1},{1,0},{2,3},{3,2},{4,5},{5,4},{6,7},{7,6},{8,9},{9,8},{10,11... | collective-permute-start | bytes 2555912 | tf_op jit(solution)/shard_map/ppermute | solution.py:232
  123.1 1.0 fusion.87
  124.1 1.0 fusion.34
  125.4 1.6 pad_maximum_fusion.4
  127.0 2.5 %collective-permute-start.7 = (bf16[256,512]{0,1:T(8,128)(2,1)}, bf16[256,512]{0,1:T(8,128)(2,1)}, u32[]{:S(2)}, u32[]{:S(2)}) collective-permute-start(bf16[256,512]{0,1:T(8,128)(2,1)} %pad_maximum_fusion.4), channel_id=1, source_target_pairs={{0,1},{1,0},{2,3},{3,2},{4,5},{5,4},{6,7},{7,6},{8,9},{9,8},{10,11... | collective-permute-start | bytes 786440 | tf_op jit(solution)/shard_map/ppermute | solution.py:252
  131.8 0.8 pad_maximum_fusion.2
  132.6 3.5 %all-to-all-start.4 = ((bf16[4,128,384]{2,1,0:T(8,128)(2,1)}), bf16[4,128,384]{2,1,0:T(8,128)(2,1)S(1)}, u32[]{:S(2)}, u32[]{:S(2)}) async-start(bf16[4,128,384]{2,1,0:T(8,128)(2,1)} %bitcast.49), calls=%async_computation.4 | async-start | bytes 786432 | tf_op jit(solution)/shard_map/all_to_all | solution.py:266
  136.2 1.0 slice.293
  137.2 0.9 slice.281
  138.2 0.9 convolution_convert_fusion.3
  139.0 4.5 %all-to-all-done.4 = bf16[4,128,384]{2,1,0:T(8,128)(2,1)S(1)} async-done(((bf16[4,128,384]{2,1,0:T(8,128)(2,1)}), bf16[4,128,384]{2,1,0:T(8,128)(2,1)S(1)}, u32[]{:S(2)}, u32[]{:S(2)}) %all-to-all-start.4) | async-done | bytes 393248 | tf_op jit(solution)/shard_map/all_to_all | solution.py:266
  144.3 6.0 %all-to-all-start.5 = ((bf16[16,16,384]{2,1,0:T(8,128)(2,1)}), bf16[16,16,384]{2,1,0:T(8,128)(2,1)S(1)}, u32[]{:S(2)}, u32[]{:S(2)}) async-start(bf16[16,16,384]{2,1,0:T(8,128)(2,1)} %bitcast.51), calls=%async_computation.5 | async-start | bytes 393216 | tf_op jit(solution)/shard_map/all_to_all | solution.py:268
  150.3 0.9 slice_convert_fusion.1
  152.4 0.9 copy.160
  153.3 1.1 fusion.155
  154.3 1.1 convolution_convert_fusion.1
  155.5 1.2 convolution_convert_fusion
  156.7 9.8 %all-to-all-done.5 = bf16[16,16,384]{2,1,0:T(8,128)(2,1)S(1)} async-done(((bf16[16,16,384]{2,1,0:T(8,128)(2,1)}), bf16[16,16,384]{2,1,0:T(8,128)(2,1)S(1)}, u32[]{:S(2)}, u32[]{:S(2)}) %all-to-all-start.5) | async-done | bytes 196640 | tf_op jit(solution)/shard_map/all_to_all | solution.py:268
  (131 shorter events, 16.0 us)
Async XLA Ops:
  0.6 16.8 %copy-start.16 = (f32[384]{0:T(512)S(1)}, f32[384]{0:T(512)}, u32[]{:S(2)}) copy-start(f32[384]{0:T(512)} %param.11) | copy-start | bytes 4612
  0.6 21.1 %copy-start.11 = (bf16[384,3,128]{2,0,1:T(8,128)(2,1)S(1)}, bf16[384,3,128]{2,0,1:T(8,128)(2,1)}, u32[]{:S(2)}) copy-start(bf16[384,3,128]{2,0,1:T(8,128)(2,1)} %param.12) | copy-start | bytes 884740
  0.7 25.7 %copy-start = (bf16[384,512]{1,0:T(8,128)(2,1)S(1)}, bf16[384,512]{1,0:T(8,128)(2,1)}, u32[]{:S(2)}) copy-start(bf16[384,512]{1,0:T(8,128)(2,1)} %param.14) | copy-start | bytes 1179652
  2.2 39.0 %all-to-all-start = ((bf16[16,16,768]{2,1,0:T(8,128)(2,1)}), bf16[16,16,768]{2,1,0:T(8,128)(2,1)S(1)}, u32[]{:S(2)}, u32[]{:S(2)}) async-start(bf16[16,16,768]{2,1,0:T(8,128)(2,1)} %broadcast_in_dim.8), calls=%async_computation | async-start | bytes 786432 | tf_op jit(solution)/shard_map/all_to_all | solution.py:105
  17.4 28.6 %collective-permute-start = (f32[384]{0:T(512)S(1)}, f32[384]{0:T(512)S(1)}, u32[]{:S(2)}, u32[]{:S(2)}) collective-permute-start(f32[384]{0:T(512)S(1)} %copy-done.16), channel_id=1, source_target_pairs={{0,1},{1,0},{2,3},{3,2},{4,5},{5,4},{6,7},{7,6},{8,9},{9,8},{10,11... | collective-permute-start | bytes 4616 | tf_op jit(solution)/shard_map/ppermute | solution.py:133
  19.4 47.4 %collective-permute-start.4 = (bf16[128,384]{1,0:T(8,128)(2,1)}, bf16[128,384]{1,0:T(8,128)(2,1)}, u32[]{:S(2)}, u32[]{:S(2)}) collective-permute-start(bf16[128,384]{1,0:T(8,128)(2,1)} %param.13), channel_id=1, source_target_pairs={{0,1},{1,0},{2,3},{3,2},{4,5},{5,4},{6,7},{7,6},{8,9},{9,8},{10,11... | collective-permute-start | bytes 294920 | tf_op jit(solution)/shard_map/ppermute | solution.py:133
  22.0 24.0 %collective-permute-start.2 = (bf16[384,384]{0,1:T(8,128)(2,1)S(1)}, bf16[384,384]{0,1:T(8,128)(2,1)S(1)}, u32[]{:S(2)}, u32[]{:S(2)}) collective-permute-start(bf16[384,384]{0,1:T(8,128)(2,1)S(1)} %bitcast.217), channel_id=1, source_target_pairs={{0,1},{1,0},{2,3},{3,2},{4,5},{5,4},{6,7},{7,6},{8,9},{9,8},{10,11... | collective-permute-start | bytes 884744 | tf_op jit(solution)/shard_map/ppermute | solution.py:133
  23.9 40.7 %collective-permute-start.3 = (bf16[512,384]{1,0:T(8,128)(2,1)}, bf16[512,384]{1,0:T(8,128)(2,1)}, u32[]{:S(2)}, u32[]{:S(2)}) collective-permute-start(bf16[512,384]{1,0:T(8,128)(2,1)} %param.15), channel_id=1, source_target_pairs={{0,1},{1,0},{2,3},{3,2},{4,5},{5,4},{6,7},{7,6},{8,9},{9,8},{10,11... | collective-permute-start | bytes 1179656 | tf_op jit(solution)/shard_map/ppermute | solution.py:133
  26.4 20.1 %collective-permute-start.1 = (bf16[384,512]{1,0:T(8,128)(2,1)S(1)}, bf16[384,512]{1,0:T(8,128)(2,1)S(1)}, u32[]{:S(2)}, u32[]{:S(2)}) collective-permute-start(bf16[384,512]{1,0:T(8,128)(2,1)S(1)} %copy-done), channel_id=1, source_target_pairs={{0,1},{1,0},{2,3},{3,2},{4,5},{5,4},{6,7},{7,6},{8,9},{9,8},{10,11... | collective-permute-start | bytes 1179656 | tf_op jit(solution)/shard_map/ppermute | solution.py:133
  42.1 15.1 %all-to-all-start.1 = ((bf16[4,128,768]{2,1,0:T(8,128)(2,1)}), bf16[4,128,768]{2,1,0:T(8,128)(2,1)S(1)}, u32[]{:S(2)}, u32[]{:S(2)}) async-start(bf16[4,128,768]{2,1,0:T(8,128)(2,1)} %bitcast.1), calls=%async_computation.1 | async-start | bytes 1572864 | tf_op jit(solution)/shard_map/all_to_all | solution.py:147
  46.1 14.2 %copy-start.1 = (bf16[384,384]{0,1:T(8,128)(2,1)}, bf16[384,384]{0,1:T(8,128)(2,1)S(1)}, u32[]{:S(2)}) copy-start(bf16[384,384]{0,1:T(8,128)(2,1)S(1)} %collective-permute-done.2) | copy-start | bytes 884740
  61.3 1.3 copy-start.3
  64.7 2.1 %copy-start.8 = (f32[256,128]{1,0:T(8,128)S(1)}, f32[256,128]{1,0:T(8,128)}, u32[]{:S(2)}) copy-start(f32[256,128]{1,0:T(8,128)} %fusion.143) | copy-start | bytes 393220
  69.9 19.9 %all-to-all-start.2 = ((bf16[8,32,1792]{2,1,0:T(8,128)(2,1)}), bf16[8,32,1792]{2,1,0:T(8,128)(2,1)S(1)}, u32[]{:S(2)}, u32[]{:S(2)}) async-start(bf16[8,32,1792]{2,1,0:T(8,128)(2,1)} %broadcast_dynamic-update-slice_fusion), calls=%async_computation.2 | async-start | bytes 1835008 | tf_op jit(solution)/shard_map/all_to_all | solution.py:192
  93.5 22.5 %all-to-all-start.3 = ((bf16[8,32,1664]{2,1,0:T(8,128)(2,1)}), bf16[8,32,1664]{2,1,0:T(8,128)(2,1)S(1)}, u32[]{:S(2)}, u32[]{:S(2)}) async-start(bf16[8,32,1664]{2,1,0:T(8,128)(2,1)} %broadcast_in_dim.9), calls=%async_computation.3 | async-start | bytes 1703936 | tf_op jit(solution)/shard_map/all_to_all | solution.py:105
  100.0 14.5 %collective-permute-start.5 = (bf16[128,768]{1,0:T(8,128)(2,1)S(1)}, bf16[128,768]{1,0:T(8,128)(2,1)S(1)}, u32[]{:S(2)}, u32[]{:S(2)}) collective-permute-start(bf16[128,768]{1,0:T(8,128)(2,1)S(1)} %bitcast.226), channel_id=1, source_target_pairs={{0,16},{16,0},{1,17},{17,1},{2,18},{18,2},{3,19},{19,3},{4,20},{20... | collective-permute-start | bytes 589832 | tf_op jit(solution)/shard_map/ppermute | solution.py:154
  116.0 0.7 copy-start.17
  116.0 0.7 copy-start.18
  120.0 30.3 %collective-permute-start.6 = (bf16[256,1664]{1,0:T(8,128)(2,1)S(1)}, bf16[256,1664]{1,0:T(8,128)(2,1)}, u32[]{:S(2)}, u32[]{:S(2)}) collective-permute-start(bf16[256,1664]{1,0:T(8,128)(2,1)S(1)} %bitcast.211), channel_id=1, source_target_pairs={{0,1},{1,0},{2,3},{3,2},{4,5},{5,4},{6,7},{7,6},{8,9},{9,8},{10,11... | collective-permute-start | bytes 2555912 | tf_op jit(solution)/shard_map/ppermute | solution.py:232
  122.5 0.7 copy-start.9
  124.1 6.4 %copy-start.6 = (bf16[256,128]{0,1:T(8,128)(2,1)}, bf16[256,128]{0,1:T(8,128)(2,1)S(1)}, u32[]{:S(2)}) copy-start(bf16[256,128]{0,1:T(8,128)(2,1)S(1)} %get-tuple-element.77) | copy-start | bytes 196612
  127.0 3.2 %copy-start.10 = (f32[256,384]{1,0:T(8,128)S(1)}, f32[256,384]{1,0:T(8,128)}, u32[]{:S(2)}) copy-start(f32[256,384]{1,0:T(8,128)} %fusion.148) | copy-start | bytes 1179652
  127.0 3.2 %copy-start.12 = (bf16[256,128]{0,1:T(8,128)(2,1)S(1)}, bf16[256,128]{0,1:T(8,128)(2,1)}, u32[]{:S(2)}) copy-start(bf16[256,128]{0,1:T(8,128)(2,1)} %fusion.18) | copy-start | bytes 196612
  127.0 9.2 %collective-permute-start.7 = (bf16[256,512]{0,1:T(8,128)(2,1)}, bf16[256,512]{0,1:T(8,128)(2,1)}, u32[]{:S(2)}, u32[]{:S(2)}) collective-permute-start(bf16[256,512]{0,1:T(8,128)(2,1)} %pad_maximum_fusion.4), channel_id=1, source_target_pairs={{0,1},{1,0},{2,3},{3,2},{4,5},{5,4},{6,7},{7,6},{8,9},{9,8},{10,11... | collective-permute-start | bytes 786440 | tf_op jit(solution)/shard_map/ppermute | solution.py:252
  130.2 1.0 copy-start.2
  132.6 10.9 %all-to-all-start.4 = ((bf16[4,128,384]{2,1,0:T(8,128)(2,1)}), bf16[4,128,384]{2,1,0:T(8,128)(2,1)S(1)}, u32[]{:S(2)}, u32[]{:S(2)}) async-start(bf16[4,128,384]{2,1,0:T(8,128)(2,1)} %bitcast.49), calls=%async_computation.4 | async-start | bytes 786432 | tf_op jit(solution)/shard_map/all_to_all | solution.py:266
  136.1 2.0 %copy-start.4 = (bf16[128,768]{1,0:T(8,128)(2,1)S(1)}, bf16[128,768]{1,0:T(8,128)(2,1)}, u32[]{:S(2)}) copy-start(bf16[128,768]{1,0:T(8,128)(2,1)} %get-tuple-element.72) | copy-start | bytes 589828
  136.1 2.0 %copy-start.5 = (bf16[128,768]{1,0:T(8,128)(2,1)S(1)}, bf16[128,768]{1,0:T(8,128)(2,1)}, u32[]{:S(2)}) copy-start(bf16[128,768]{1,0:T(8,128)(2,1)} %get-tuple-element.73) | copy-start | bytes 589828
  136.1 2.0 %copy-start.14 = (bf16[256,384]{1,0:T(8,128)(2,1)S(1)}, bf16[256,384]{1,0:T(8,128)(2,1)}, u32[]{:S(2)}) copy-start(bf16[256,384]{1,0:T(8,128)(2,1)} %slice.243) | copy-start | bytes 589828
  136.1 2.0 %copy-start.15 = (bf16[256,128]{0,1:T(8,128)(2,1)S(1)}, bf16[256,128]{0,1:T(8,128)(2,1)}, u32[]{:S(2)}) copy-start(bf16[256,128]{0,1:T(8,128)(2,1)} %fusion.19) | copy-start | bytes 196612
  144.3 22.2 %all-to-all-start.5 = ((bf16[16,16,384]{2,1,0:T(8,128)(2,1)}), bf16[16,16,384]{2,1,0:T(8,128)(2,1)S(1)}, u32[]{:S(2)}, u32[]{:S(2)}) async-start(bf16[16,16,384]{2,1,0:T(8,128)(2,1)} %bitcast.51), calls=%async_computation.5 | async-start | bytes 393216 | tf_op jit(solution)/shard_map/all_to_all | solution.py:268
  151.1 0.8 copy-start.7
  151.1 0.9 copy-start.13

commit v3 on v2

v3 whole, which is shorter than its diff:
```python
import functools
import math

import jax
import jax.numpy as jnp
from jax import lax
from jax.experimental import pallas as pl
from jax.experimental.pallas import tpu as pltpu
from jax.sharding import Mesh
from jax.sharding import PartitionSpec as P

HEAD_DIM = 128
PATCHES = 256
EPSILON = 1e-06
Z_COUNT = 16
CHIPS = 8
VMEM_BYTES = 24 * 1024 * 1024
F32 = jnp.float32
BF16 = jnp.bfloat16


def product(form, left_arr, right_arr):
    return jnp.einsum(form, left_arr, right_arr, preferred_element_type=F32)


def exact(form, left_arr, right_arr):
    return jnp.einsum(
        form, left_arr, right_arr, preferred_element_type=F32, precision=lax.Precision.HIGHEST
    )


def pieces(value, count):
    out = []
    for _ in range(count):
        piece = lax.reduce_precision(value, 8, 7)
        out.append(piece.astype(BF16))
        value = value - piece
    return out


def split(value, count):
    out = []
    for _ in range(count):
        piece = value.astype(BF16).astype(F32)
        out.append(piece)
        value = value - piece
    return out


def lanes(columns, rows):
    lane = lax.broadcasted_iota(jnp.int32, (rows, 128), 1)
    out = jnp.zeros((rows, 128), F32)
    for i, column in enumerate(columns):
        out = jnp.where(lane == i, column, out)
    return out.astype(BF16)


def dot(left, right, left_dim=1, right_dim=0):
    return lax.dot_general(
        left, right, (((left_dim,), (right_dim,)), ((), ())), preferred_element_type=F32
    )


def spread_kernel(inputs, cotangent, out):
    width = inputs.shape[1]
    for i in range(out.shape[0]):
        out[i, :, :width] = inputs[...]
        out[i, :, width:] = cotangent[...]


def forward_kernel(
    core,
    pair,
    own_gain,
    other_gain,
    own_up,
    other_up,
    own_qkv,
    other_qkv,
    own_down,
    other_down,
    own_out,
    other_out,
    sum_rows,
    sent,
    own_rows,
    other_rows,
):
    own_index, other_index = core[0], 1 - core[0]
    half, width = pair.shape[1], own_gain.shape[1]
    hidden_size, heads3 = own_up.shape[1], own_qkv.shape[1]
    edge = 2 * hidden_size + heads3 + own_out.shape[0]
    for y in range(2):
        at = slice(y * half, (y + 1) * half)
        own = pair[2 * y + own_index]
        other = pair[2 * y + other_index]
        own_rows[at, width:] = own[:, width:]
        other_rows[at, width:] = other[:, width:]
        own, other = own[:, :width].astype(F32), other[:, :width].astype(F32)
        part_mean = (
            jnp.sum(own, axis=1, keepdims=True) + jnp.sum(other, axis=1, keepdims=True)
        ) / float(2 * width)
        own, other = own - part_mean, other - part_mean
        part_square = jnp.sum(own * own, axis=1, keepdims=True) + jnp.sum(
            other * other, axis=1, keepdims=True
        )
        own_rows[at, :width] = (own * own_gain[...]).astype(BF16)
        other_rows[at, :width] = (other * other_gain[...]).astype(BF16)
        sent[at, edge : edge + 128] = lanes(split(part_mean, 3) + split(part_square, 3), half)
    for i in range(sent.shape[0] // sum_rows.shape[0]):
        sent[i * sum_rows.shape[0] : (i + 1) * sum_rows.shape[0], edge + 128 :] = sum_rows[...]
    start = 0
    for own_weight, other_weight, first, dim in (
        (own_up, other_up, 0, 0),
        (own_qkv, other_qkv, 0, 0),
        (own_down, other_down, width, 1),
        (own_out, other_out, width, 1),
    ):
        size = own_weight.shape[1 - dim]
        sent[:, start : start + size] = (
            dot(own_rows[:, first : first + width], own_weight[...], 1, dim)
            + dot(other_rows[:, first : first + width], other_weight[...], 1, dim)
        ).astype(BF16)
        start += size


def middle_kernel(hidden_size, width, got, block, totals):
    chips, own, _ = got.shape
    heads3 = 3 * HEAD_DIM
    normal = hidden_size + heads3
    edge = normal + hidden_size + HEAD_DIM
    lines = normal // 128
    means, squares = [], []
    for w in range(chips):
        stats = got[w, :, edge : edge + 128].astype(F32)
        means.append(stats[:, 0:1] + stats[:, 1:2] + stats[:, 2:3])
        squares.append(stats[:, 3:4] + stats[:, 4:5] + stats[:, 5:6])
    mean = sum(means) / float(chips)
    offsets = [m - mean for m in means]
    count = float(width)
    variance = (sum(squares) + count * sum(o * o for o in offsets)) / (count * chips)
    inverse = lax.rsqrt(variance + EPSILON)

    column_sums = []
    for w in range(chips):
        rows = got[w, :, edge + 128 :].astype(F32)
        column_sums.append(
            rows[:lines] + rows[lines : 2 * lines] + rows[2 * lines : 3 * lines]
        )
    total_sums = sum(column_sums)

    def summed(start):
        return sum(got[w, :, start : start + 128].astype(F32) for w in range(chips))

    def store(start, value):
        value = value.astype(BF16)
        for w in range(chips):
            block[w, :, start : start + 128] = value

    def normal_rows(line):
        value = summed(line * 128)
        for w in range(chips):
            value = value + offsets[w] * column_sums[w][line : line + 1]
        return inverse * value

    grad_sum = jnp.zeros((own, 1), F32)
    grad_project = jnp.zeros((own, 1), F32)
    scale = math.sqrt(2.0 / math.pi)
    for line in range(hidden_size // 128):
        at = line * 128
        pre_act = normal_rows(line)
        hidden_grad = summed(normal + at)
        square = pre_act * pre_act
        tanh = jnp.tanh(scale * (pre_act + 0.044715 * (square * pre_act)))
        gate = 0.5 * (1.0 + tanh)
        slope = gate + (0.5 * scale) * pre_act * (1.0 - tanh * tanh) * (1.0 + 0.134145 * square)
        pre_grad = (slope * hidden_grad).astype(BF16)
        store(at, pre_act * gate)
        store(hidden_size + at, pre_grad)
        back = pre_grad.astype(F32)
        grad_sum += jnp.sum(back * total_sums[line : line + 1], axis=1, keepdims=True)
        grad_project += jnp.sum(back * pre_act, axis=1, keepdims=True)
    for line in range(3):
        store(2 * hidden_size + line * 128, normal_rows(hidden_size // 128 + line))
    store(2 * hidden_size + heads3, summed(normal + hidden_size))
    stats = lanes(split(mean, 3) + split(inverse, 3) + split(grad_sum, 3) + split(grad_project, 3), own)
    for w in range(chips):
        block[w, :, edge:] = stats
    totals[...] = jnp.zeros(totals.shape, F32)
    totals[0:3, :] = total_sums[hidden_size // 128 :]


def head_norm(values, gain):
    centred = values - jnp.mean(values, axis=1, keepdims=True)
    inverse = lax.rsqrt(jnp.mean(centred * centred, axis=1, keepdims=True) + EPSILON)
    unit_rows = centred * inverse
    return unit_rows, inverse, (unit_rows * gain).astype(BF16)


def head_norm_back(upstream, unit_rows, inverse, gain):
    scaled = upstream * gain
    return inverse * (
        scaled
        - jnp.mean(scaled, axis=1, keepdims=True)
        - unit_rows * jnp.mean(scaled * unit_rows, axis=1, keepdims=True)
    )


def backward_kernel(
    total,
    core,
    shared,
    pair,
    own_gain,
    other_gain,
    own_up,
    other_up,
    own_qkv,
    other_qkv,
    totals,
    query_gain,
    key_gain,
    parts,
    attention,
    own_normed,
    other_normed,
):
    half, width = pair.shape[1], own_gain.shape[1]
    hidden_size = own_up.shape[1]
    start = 2 * hidden_size
    edge = start + 4 * HEAD_DIM
    score_scale = 1.0 / math.sqrt(HEAD_DIM)

    stats = shared[:, edge:].astype(F32)
    mean, inverse, grad_sum, grad_project = (
        stats[:, i : i + 1] + stats[:, i + 1 : i + 2] + stats[:, i + 2 : i + 3] for i in (0, 3, 6, 9)
    )
    query = shared[:, start : start + HEAD_DIM].astype(F32)
    key = shared[:, start + HEAD_DIM : start + 2 * HEAD_DIM].astype(F32)
    value = shared[:, start + 2 * HEAD_DIM : start + 3 * HEAD_DIM]
    att_grad = shared[:, start + 3 * HEAD_DIM : edge]
    query_unit, query_inverse, query_normed = head_norm(query, query_gain[...])
    key_unit, key_inverse, key_normed = head_norm(key, key_gain[...])
    exponent = jnp.exp(dot(query_normed, key_normed, 1, 1) * score_scale)
    probs = exponent / jnp.sum(exponent, axis=1, keepdims=True)
    probs_low = probs.astype(BF16)
    attention[:, :HEAD_DIM] = dot(probs_low, value).astype(BF16)
    probs_grad = dot(att_grad, value, 1, 1)
    value_grad = dot(probs_low, att_grad, 0, 0)
    score_grad = (
        probs * (probs_grad - jnp.sum(probs * probs_grad, axis=1, keepdims=True)) * score_scale
    ).astype(BF16)
    qn_grad = dot(score_grad, key_normed)
    kn_grad = dot(score_grad, query_normed, 0, 0)
    backs = (
        head_norm_back(qn_grad, query_unit, query_inverse, query_gain[...]),
        head_norm_back(kn_grad, key_unit, key_inverse, key_gain[...]),
        value_grad,
    )
    for i, (back, rows) in enumerate(zip(backs, (query, key, value.astype(F32)))):
        back = back.astype(BF16)
        attention[:, (i + 1) * HEAD_DIM : (i + 2) * HEAD_DIM] = back
        back = back.astype(F32)
        grad_sum += jnp.sum(back * totals[i : i + 1, :], axis=1, keepdims=True)
        grad_project += jnp.sum(back * rows, axis=1, keepdims=True)
    grad_sum, grad_project = grad_sum / total, grad_project / total
    for index, gain, up, qkv, normed in (
        (core[0], own_gain, own_up, own_qkv, own_normed),
        (1 - core[0], other_gain, other_up, other_qkv, other_normed),
    ):
        unit_grad = gain[...] * (
            dot(shared[:, hidden_size:start], up[...], 1, 1)
            + dot(attention[:, HEAD_DIM:], qkv[...], 1, 1)
        )
        for y in range(2):
            at = slice(y * half, (y + 1) * half)
            unit_rows = (pair[2 * y + index, :, :width].astype(F32) - mean[at]) * inverse[at]
            normed[at, :] = (unit_rows * gain[...]).astype(BF16)
            parts[2 * y + index] = (
                inverse[at] * (unit_grad[at] - grad_sum[at] - unit_rows * grad_project[at])
            ).astype(BF16)


def call(kernel, outs, args, scratch=(), flops=0, scalars=0):
    size = sum(math.prod(a.shape) * a.dtype.itemsize for a in (*args, *outs))
    return pl.pallas_call(
        kernel,
        out_shape=outs,
        in_specs=[pl.BlockSpec(memory_space=pltpu.SMEM)] * scalars
        + [pl.BlockSpec(memory_space=pltpu.VMEM)] * (len(args) - scalars),
        out_specs=[pl.BlockSpec(memory_space=pltpu.VMEM)] * len(outs),
        scratch_shapes=scratch,
        compiler_params=pltpu.CompilerParams(vmem_limit_bytes=VMEM_BYTES),
        cost_estimate=pl.CostEstimate(flops=flops, bytes_accessed=size, transcendentals=0),
    )(*args)


def shape(dims, dtype=BF16):
    return jax.ShapeDtypeStruct(dims, dtype)


def local(
    inputs,
    cotangent,
    norm_gain,
    qkv_weight,
    out_weight,
    up_weight,
    down_weight,
    query_gain,
    key_gain,
):
    block, width = inputs.shape
    total = float(width * CHIPS * 2)
    image = block * Z_COUNT
    own = image // CHIPS
    half = image // 2
    hidden_size = up_weight.shape[1]
    head_size = out_weight.shape[0]
    heads3 = 3 * head_size
    edge = 2 * hidden_size + heads3 + head_size
    core = lax.axis_index("core").astype(jnp.int32).reshape(1)
    swap = [(0, 1), (1, 0)]

    (spread,) = call(spread_kernel, [shape((Z_COUNT, block, 2 * width))], (inputs, cotangent))
    both = lax.all_to_all(spread.reshape(-1, 2 * width), "z", 0, 0, tiled=True)

    flat_qkv = qkv_weight.reshape(width, heads3)
    own_weights = (norm_gain.reshape(1, width), up_weight, flat_qkv, down_weight, out_weight)
    other_weights = tuple(lax.ppermute(w, "core", swap) for w in own_weights)

    def column_sums(weights):
        gain, up, qkv = weights[:3]
        return jnp.concatenate(
            [exact("d,df->f", gain[0], up.astype(F32)), exact("d,df->f", gain[0], qkv.astype(F32))]
        )

    sums = column_sums(own_weights) + column_sums(other_weights)
    sum_rows = jnp.concatenate([p.reshape(-1, 128) for p in pieces(sums, 3)])
    sum_rows = jnp.pad(sum_rows, ((0, own - sum_rows.shape[0]), (0, 0)))

    low, high = both[:half], both[half:]
    pair = lax.all_to_all(
        jnp.concatenate([low, high, low, high]), ("y_lo", "core"), 0, 0, tiled=True
    ).reshape(4, half, 2 * width)
    weight_pairs = [w for two in zip(own_weights, other_weights) for w in two]
    (sent,) = call(
        forward_kernel,
        [shape((image, edge + 256))],
        (core, pair, *weight_pairs, sum_rows),
        scratch=[pltpu.VMEM((image, 2 * width), BF16)] * 2,
        flops=4 * image * width * edge,
        scalars=1,
    )
    got = lax.all_to_all(sent, ("y_hi", "x"), 0, 0, tiled=True).reshape(CHIPS, own, -1)
    share, totals = call(
        functools.partial(middle_kernel, hidden_size, 2 * width),
        [shape((CHIPS, own, edge + 128)), shape((8, 128), F32)],
        (got,),
    )
    shared = lax.all_to_all(share.reshape(image, -1), ("y_hi", "x"), 0, 0, tiled=True)
    parts, attention, own_normed, other_normed = call(
        functools.partial(backward_kernel, total),
        [
            shape((4, half, width)),
            shape((image, 4 * head_size)),
            shape((image, width)),
            shape((image, width)),
        ],
        (
            core,
            shared,
            pair,
            *weight_pairs[:6],
            totals,
            query_gain.reshape(1, -1),
            key_gain.reshape(1, -1),
        ),
        flops=4 * image * width * (hidden_size + heads3) + 14 * image * image * head_size,
        scalars=1,
    )
    parts = lax.all_to_all(
        parts.reshape(4 * half, width), ("y_lo", "core"), 0, 0, tiled=True
    ).reshape(2, image, width)
    parts = jnp.sum(parts.astype(F32), axis=0).astype(BF16)
    parts = lax.all_to_all(parts, "z", 0, 0, tiled=True).reshape(Z_COUNT, -1, width)
    input_grad = jnp.sum(parts.astype(F32), axis=0).astype(BF16)

    hidden, pre_grad = shared[:, :hidden_size], shared[:, hidden_size : 2 * hidden_size]
    attended, qkv_back = attention[:, :head_size], attention[:, head_size:]
    by_slice = pair.reshape(2, 2, half, 2 * width)[:, :, :, width:]

    def shares(normed, index):
        grads = lax.dynamic_index_in_dim(by_slice, index, 1, keepdims=False).reshape(image, width)
        return (
            product("td,tf->df", normed, qkv_back),
            product("th,td->hd", attended, grads),
            product("td,tf->df", normed, pre_grad),
            product("tf,td->fd", hidden, grads),
        )

    moved = [lax.ppermute(s, "core", swap) for s in shares(other_normed, 1 - core[0])]
    qkv_grad, out_grad, up_grad, down_grad = (
        (mine + theirs).astype(BF16) for mine, theirs in zip(shares(own_normed, core[0]), moved)
    )
    return (input_grad, qkv_grad.reshape(qkv_weight.shape), out_grad, up_grad, down_grad)


def solution(mesh):
    mesh = Mesh(mesh.devices.reshape(Z_COUNT, 2, 2, 4, 2), ("z", "y_lo", "y_hi", "x", "core"))
    hid, wid = ("z", "y_lo"), ("y_hi", "x", "core")
    return jax.shard_map(
        local,
        mesh=mesh,
        in_specs=(
            P(hid, wid),
            P(hid, wid),
            P(wid),
            P(wid, None, hid),
            P(hid, wid),
            P(wid, hid),
            P(hid, wid),
            P(),
            P(),
        ),
        out_specs=(
            P(hid, wid),
            P(wid, None, hid),
            P(hid, wid),
            P(wid, hid),
            P(hid, wid),
        ),
        check_vma=False,
    )
```

time: 168 us -> 145 us (0.86)
  the two profiles are of different devices: /device:TPU:16 before, /device:TPU:40 now
where the time goes in v3:
time: 145 us; the launch traced here: 144 us
  starting transfers between devices  54.5 us (38%)
  waiting for transfers between devices  41.1 us (28%)
  blocking collectives  22 us (15%)
  matrix products  11.6 us (8%)
  local copies, waits for them, and re-layouts  6.72 us (5%)
  Pallas kernels  4.31 us (3%)
  other arithmetic  2.35 us (2%)
    all_to_all x1, blocking collectives, local(): lax.all_to_all(sent, ('y_hi', 'x'), 0, 0, tiled=True)  22 us
    all_to_all x1, starting transfers between devices, local(): both = lax.all_to_all(spread.reshape(-1, 2 * width), 'z', 0, 0, tiled=True)  15.3 us
    all_to_all x1, waiting for transfers between devices, local(): lax.all_to_all(share.reshape(image, -1), ('y_hi', 'x'), 0, 0, tiled=True)  13.7 us
    ppermute x5, starting transfers between devices, local(): other_weights = tuple((lax.ppermute(w, 'core', swap) for w in own_weights))  10.6 us
    all_to_all x1, waiting for transfers between devices, local(): both = lax.all_to_all(spread.reshape(-1, 2 * width), 'z', 0, 0, tiled=True)  9.78 us
    all_to_all x1, waiting for transfers between devices, local(): lax.all_to_all(parts, 'z', 0, 0, tiled=True).reshape(Z_COUNT, -1, width)  9.57 us
    dot_general x8, matrix products, product(): return jnp.einsum(form, left_arr, right_arr, preferred_element_type=F32)  9.47 us
    ppermute x4, starting transfers between devices, local(): lax.ppermute(s, 'core', swap)  8.76 us
  transfers between devices with their start and end apart: 14, of which 4 were waited for; matrix products, arithmetic and copies ran while one was open for 11% of the time, Pallas kernels for 0%

profile of v3, /device:TPU:40, one launch (start us, length us, event | category | flops | bytes accessed | tf_op | source)
XLA Modules:
  0.0 143.6 jit_solution(6732086220384015169)
XLA Ops:
  0.7 0.7 copy-done.7
  1.4 0.7 copy-done.8
  2.1 0.8 shard_map.128
  2.9 15.3 %all-to-all-start = ((bf16[16,16,768]{2,1,0:T(8,128)(2,1)}), bf16[16,16,768]{2,1,0:T(8,128)(2,1)S(1)}, u32[]{:S(2)}, u32[]{:S(2)}) async-start(bf16[16,16,768]{2,1,0:T(8,128)(2,1)} %shard_map.128), calls=%async_computation | async-start | bytes 786432 | tf_op jit(solution)/shard_map/all_to_all | solution.py:326
  18.3 1.9 %collective-permute-start = (f32[1,384]{1,0:T(1,128)S(1)}, f32[1,384]{1,0:T(1,128)S(1)}, u32[]{:S(2)}, u32[]{:S(2)}) collective-permute-start(f32[1,384]{1,0:T(1,128)S(1)} %reshape.76.own_gain), channel_id=1, source_target_pairs={{0,1},{1,0},{2,3},{3,2},{4,5},{5,4},{6,7},{7,6},{8,9},{9,8},{10,11... | collective-permute-start | bytes 4616 | tf_op jit(solution)/shard_map/ppermute | solution.py:330
  20.2 2.4 %collective-permute-start.1 = (bf16[384,512]{1,0:T(8,128)(2,1)S(1)}, bf16[384,512]{1,0:T(8,128)(2,1)S(1)}, u32[]{:S(2)}, u32[]{:S(2)}) collective-permute-start(bf16[384,512]{1,0:T(8,128)(2,1)S(1)} %copy-done), channel_id=1, source_target_pairs={{0,1},{1,0},{2,3},{3,2},{4,5},{5,4},{6,7},{7,6},{8,9},{9,8},{10,11... | collective-permute-start | bytes 1179656 | tf_op jit(solution)/shard_map/ppermute | solution.py:330
  22.6 0.2 copy.23
  22.9 0.7 copy-done.11
  23.6 0.2 copy.25.own_qkv
  23.8 1.9 %collective-permute-start.2 = (bf16[384,384]{1,0:T(8,128)(2,1)S(1)}, bf16[384,384]{1,0:T(8,128)(2,1)S(1)}, u32[]{:S(2)}, u32[]{:S(2)}) collective-permute-start(bf16[384,384]{1,0:T(8,128)(2,1)S(1)} %copy.25.own_qkv), channel_id=1, source_target_pairs={{0,1},{1,0},{2,3},{3,2},{4,5},{5,4},{6,7},{7,6},{8,9},{9,8},{10,11... | collective-permute-start | bytes 884744 | tf_op jit(solution)/shard_map/ppermute | solution.py:330
  25.7 2.4 %collective-permute-start.3 = (bf16[512,384]{1,0:T(8,128)(2,1)S(1)}, bf16[512,384]{1,0:T(8,128)(2,1)S(1)}, u32[]{:S(2)}, u32[]{:S(2)}) collective-permute-start(bf16[512,384]{1,0:T(8,128)(2,1)S(1)} %copy-done.4), channel_id=1, source_target_pairs={{0,1},{1,0},{2,3},{3,2},{4,5},{5,4},{6,7},{7,6},{8,9},{9,8},{10,11... | collective-permute-start | bytes 1179656 | tf_op jit(solution)/shard_map/ppermute | solution.py:330
  28.1 1.9 %collective-permute-start.4 = (bf16[128,384]{1,0:T(8,128)(2,1)S(1)}, bf16[128,384]{1,0:T(8,128)(2,1)S(1)}, u32[]{:S(2)}, u32[]{:S(2)}) collective-permute-start(bf16[128,384]{1,0:T(8,128)(2,1)S(1)} %copy-done.6), channel_id=1, source_target_pairs={{0,1},{1,0},{2,3},{3,2},{4,5},{5,4},{6,7},{7,6},{8,9},{9,8},{10,11... | collective-permute-start | bytes 294920 | tf_op jit(solution)/shard_map/ppermute | solution.py:330
  30.1 0.3 fusion.27
  30.3 9.8 %all-to-all-done = bf16[16,16,768]{2,1,0:T(8,128)(2,1)S(1)} async-done(((bf16[16,16,768]{2,1,0:T(8,128)(2,1)}), bf16[16,16,768]{2,1,0:T(8,128)(2,1)S(1)}, u32[]{:S(2)}, u32[]{:S(2)}) %all-to-all-start) | async-done | bytes 393248 | tf_op jit(solution)/shard_map/all_to_all | solution.py:326
  40.1 0.9 pad_maximum_fusion
  41.1 3.9 %all-to-all-start.1 = ((bf16[4,128,768]{2,1,0:T(8,128)(2,1)}), bf16[4,128,768]{2,1,0:T(8,128)(2,1)S(1)}, u32[]{:S(2)}, u32[]{:S(2)}) async-start(bf16[4,128,768]{2,1,0:T(8,128)(2,1)} %bitcast.54), calls=%async_computation.1 | async-start | bytes 1572864 | tf_op jit(solution)/shard_map/all_to_all | solution.py:343
  45.0 1.4 convolution_reduce_fusion.1
  46.3 0.3 convolution_reduce_fusion
  46.6 0.3 fusion.25
  46.9 8.0 %all-to-all-done.1.pair = bf16[4,128,768]{2,1,0:T(8,128)(2,1)S(1)} async-done(((bf16[4,128,768]{2,1,0:T(8,128)(2,1)}), bf16[4,128,768]{2,1,0:T(8,128)(2,1)S(1)}, u32[]{:S(2)}, u32[]{:S(2)}) %all-to-all-start.1) | async-done | bytes 786464 | tf_op jit(solution)/shard_map/all_to_all | solution.py:343
  55.0 1.2 shard_map.129
  56.2 22.0 %all_to_all.50.got = bf16[8,32,1792]{2,1,0:T(8,128)(2,1)S(1)} all-to-all(bf16[8,32,1792]{2,1,0:T(8,128)(2,1)S(1)} %bitcast.51), channel_id=1, replica_groups=mesh['z'=16,'y_lo'=2,'y_hi'=2,'x'=4,'core'=2] {'y_hi','x'}, dimensions={0} | all-to-all | bytes 1835008 | tf_op jit(solution)/shard_map/all_to_all | solution.py:355
  78.2 0.5 shard_map.130
  78.7 0.9 copy-done.1
  79.6 3.5 %all-to-all-start.3 = ((bf16[8,32,1664]{2,1,0:T(8,128)(2,1)}), bf16[8,32,1664]{2,1,0:T(8,128)(2,1)S(1)}, u32[]{:S(2)}, u32[]{:S(2)}) async-start(bf16[8,32,1664]{2,1,0:T(8,128)(2,1)} %copy-done.1), calls=%async_computation.3 | async-start | bytes 1703936 | tf_op jit(solution)/shard_map/all_to_all | solution.py:361
  83.2 0.8 constant_dynamic-slice_fusion.1
  84.0 13.7 %all-to-all-done.3 = bf16[8,32,1664]{2,1,0:T(8,128)(2,1)S(1)} async-done(((bf16[8,32,1664]{2,1,0:T(8,128)(2,1)}), bf16[8,32,1664]{2,1,0:T(8,128)(2,1)S(1)}, u32[]{:S(2)}, u32[]{:S(2)}) %all-to-all-start.3) | async-done | bytes 852000 | tf_op jit(solution)/shard_map/all_to_all | solution.py:361
  97.7 1.8 %shard_map.131 = (bf16[4,128,384]{2,1,0:T(8,128)(2,1)S(1)}, bf16[256,512]{1,0:T(8,128)(2,1)S(1)}, bf16[256,384]{1,0:T(8,128)(2,1)S(1)}, bf16[256,384]{1,0:T(8,128)(2,1)S(1)}) custom-call(s32[1]{0:T(128)} %bitcast.core, bf16[256,1664]{1,0:T(8,128)(2,1)S(1)} %bitcast.46, bf16[4,128,768]{2,1,0:T(8,128)(2,1)S(1)} %all-to-all-done.1.pair, ...), custom_call_target="tpu_custom_call" | custom-call | flops 469762048 | bytes 4071428 | tf_op jit(solution)/shard_map/pallas_call | solution.py:286
  99.6 0.7 copy-done.2
  100.2 0.7 copy-done.5
  101.0 4.5 %all-to-all-start.4 = ((bf16[4,128,384]{2,1,0:T(8,128)(2,1)}), bf16[4,128,384]{2,1,0:T(8,128)(2,1)S(1)}, u32[]{:S(2)}, u32[]{:S(2)}) async-start(bf16[4,128,384]{2,1,0:T(8,128)(2,1)} %copy-done.5), calls=%async_computation.4 | async-start | bytes 786432 | tf_op jit(solution)/shard_map/all_to_all | solution.py:382
  105.5 0.3 fusion.7
  105.8 1.1 fusion.10
  106.9 2.2 %collective-permute-start.5 = (f32[384,384]{0,1:T(8,128)}, f32[384,384]{0,1:T(8,128)}, u32[]{:S(2)}, u32[]{:S(2)}) collective-permute-start(f32[384,384]{0,1:T(8,128)} %fusion.10), channel_id=1, source_target_pairs={{0,1},{1,0},{2,3},{3,2},{4,5},{5,4},{6,7},{7,6},{8,9},{9,8},{10,11... | collective-permute-start | bytes 1769480 | tf_op jit(solution)/shard_map/ppermute | solution.py:402
  109.1 0.2 fusion.13
  109.3 2.3 %collective-permute-start.6 = (f32[128,384]{1,0:T(8,128)S(1)}, f32[128,384]{1,0:T(8,128)S(1)}, u32[]{:S(2)}, u32[]{:S(2)}) collective-permute-start(f32[128,384]{1,0:T(8,128)S(1)} %fusion.13), channel_id=1, source_target_pairs={{0,1},{1,0},{2,3},{3,2},{4,5},{5,4},{6,7},{7,6},{8,9},{9,8},{10,11... | collective-permute-start | bytes 589832 | tf_op jit(solution)/shard_map/ppermute | solution.py:402
  111.6 2.1 %collective-permute-start.7 = (f32[384,512]{1,0:T(8,128)S(1)}, f32[384,512]{1,0:T(8,128)}, u32[]{:S(2)}, u32[]{:S(2)}) collective-permute-start(f32[384,512]{1,0:T(8,128)S(1)} %fusion.7), channel_id=1, source_target_pairs={{0,1},{1,0},{2,3},{3,2},{4,5},{5,4},{6,7},{7,6},{8,9},{9,8},{10,11... | collective-permute-start | bytes 2359304 | tf_op jit(solution)/shard_map/ppermute | solution.py:402
  113.7 1.3 fusion.4
  114.9 2.3 %collective-permute-start.8 = (f32[512,384]{1,0:T(8,128)}, f32[512,384]{1,0:T(8,128)}, u32[]{:S(2)}, u32[]{:S(2)}) collective-permute-start(f32[512,384]{1,0:T(8,128)} %fusion.4), channel_id=1, source_target_pairs={{0,1},{1,0},{2,3},{3,2},{4,5},{5,4},{6,7},{7,6},{8,9},{9,8},{10,11... | collective-permute-start | bytes 2359304 | tf_op jit(solution)/shard_map/ppermute | solution.py:402
  117.2 0.9 fusion.3
  118.1 0.7 bitcast_reduce_fusion
  118.8 7.9 %all-to-all-start.5 = ((bf16[16,16,384]{2,1,0:T(8,128)(2,1)}), bf16[16,16,384]{2,1,0:T(8,128)(2,1)S(1)}, u32[]{:S(2)}, u32[]{:S(2)}) async-start(bf16[16,16,384]{2,1,0:T(8,128)(2,1)} %bitcast.12), calls=%async_computation.5 | async-start | bytes 393216 | tf_op jit(solution)/shard_map/all_to_all | solution.py:386
  126.7 1.4 fusion.2
  128.1 0.9 copy.28
  129.0 2.2 %fusion = bf16[384,512]{1,0:T(8,128)(2,1)} fusion(f32[384,512]{1,0:T(8,128)} %collective-permute-done.7, bf16[256,384]{1,0:T(8,128)(2,1)S(1)} %get-tuple-element.14, bf16[256,1664]{1,0:T(8,128)(2,1)S(1)} %bitcast.49), kind=kOutput, calls=%fused_computation.3 | convolution fusion | flops 101056512 | bytes 1638400 | tf_op jit(solution)/shard_map/td,tf->df/dot_general | solution.py:23
  131.2 2.2 %fusion.1 = bf16[512,384]{1,0:T(8,128)(2,1)} fusion(f32[512,384]{1,0:T(8,128)} %collective-permute-done.8, bf16[256,384]{1,0:T(8,128)(2,1)S(1)} %bitcast.58, bf16[256,1664]{1,0:T(8,128)(2,1)S(1)} %bitcast.50), kind=kOutput, calls=%fused_computation.4 | convolution fusion | flops 101056512 | bytes 1638400 | tf_op jit(solution)/shard_map/tf,td->fd/dot_general | solution.py:23
  133.4 9.6 %all-to-all-done.5 = bf16[16,16,384]{2,1,0:T(8,128)(2,1)S(1)} async-done(((bf16[16,16,384]{2,1,0:T(8,128)(2,1)}), bf16[16,16,384]{2,1,0:T(8,128)(2,1)S(1)}, u32[]{:S(2)}, u32[]{:S(2)}) %all-to-all-start.5) | async-done | bytes 196640 | tf_op jit(solution)/shard_map/all_to_all | solution.py:386
  142.9 0.6 reduce_sum.25
  (41 shorter events, 0.2 us)
Async XLA Ops:
  0.6 19.6 %copy-start = (bf16[384,512]{1,0:T(8,128)(2,1)S(1)}, bf16[384,512]{1,0:T(8,128)(2,1)}, u32[]{:S(2)}) copy-start(bf16[384,512]{1,0:T(8,128)(2,1)} %own_up.3) | copy-start | bytes 1179652
  0.6 0.8 copy-start.7
  1.4 0.7 copy-start.8
  2.1 16.1 %copy-start.15 = (f32[384]{0:T(512)S(1)}, f32[384]{0:T(512)}, u32[]{:S(2)}) copy-start(f32[384]{0:T(512)} %param.11) | copy-start | bytes 4612
  2.1 20.5 %copy-start.14 = (bf16[384,3,128]{2,0,1:T(8,128)(2,1)S(1)}, bf16[384,3,128]{2,0,1:T(8,128)(2,1)}, u32[]{:S(2)}) copy-start(bf16[384,3,128]{2,0,1:T(8,128)(2,1)} %param.12) | copy-start | bytes 884740
  2.9 22.8 %copy-start.4 = (bf16[512,384]{1,0:T(8,128)(2,1)S(1)}, bf16[512,384]{1,0:T(8,128)(2,1)}, u32[]{:S(2)}) copy-start(bf16[512,384]{1,0:T(8,128)(2,1)} %own_down.1) | copy-start | bytes 1179652
  2.9 25.2 %copy-start.6 = (bf16[128,384]{1,0:T(8,128)(2,1)S(1)}, bf16[128,384]{1,0:T(8,128)(2,1)}, u32[]{:S(2)}) copy-start(bf16[128,384]{1,0:T(8,128)(2,1)} %own_out.1) | copy-start | bytes 294916
  2.9 37.2 %all-to-all-start = ((bf16[16,16,768]{2,1,0:T(8,128)(2,1)}), bf16[16,16,768]{2,1,0:T(8,128)(2,1)S(1)}, u32[]{:S(2)}, u32[]{:S(2)}) async-start(bf16[16,16,768]{2,1,0:T(8,128)(2,1)} %shard_map.128), calls=%async_computation | async-start | bytes 786432 | tf_op jit(solution)/shard_map/all_to_all | solution.py:326
  18.3 28.1 %collective-permute-start = (f32[1,384]{1,0:T(1,128)S(1)}, f32[1,384]{1,0:T(1,128)S(1)}, u32[]{:S(2)}, u32[]{:S(2)}) collective-permute-start(f32[1,384]{1,0:T(1,128)S(1)} %reshape.76.own_gain), channel_id=1, source_target_pairs={{0,1},{1,0},{2,3},{3,2},{4,5},{5,4},{6,7},{7,6},{8,9},{9,8},{10,11... | collective-permute-start | bytes 4616 | tf_op jit(solution)/shard_map/ppermute | solution.py:330
  20.2 26.4 %collective-permute-start.1 = (bf16[384,512]{1,0:T(8,128)(2,1)S(1)}, bf16[384,512]{1,0:T(8,128)(2,1)S(1)}, u32[]{:S(2)}, u32[]{:S(2)}) collective-permute-start(bf16[384,512]{1,0:T(8,128)(2,1)S(1)} %copy-done), channel_id=1, source_target_pairs={{0,1},{1,0},{2,3},{3,2},{4,5},{5,4},{6,7},{7,6},{8,9},{9,8},{10,11... | collective-permute-start | bytes 1179656 | tf_op jit(solution)/shard_map/ppermute | solution.py:330
  22.8 0.7 copy-start.11
  23.8 22.5 %collective-permute-start.2 = (bf16[384,384]{1,0:T(8,128)(2,1)S(1)}, bf16[384,384]{1,0:T(8,128)(2,1)S(1)}, u32[]{:S(2)}, u32[]{:S(2)}) collective-permute-start(bf16[384,384]{1,0:T(8,128)(2,1)S(1)} %copy.25.own_qkv), channel_id=1, source_target_pairs={{0,1},{1,0},{2,3},{3,2},{4,5},{5,4},{6,7},{7,6},{8,9},{9,8},{10,11... | collective-permute-start | bytes 884744 | tf_op jit(solution)/shard_map/ppermute | solution.py:330
  25.7 21.2 %collective-permute-start.3 = (bf16[512,384]{1,0:T(8,128)(2,1)S(1)}, bf16[512,384]{1,0:T(8,128)(2,1)S(1)}, u32[]{:S(2)}, u32[]{:S(2)}) collective-permute-start(bf16[512,384]{1,0:T(8,128)(2,1)S(1)} %copy-done.4), channel_id=1, source_target_pairs={{0,1},{1,0},{2,3},{3,2},{4,5},{5,4},{6,7},{7,6},{8,9},{9,8},{10,11... | collective-permute-start | bytes 1179656 | tf_op jit(solution)/shard_map/ppermute | solution.py:330
  28.1 18.8 %collective-permute-start.4 = (bf16[128,384]{1,0:T(8,128)(2,1)S(1)}, bf16[128,384]{1,0:T(8,128)(2,1)S(1)}, u32[]{:S(2)}, u32[]{:S(2)}) collective-permute-start(bf16[128,384]{1,0:T(8,128)(2,1)S(1)} %copy-done.6), channel_id=1, source_target_pairs={{0,1},{1,0},{2,3},{3,2},{4,5},{5,4},{6,7},{7,6},{8,9},{9,8},{10,11... | collective-permute-start | bytes 294920 | tf_op jit(solution)/shard_map/ppermute | solution.py:330
  41.1 13.9 %all-to-all-start.1 = ((bf16[4,128,768]{2,1,0:T(8,128)(2,1)}), bf16[4,128,768]{2,1,0:T(8,128)(2,1)S(1)}, u32[]{:S(2)}, u32[]{:S(2)}) async-start(bf16[4,128,768]{2,1,0:T(8,128)(2,1)} %bitcast.54), calls=%async_computation.1 | async-start | bytes 1572864 | tf_op jit(solution)/shard_map/all_to_all | solution.py:343
  78.7 0.9 copy-start.1
  79.6 18.1 %all-to-all-start.3 = ((bf16[8,32,1664]{2,1,0:T(8,128)(2,1)}), bf16[8,32,1664]{2,1,0:T(8,128)(2,1)S(1)}, u32[]{:S(2)}, u32[]{:S(2)}) async-start(bf16[8,32,1664]{2,1,0:T(8,128)(2,1)} %copy-done.1), calls=%async_computation.3 | async-start | bytes 1703936 | tf_op jit(solution)/shard_map/all_to_all | solution.py:361
  83.1 14.6 %copy-start.9 = (f32[128]{0:T(128)S(1)}, f32[128]{0:T(128)}, u32[]{:S(2)}) copy-start(f32[128]{0:T(128)} %param.16) | copy-start | bytes 1540
  83.1 14.6 %copy-start.10 = (f32[128]{0:T(128)S(1)}, f32[128]{0:T(128)}, u32[]{:S(2)}) copy-start(f32[128]{0:T(128)} %param.17) | copy-start | bytes 1540
  99.5 0.7 copy-start.2
  100.2 0.7 copy-start.5
  101.0 4.5 %copy-start.3 = (bf16[256,384]{1,0:T(8,128)(2,1)S(1)}, bf16[256,384]{1,0:T(8,128)(2,1)}, u32[]{:S(2)}) copy-start(bf16[256,384]{1,0:T(8,128)(2,1)} %copy-done.2) | copy-start | bytes 589828
  101.0 17.1 %all-to-all-start.4 = ((bf16[4,128,384]{2,1,0:T(8,128)(2,1)}), bf16[4,128,384]{2,1,0:T(8,128)(2,1)S(1)}, u32[]{:S(2)}, u32[]{:S(2)}) async-start(bf16[4,128,384]{2,1,0:T(8,128)(2,1)} %copy-done.5), calls=%async_computation.4 | async-start | bytes 786432 | tf_op jit(solution)/shard_map/all_to_all | solution.py:382
  105.5 3.6 %copy-start.13 = (bf16[2,1,128,384]{3,2,1,0:T(8,128)(2,1)S(1)}, bf16[2,1,128,384]{3,2,1,0:T(8,128)(2,1)}, u32[]{:S(2)}) copy-start(bf16[2,1,128,384]{3,2,1,0:T(8,128)(2,1)} %get-tuple-element.33) | copy-start | bytes 589828
  106.9 10.3 %copy-start.12 = (bf16[2,1,128,384]{3,2,1,0:T(8,128)(2,1)S(1)}, bf16[2,1,128,384]{3,2,1,0:T(8,128)(2,1)}, u32[]{:S(2)}) copy-start(bf16[2,1,128,384]{3,2,1,0:T(8,128)(2,1)} %get-tuple-element.32) | copy-start | bytes 589828
  106.9 19.8 %collective-permute-start.5 = (f32[384,384]{0,1:T(8,128)}, f32[384,384]{0,1:T(8,128)}, u32[]{:S(2)}, u32[]{:S(2)}) collective-permute-start(f32[384,384]{0,1:T(8,128)} %fusion.10), channel_id=1, source_target_pairs={{0,1},{1,0},{2,3},{3,2},{4,5},{5,4},{6,7},{7,6},{8,9},{9,8},{10,11... | collective-permute-start | bytes 1769480 | tf_op jit(solution)/shard_map/ppermute | solution.py:402
  109.3 7.9 %collective-permute-start.6 = (f32[128,384]{1,0:T(8,128)S(1)}, f32[128,384]{1,0:T(8,128)S(1)}, u32[]{:S(2)}, u32[]{:S(2)}) collective-permute-start(f32[128,384]{1,0:T(8,128)S(1)} %fusion.13), channel_id=1, source_target_pairs={{0,1},{1,0},{2,3},{3,2},{4,5},{5,4},{6,7},{7,6},{8,9},{9,8},{10,11... | collective-permute-start | bytes 589832 | tf_op jit(solution)/shard_map/ppermute | solution.py:402
  111.6 17.4 %collective-permute-start.7 = (f32[384,512]{1,0:T(8,128)S(1)}, f32[384,512]{1,0:T(8,128)}, u32[]{:S(2)}, u32[]{:S(2)}) collective-permute-start(f32[384,512]{1,0:T(8,128)S(1)} %fusion.7), channel_id=1, source_target_pairs={{0,1},{1,0},{2,3},{3,2},{4,5},{5,4},{6,7},{7,6},{8,9},{9,8},{10,11... | collective-permute-start | bytes 2359304 | tf_op jit(solution)/shard_map/ppermute | solution.py:402
  114.9 16.2 %collective-permute-start.8 = (f32[512,384]{1,0:T(8,128)}, f32[512,384]{1,0:T(8,128)}, u32[]{:S(2)}, u32[]{:S(2)}) collective-permute-start(f32[512,384]{1,0:T(8,128)} %fusion.4), channel_id=1, source_target_pairs={{0,1},{1,0},{2,3},{3,2},{4,5},{5,4},{6,7},{7,6},{8,9},{9,8},{10,11... | collective-permute-start | bytes 2359304 | tf_op jit(solution)/shard_map/ppermute | solution.py:402
  118.8 24.1 %all-to-all-start.5 = ((bf16[16,16,384]{2,1,0:T(8,128)(2,1)}), bf16[16,16,384]{2,1,0:T(8,128)(2,1)S(1)}, u32[]{:S(2)}, u32[]{:S(2)}) async-start(bf16[16,16,384]{2,1,0:T(8,128)(2,1)} %bitcast.12), calls=%async_computation.5 | async-start | bytes 393216 | tf_op jit(solution)/shard_map/all_to_all | solution.py:386

commit v4 on v3

--- a/solution.py
+++ b/solution.py
@@ -59,13 +59,6 @@
     return lax.dot_general(
         left, right, (((left_dim,), (right_dim,)), ((), ())), preferred_element_type=F32
     )
-
-
-def spread_kernel(inputs, cotangent, out):
-    width = inputs.shape[1]
-    for i in range(out.shape[0]):
-        out[i, :, :width] = inputs[...]
-        out[i, :, width:] = cotangent[...]
 
 
 def forward_kernel(
@@ -88,7 +81,7 @@
 ):
     own_index, other_index = core[0], 1 - core[0]
     half, width = pair.shape[1], own_gain.shape[1]
-    hidden_size, heads3 = own_up.shape[1], own_qkv.shape[1]
+    hidden_size, heads3 = own_up.shape[1], 3 * HEAD_DIM
     edge = 2 * hidden_size + heads3 + own_out.shape[0]
     for y in range(2):
         at = slice(y * half, (y + 1) * half)
@@ -112,7 +105,7 @@
     start = 0
     for own_weight, other_weight, first, dim in (
         (own_up, other_up, 0, 0),
-        (own_qkv, other_qkv, 0, 0),
+        *((own_qkv.at[i], other_qkv.at[i], 0, 0) for i in range(3)),
         (own_down, other_down, width, 1),
         (own_out, other_out, width, 1),
     ):
@@ -221,14 +214,18 @@
     query_gain,
     key_gain,
     parts,
-    attention,
     own_normed,
-    other_normed,
+    bundle,
 ):
     half, width = pair.shape[1], own_gain.shape[1]
     hidden_size = own_up.shape[1]
     start = 2 * hidden_size
     edge = start + 4 * HEAD_DIM
+    other_normed = bundle.at[:, edge : edge + width]
+    attention = bundle.at[:, start:edge]
+    bundle[:, :start] = shared[:, :start]
+    for y in range(2):
+        bundle[y * half : (y + 1) * half, edge + width :] = pair[2 * y + 1 - core[0], :, width:]
     score_scale = 1.0 / math.sqrt(HEAD_DIM)
 
     stats = shared[:, edge:].astype(F32)
@@ -270,7 +267,10 @@
     ):
         unit_grad = gain[...] * (
             dot(shared[:, hidden_size:start], up[...], 1, 1)
-            + dot(attention[:, HEAD_DIM:], qkv[...], 1, 1)
+            + sum(
+                dot(attention[:, (i + 1) * HEAD_DIM : (i + 2) * HEAD_DIM], qkv[i], 1, 1)
+                for i in range(3)
+            )
         )
         for y in range(2):
             at = slice(y * half, (y + 1) * half)
@@ -279,6 +279,30 @@
             parts[2 * y + index] = (
                 inverse[at] * (unit_grad[at] - grad_sum[at] - unit_rows * grad_project[at])
             ).astype(BF16)
+
+
+def weight_kernel(
+    hidden_size, core, bundle, theirs, normed, pair, qkv_out, out_out, up_out, down_out
+):
+    width = normed.shape[1]
+    start = 2 * hidden_size
+    edge = start + 4 * HEAD_DIM
+    mine = (normed[...], jnp.concatenate([pair[2 * y + core[0], :, width:] for y in range(2)]))
+    other = (theirs[:, edge : edge + width], theirs[:, edge + width :])
+
+    def both(side, first, last):
+        at = slice(first, last)
+        left, right = (mine[side], other[side]), (bundle[:, at], theirs[:, at])
+        if side == 1:
+            left, right = right, left
+        return (dot(left[0], right[0], 0, 0) + dot(left[1], right[1], 0, 0)).astype(BF16)
+
+    down_out[...] = both(1, 0, hidden_size)
+    up_out[...] = both(0, hidden_size, start)
+    out_out[...] = both(1, start, start + HEAD_DIM)
+    qkv = both(0, start + HEAD_DIM, edge)
+    for i in range(3):
+        qkv_out[i] = qkv[:, i * HEAD_DIM : (i + 1) * HEAD_DIM]
 
 
 def call(kernel, outs, args, scratch=(), flops=0, scalars=0):
@@ -322,17 +346,22 @@
     core = lax.axis_index("core").astype(jnp.int32).reshape(1)
     swap = [(0, 1), (1, 0)]
 
-    (spread,) = call(spread_kernel, [shape((Z_COUNT, block, 2 * width))], (inputs, cotangent))
-    both = lax.all_to_all(spread.reshape(-1, 2 * width), "z", 0, 0, tiled=True)
-
-    flat_qkv = qkv_weight.reshape(width, heads3)
-    own_weights = (norm_gain.reshape(1, width), up_weight, flat_qkv, down_weight, out_weight)
+    spread = jnp.broadcast_to(
+        jnp.concatenate([inputs, cotangent], axis=1), (Z_COUNT, block, 2 * width)
+    ).reshape(-1, 2 * width)
+    both = lax.all_to_all(spread, "z", 0, 0, tiled=True)
+
+    by_kind = jnp.transpose(qkv_weight, (1, 0, 2))
+    own_weights = (norm_gain.reshape(1, width), up_weight, by_kind, down_weight, out_weight)
     other_weights = tuple(lax.ppermute(w, "core", swap) for w in own_weights)
 
     def column_sums(weights):
         gain, up, qkv = weights[:3]
         return jnp.concatenate(
-            [exact("d,df->f", gain[0], up.astype(F32)), exact("d,df->f", gain[0], qkv.astype(F32))]
+            [
+                exact("d,df->f", gain[0], up.astype(F32)),
+                exact("d,cdj->cj", gain[0], qkv.astype(F32)).reshape(-1),
+            ]
         )
 
     sums = column_sums(own_weights) + column_sums(other_weights)
@@ -359,13 +388,12 @@
         (got,),
     )
     shared = lax.all_to_all(share.reshape(image, -1), ("y_hi", "x"), 0, 0, tiled=True)
-    parts, attention, own_normed, other_normed = call(
+    parts, own_normed, bundle = call(
         functools.partial(backward_kernel, total),
         [
             shape((4, half, width)),
-            shape((image, 4 * head_size)),
             shape((image, width)),
-            shape((image, width)),
+            shape((image, edge + 2 * width)),
         ],
         (
             core,
@@ -383,27 +411,26 @@
         parts.reshape(4 * half, width), ("y_lo", "core"), 0, 0, tiled=True
     ).reshape(2, image, width)
     parts = jnp.sum(parts.astype(F32), axis=0).astype(BF16)
-    parts = lax.all_to_all(parts, "z", 0, 0, tiled=True).reshape(Z_COUNT, -1, width)
-    input_grad = jnp.sum(parts.astype(F32), axis=0).astype(BF16)
-
-    hidden, pre_grad = shared[:, :hidden_size], shared[:, hidden_size : 2 * hidden_size]
-    attended, qkv_back = attention[:, :head_size], attention[:, head_size:]
-    by_slice = pair.reshape(2, 2, half, 2 * width)[:, :, :, width:]
-
-    def shares(normed, index):
-        grads = lax.dynamic_index_in_dim(by_slice, index, 1, keepdims=False).reshape(image, width)
-        return (
-            product("td,tf->df", normed, qkv_back),
-            product("th,td->hd", attended, grads),
-            product("td,tf->df", normed, pre_grad),
-            product("tf,td->fd", hidden, grads),
-        )
-
-    moved = [lax.ppermute(s, "core", swap) for s in shares(other_normed, 1 - core[0])]
-    qkv_grad, out_grad, up_grad, down_grad = (
-        (mine + theirs).astype(BF16) for mine, theirs in zip(shares(own_normed, core[0]), moved)
-    )
-    return (input_grad, qkv_grad.reshape(qkv_weight.shape), out_grad, up_grad, down_grad)
+    last = lax.all_to_all(parts, "z", 0, 0, tiled=True).reshape(Z_COUNT, -1, width)
+
+    theirs = lax.ppermute(bundle, "core", swap)
+    theirs, _ = lax.optimization_barrier((theirs, parts))
+    grads = call(
+        functools.partial(weight_kernel, hidden_size),
+        [
+            shape(by_kind.shape),
+            shape(out_weight.shape),
+            shape(up_weight.shape),
+            shape(down_weight.shape),
+        ],
+        (core, bundle, theirs, own_normed, pair),
+        flops=4 * image * width * edge,
+        scalars=1,
+    )
+    *grads, last = lax.optimization_barrier((*grads, last))
+    input_grad = jnp.sum(last.astype(F32), axis=0).astype(BF16)
+    qkv_grad, out_grad, up_grad, down_grad = grads
+    return (input_grad, jnp.transpose(qkv_grad, (1, 0, 2)), out_grad, up_grad, down_grad)
 
 
 def solution(mesh):

time: 145 us -> 135 us (0.931)
  the two profiles are of different devices: /device:TPU:40 before, /device:TPU:2 now
where the time goes in v4:
time: 135 us; the launch traced here: 134 us
  blocking collectives  47.8 us (35%)
  waiting for transfers between devices  37.6 us (28%)
  starting transfers between devices  37.2 us (28%)
  Pallas kernels  5.58 us (4%)
  other arithmetic  3.19 us (2%)
    all_to_all x1, blocking collectives, local(): lax.all_to_all(sent, ('y_hi', 'x'), 0, 0, tiled=True)  21.7 us
    all_to_all x1, blocking collectives, local(): lax.all_to_all(share.reshape(image, -1), ('y_hi', 'x'), 0, 0, tiled=True)  16.3 us
    all_to_all x1, starting transfers between devices, local(): both = lax.all_to_all(spread, 'z', 0, 0, tiled=True)  15.2 us
    all_to_all x1, waiting for transfers between devices, local(): lax.all_to_all(parts, 'z', 0, 0, tiled=True).reshape(Z_COUNT, -1, width)  14.4 us
    all_to_all x1, waiting for transfers between devices, local(): both = lax.all_to_all(spread, 'z', 0, 0, tiled=True)  12.8 us
    ppermute x5, starting transfers between devices, local(): other_weights = tuple((lax.ppermute(w, 'core', swap) for w in own_weights))  10.6 us
    all_to_all x1, waiting for transfers between devices, local(): lax.all_to_all(jnp.concatenate([low, high, low, high]), ('y_lo', 'core'),...  10.4 us
    all_to_all x1, blocking collectives, local(): lax.all_to_all(parts.reshape(4 * half, width), ('y_lo', 'core'), 0, 0, ti...  9.84 us
  transfers between devices with their start and end apart: 9, of which 3 were waited for; matrix products, arithmetic and copies ran while one was open for 2% of the time, Pallas kernels for 1%

profile of v4, /device:TPU:2, one launch (start us, length us, event | category | flops | bytes accessed | tf_op | source)
XLA Modules:
  0.0 134.4 jit_solution(4470801688591145987)
XLA Ops:
  0.6 0.0 copy-start.6
  0.6 0.0 copy-start.3
  0.7 0.0 copy-start.1
  0.7 0.0 copy-start.2
  0.7 0.0 copy-start
  0.7 0.8 pad_maximum_fusion.1
  1.5 0.8 broadcast_in_dim.3
  2.3 15.2 %all-to-all-start = ((bf16[16,16,768]{2,1,0:T(8,128)(2,1)}), bf16[16,16,768]{2,1,0:T(8,128)(2,1)S(1)}, u32[]{:S(2)}, u32[]{:S(2)}) async-start(bf16[16,16,768]{2,1,0:T(8,128)(2,1)} %broadcast_in_dim.3), calls=%async_computation | async-start | bytes 786432 | tf_op jit(solution)/shard_map/all_to_all | solution.py:352
  17.5 0.0 copy-done.6
  17.5 1.9 %collective-permute-start = (f32[1,384]{1,0:T(1,128)S(1)}, f32[1,384]{1,0:T(1,128)S(1)}, u32[]{:S(2)}, u32[]{:S(2)}) collective-permute-start(f32[1,384]{1,0:T(1,128)S(1)} %reshape.66.own_gain), channel_id=1, source_target_pairs={{0,1},{1,0},{2,3},{3,2},{4,5},{5,4},{6,7},{7,6},{8,9},{9,8},{10,11... | collective-permute-start | bytes 4616 | tf_op jit(solution)/shard_map/ppermute | solution.py:356
  19.4 0.0 copy-done.3
  19.4 2.4 %collective-permute-start.4 = (bf16[128,384]{1,0:T(8,128)(2,1)S(1)}, bf16[128,384]{1,0:T(8,128)(2,1)S(1)}, u32[]{:S(2)}, u32[]{:S(2)}) collective-permute-start(bf16[128,384]{1,0:T(8,128)(2,1)S(1)} %copy-done.3), channel_id=1, source_target_pairs={{0,1},{1,0},{2,3},{3,2},{4,5},{5,4},{6,7},{7,6},{8,9},{9,8},{10,11... | collective-permute-start | bytes 294920 | tf_op jit(solution)/shard_map/ppermute | solution.py:356
  21.9 0.0 copy-done.1
  21.9 1.9 %collective-permute-start.2 = (bf16[3,384,128]{2,1,0:T(8,128)(2,1)S(1)}, bf16[3,384,128]{2,1,0:T(8,128)(2,1)S(1)}, u32[]{:S(2)}, u32[]{:S(2)}) collective-permute-start(bf16[3,384,128]{2,1,0:T(8,128)(2,1)S(1)} %bitcast.45), channel_id=1, source_target_pairs={{0,1},{1,0},{2,3},{3,2},{4,5},{5,4},{6,7},{7,6},{8,9},{9,8},{10,11... | collective-permute-start | bytes 884744 | tf_op jit(solution)/shard_map/ppermute | solution.py:356
  23.8 0.0 copy-done.2
  23.8 2.4 %collective-permute-start.3 = (bf16[512,384]{1,0:T(8,128)(2,1)S(1)}, bf16[512,384]{1,0:T(8,128)(2,1)S(1)}, u32[]{:S(2)}, u32[]{:S(2)}) collective-permute-start(bf16[512,384]{1,0:T(8,128)(2,1)S(1)} %copy-done.2), channel_id=1, source_target_pairs={{0,1},{1,0},{2,3},{3,2},{4,5},{5,4},{6,7},{7,6},{8,9},{9,8},{10,11... | collective-permute-start | bytes 1179656 | tf_op jit(solution)/shard_map/ppermute | solution.py:356
  26.2 0.0 copy-done
  26.2 1.9 %collective-permute-start.1 = (bf16[384,512]{1,0:T(8,128)(2,1)S(1)}, bf16[384,512]{1,0:T(8,128)(2,1)S(1)}, u32[]{:S(2)}, u32[]{:S(2)}) collective-permute-start(bf16[384,512]{1,0:T(8,128)(2,1)S(1)} %copy-done), channel_id=1, source_target_pairs={{0,1},{1,0},{2,3},{3,2},{4,5},{5,4},{6,7},{7,6},{8,9},{9,8},{10,11... | collective-permute-start | bytes 1179656 | tf_op jit(solution)/shard_map/ppermute | solution.py:356
  28.2 0.3 fusion.13
  28.4 12.8 %all-to-all-done = bf16[16,16,768]{2,1,0:T(8,128)(2,1)S(1)} async-done(((bf16[16,16,768]{2,1,0:T(8,128)(2,1)}), bf16[16,16,768]{2,1,0:T(8,128)(2,1)S(1)}, u32[]{:S(2)}, u32[]{:S(2)}) %all-to-all-start) | async-done | bytes 393248 | tf_op jit(solution)/shard_map/all_to_all | solution.py:352
  41.3 1.0 pad_maximum_fusion
  42.2 3.5 %all-to-all-start.1 = ((bf16[4,128,768]{2,1,0:T(8,128)(2,1)}), bf16[4,128,768]{2,1,0:T(8,128)(2,1)S(1)}, u32[]{:S(2)}, u32[]{:S(2)}) async-start(bf16[4,128,768]{2,1,0:T(8,128)(2,1)} %bitcast.51), calls=%async_computation.1 | async-start | bytes 1572864 | tf_op jit(solution)/shard_map/all_to_all | solution.py:372
  45.7 0.2 fusion.11
  46.0 0.0 collective-permute-done.2.other_qkv
  46.0 0.2 copy.14
  46.2 0.0 collective-permute-done.other_gain
  46.2 0.4 convolution_reduce_fusion
  46.6 0.0 collective-permute-done.1.other_up
  46.6 0.3 fusion.9
  46.9 0.0 collective-permute-done.4.other_out
  46.9 0.0 collective-permute-done.3.other_down
  46.9 10.4 %all-to-all-done.1.pair = bf16[4,128,768]{2,1,0:T(8,128)(2,1)S(1)} async-done(((bf16[4,128,768]{2,1,0:T(8,128)(2,1)}), bf16[4,128,768]{2,1,0:T(8,128)(2,1)S(1)}, u32[]{:S(2)}, u32[]{:S(2)}) %all-to-all-start.1) | async-done | bytes 786464 | tf_op jit(solution)/shard_map/all_to_all | solution.py:372
  57.3 1.3 shard_map.128
  58.6 21.7 %all_to_all.50.got = bf16[8,32,1792]{2,1,0:T(8,128)(2,1)S(1)} all-to-all(bf16[8,32,1792]{2,1,0:T(8,128)(2,1)S(1)} %bitcast.43), channel_id=1, replica_groups=mesh['z'=16,'y_lo'=2,'y_hi'=2,'x'=4,'core'=2] {'y_hi','x'}, dimensions={0} | all-to-all | bytes 1835008 | tf_op jit(solution)/shard_map/all_to_all | solution.py:384
  80.3 0.0 copy-start.4
  80.3 0.5 shard_map.129
  80.8 16.3 %all_to_all.51 = bf16[8,32,1664]{2,1,0:T(8,128)(2,1)S(1)} all-to-all(bf16[8,32,1664]{2,1,0:T(8,128)(2,1)S(1)} %get-tuple-element.20), channel_id=1, replica_groups=mesh['z'=16,'y_lo'=2,'y_hi'=2,'x'=4,'core'=2] {'y_hi','x'}, dimensions={0} | all-to-all | bytes 1703936 | tf_op jit(solution)/shard_map/all_to_all | solution.py:390
  97.1 0.0 copy-done.4
  97.1 0.0 copy-done.5
  97.1 2.1 %shard_map.130 = (bf16[4,128,384]{2,1,0:T(8,128)(2,1)S(1)}, bf16[256,384]{1,0:T(8,128)(2,1)S(1)}, bf16[256,2304]{1,0:T(8,128)(2,1)S(1)}) custom-call(s32[1]{0:T(128)} %bitcast.2.core, bf16[256,1664]{1,0:T(8,128)(2,1)S(1)} %bitcast.44, bf16[4,128,768]{2,1,0:T(8,128)(2,1)S(1)} %all-to-all-done.1.pair, f32[1,384]{1,0:T(1,128)S(1)} %reshape.66.own_gain, ...), custom_call_target="tpu_custom_call" | custom-call | flops 469762048 | bytes 4792324 | tf_op jit(solution)/shard_map/pallas_call | solution.py:310
  99.2 1.9 %collective-permute-start.5 = (bf16[256,2304]{1,0:T(8,128)(2,1)S(1)}, bf16[256,2304]{1,0:T(8,128)(2,1)S(1)}, u32[]{:S(2)}, u32[]{:S(2)}) collective-permute-start(bf16[256,2304]{1,0:T(8,128)(2,1)S(1)} %get-tuple-element.22.bundle), channel_id=1, source_target_pairs={{0,1},{1,0},{2,3},{3,2},{4,5},{5,4},{6,7},{7,6},{8,9},{9,8},{10,11... | collective-permute-start | bytes 3538952 | tf_op jit(solution)/shard_map/ppermute | solution.py:416
  101.1 9.8 %all_to_all.52 = bf16[4,128,384]{2,1,0:T(8,128)(2,1)S(1)} all-to-all(bf16[4,128,384]{2,1,0:T(8,128)(2,1)S(1)} %get-tuple-element.23), channel_id=1, replica_groups=mesh['z'=16,'y_lo'=2,'y_hi'=2,'x'=4,'core'=2] {'y_lo','core'}, dimensions={0} | all-to-all | bytes 786432 | tf_op jit(solution)/shard_map/all_to_all | solution.py:410
  110.9 0.7 bitcast_reduce_fusion
  111.7 6.0 %all-to-all-start.5 = ((bf16[16,16,384]{2,1,0:T(8,128)(2,1)}), bf16[16,16,384]{2,1,0:T(8,128)(2,1)S(1)}, u32[]{:S(2)}, u32[]{:S(2)}) async-start(bf16[16,16,384]{2,1,0:T(8,128)(2,1)} %bitcast.55), calls=%async_computation.5 | async-start | bytes 393216 | tf_op jit(solution)/shard_map/all_to_all | solution.py:414
  117.7 0.0 collective-permute-done.5.theirs
  117.7 1.8 %shard_map.131 = (bf16[3,384,128]{2,1,0:T(8,128)(2,1)}, bf16[128,384]{1,0:T(8,128)(2,1)}, bf16[384,512]{1,0:T(8,128)(2,1)}, bf16[512,384]{1,0:T(8,128)(2,1)}) custom-call(s32[1]{0:T(128)} %bitcast.2.core, bf16[256,2304]{1,0:T(8,128)(2,1)S(1)} %get-tuple-element.22.bundle, bf16[256,2304]{1,0:T(8,128)(2,1)S(1)} %collective-permute-done.5.theirs, ...), custom_call_target="tpu_custom_call" | custom-call | flops 603979776 | bytes 4521988 | tf_op jit(solution)/shard_map/pallas_call | solution.py:310
  119.4 14.4 %all-to-all-done.5 = bf16[16,16,384]{2,1,0:T(8,128)(2,1)S(1)} async-done(((bf16[16,16,384]{2,1,0:T(8,128)(2,1)}), bf16[16,16,384]{2,1,0:T(8,128)(2,1)S(1)}, u32[]{:S(2)}, u32[]{:S(2)}) %all-to-all-start.5) | async-done | bytes 196640 | tf_op jit(solution)/shard_map/all_to_all | solution.py:414
  133.8 0.6 reduce_sum.25
  (7 shorter events, 0.0 us)
Async XLA Ops:
  0.6 16.9 %copy-start.6 = (f32[384]{0:T(512)S(1)}, f32[384]{0:T(512)}, u32[]{:S(2)}) copy-start(f32[384]{0:T(512)} %param.11) | copy-start | bytes 4612
  0.6 18.8 %copy-start.3 = (bf16[128,384]{1,0:T(8,128)(2,1)S(1)}, bf16[128,384]{1,0:T(8,128)(2,1)}, u32[]{:S(2)}) copy-start(bf16[128,384]{1,0:T(8,128)(2,1)} %own_out.1) | copy-start | bytes 294916
  0.7 21.2 %copy-start.1 = (bf16[384,3,128]{2,0,1:T(8,128)(2,1)S(1)}, bf16[384,3,128]{2,0,1:T(8,128)(2,1)}, u32[]{:S(2)}) copy-start(bf16[384,3,128]{2,0,1:T(8,128)(2,1)} %param.12) | copy-start | bytes 884740
  0.7 23.1 %copy-start.2 = (bf16[512,384]{1,0:T(8,128)(2,1)S(1)}, bf16[512,384]{1,0:T(8,128)(2,1)}, u32[]{:S(2)}) copy-start(bf16[512,384]{1,0:T(8,128)(2,1)} %own_down.1) | copy-start | bytes 1179652
  0.7 25.5 %copy-start = (bf16[384,512]{1,0:T(8,128)(2,1)S(1)}, bf16[384,512]{1,0:T(8,128)(2,1)}, u32[]{:S(2)}) copy-start(bf16[384,512]{1,0:T(8,128)(2,1)} %own_up.3) | copy-start | bytes 1179652
  2.3 39.0 %all-to-all-start = ((bf16[16,16,768]{2,1,0:T(8,128)(2,1)}), bf16[16,16,768]{2,1,0:T(8,128)(2,1)S(1)}, u32[]{:S(2)}, u32[]{:S(2)}) async-start(bf16[16,16,768]{2,1,0:T(8,128)(2,1)} %broadcast_in_dim.3), calls=%async_computation | async-start | bytes 786432 | tf_op jit(solution)/shard_map/all_to_all | solution.py:352
  17.5 28.7 %collective-permute-start = (f32[1,384]{1,0:T(1,128)S(1)}, f32[1,384]{1,0:T(1,128)S(1)}, u32[]{:S(2)}, u32[]{:S(2)}) collective-permute-start(f32[1,384]{1,0:T(1,128)S(1)} %reshape.66.own_gain), channel_id=1, source_target_pairs={{0,1},{1,0},{2,3},{3,2},{4,5},{5,4},{6,7},{7,6},{8,9},{9,8},{10,11... | collective-permute-start | bytes 4616 | tf_op jit(solution)/shard_map/ppermute | solution.py:356
  19.4 27.5 %collective-permute-start.4 = (bf16[128,384]{1,0:T(8,128)(2,1)S(1)}, bf16[128,384]{1,0:T(8,128)(2,1)S(1)}, u32[]{:S(2)}, u32[]{:S(2)}) collective-permute-start(bf16[128,384]{1,0:T(8,128)(2,1)S(1)} %copy-done.3), channel_id=1, source_target_pairs={{0,1},{1,0},{2,3},{3,2},{4,5},{5,4},{6,7},{7,6},{8,9},{9,8},{10,11... | collective-permute-start | bytes 294920 | tf_op jit(solution)/shard_map/ppermute | solution.py:356
  21.9 24.1 %collective-permute-start.2 = (bf16[3,384,128]{2,1,0:T(8,128)(2,1)S(1)}, bf16[3,384,128]{2,1,0:T(8,128)(2,1)S(1)}, u32[]{:S(2)}, u32[]{:S(2)}) collective-permute-start(bf16[3,384,128]{2,1,0:T(8,128)(2,1)S(1)} %bitcast.45), channel_id=1, source_target_pairs={{0,1},{1,0},{2,3},{3,2},{4,5},{5,4},{6,7},{7,6},{8,9},{9,8},{10,11... | collective-permute-start | bytes 884744 | tf_op jit(solution)/shard_map/ppermute | solution.py:356
  23.8 23.1 %collective-permute-start.3 = (bf16[512,384]{1,0:T(8,128)(2,1)S(1)}, bf16[512,384]{1,0:T(8,128)(2,1)S(1)}, u32[]{:S(2)}, u32[]{:S(2)}) collective-permute-start(bf16[512,384]{1,0:T(8,128)(2,1)S(1)} %copy-done.2), channel_id=1, source_target_pairs={{0,1},{1,0},{2,3},{3,2},{4,5},{5,4},{6,7},{7,6},{8,9},{9,8},{10,11... | collective-permute-start | bytes 1179656 | tf_op jit(solution)/shard_map/ppermute | solution.py:356
  26.2 20.4 %collective-permute-start.1 = (bf16[384,512]{1,0:T(8,128)(2,1)S(1)}, bf16[384,512]{1,0:T(8,128)(2,1)S(1)}, u32[]{:S(2)}, u32[]{:S(2)}) collective-permute-start(bf16[384,512]{1,0:T(8,128)(2,1)S(1)} %copy-done), channel_id=1, source_target_pairs={{0,1},{1,0},{2,3},{3,2},{4,5},{5,4},{6,7},{7,6},{8,9},{9,8},{10,11... | collective-permute-start | bytes 1179656 | tf_op jit(solution)/shard_map/ppermute | solution.py:356
  42.2 15.1 %all-to-all-start.1 = ((bf16[4,128,768]{2,1,0:T(8,128)(2,1)}), bf16[4,128,768]{2,1,0:T(8,128)(2,1)S(1)}, u32[]{:S(2)}, u32[]{:S(2)}) async-start(bf16[4,128,768]{2,1,0:T(8,128)(2,1)} %bitcast.51), calls=%async_computation.1 | async-start | bytes 1572864 | tf_op jit(solution)/shard_map/all_to_all | solution.py:372
  80.3 16.8 %copy-start.4 = (f32[128]{0:T(128)S(1)}, f32[128]{0:T(128)}, u32[]{:S(2)}) copy-start(f32[128]{0:T(128)} %param.16) | copy-start | bytes 1540
  80.3 16.8 %copy-start.5 = (f32[128]{0:T(128)S(1)}, f32[128]{0:T(128)}, u32[]{:S(2)}) copy-start(f32[128]{0:T(128)} %param.17) | copy-start | bytes 1540
  99.2 18.5 %collective-permute-start.5 = (bf16[256,2304]{1,0:T(8,128)(2,1)S(1)}, bf16[256,2304]{1,0:T(8,128)(2,1)S(1)}, u32[]{:S(2)}, u32[]{:S(2)}) collective-permute-start(bf16[256,2304]{1,0:T(8,128)(2,1)S(1)} %get-tuple-element.22.bundle), channel_id=1, source_target_pairs={{0,1},{1,0},{2,3},{3,2},{4,5},{5,4},{6,7},{7,6},{8,9},{9,8},{10,11... | collective-permute-start | bytes 3538952 | tf_op jit(solution)/shard_map/ppermute | solution.py:416
  111.7 22.1 %all-to-all-start.5 = ((bf16[16,16,384]{2,1,0:T(8,128)(2,1)}), bf16[16,16,384]{2,1,0:T(8,128)(2,1)S(1)}, u32[]{:S(2)}, u32[]{:S(2)}) async-start(bf16[16,16,384]{2,1,0:T(8,128)(2,1)} %bitcast.55), calls=%async_computation.5 | async-start | bytes 393216 | tf_op jit(solution)/shard_map/all_to_all | solution.py:414

commit v5 on v4

--- a/solution.py
+++ b/solution.py
@@ -14,6 +14,9 @@
 EPSILON = 1e-06
 Z_COUNT = 16
 CHIPS = 8
+ALONG_Z = [8, 9, 10, 11, 12, 13, 14, 15, 0, 1, 2, 3, 4, 5, 6, 7]
+WITHIN = [1, 0, 3, 2]
+ACROSS = [6, 7, 4, 5, 2, 3, 0, 1]
 VMEM_BYTES = 24 * 1024 * 1024
 F32 = jnp.float32
 BF16 = jnp.bfloat16
@@ -79,7 +82,7 @@
     own_rows,
     other_rows,
 ):
-    own_index, other_index = core[0], 1 - core[0]
+    own_index, other_index = 1 - core[0], core[0]
     half, width = pair.shape[1], own_gain.shape[1]
     hidden_size, heads3 = own_up.shape[1], 3 * HEAD_DIM
     edge = 2 * hidden_size + heads3 + own_out.shape[0]
@@ -225,7 +228,7 @@
     attention = bundle.at[:, start:edge]
     bundle[:, :start] = shared[:, :start]
     for y in range(2):
-        bundle[y * half : (y + 1) * half, edge + width :] = pair[2 * y + 1 - core[0], :, width:]
+        bundle[y * half : (y + 1) * half, edge + width :] = pair[2 * y + core[0], :, width:]
     score_scale = 1.0 / math.sqrt(HEAD_DIM)
 
     stats = shared[:, edge:].astype(F32)
@@ -262,8 +265,8 @@
         grad_project += jnp.sum(back * rows, axis=1, keepdims=True)
     grad_sum, grad_project = grad_sum / total, grad_project / total
     for index, gain, up, qkv, normed in (
-        (core[0], own_gain, own_up, own_qkv, own_normed),
-        (1 - core[0], other_gain, other_up, other_qkv, other_normed),
+        (1 - core[0], own_gain, own_up, own_qkv, own_normed),
+        (core[0], other_gain, other_up, other_qkv, other_normed),
     ):
         unit_grad = gain[...] * (
             dot(shared[:, hidden_size:start], up[...], 1, 1)
@@ -287,7 +290,7 @@
     width = normed.shape[1]
     start = 2 * hidden_size
     edge = start + 4 * HEAD_DIM
-    mine = (normed[...], jnp.concatenate([pair[2 * y + core[0], :, width:] for y in range(2)]))
+    mine = (normed[...], jnp.concatenate([pair[2 * y + 1 - core[0], :, width:] for y in range(2)]))
     other = (theirs[:, edge : edge + width], theirs[:, edge + width :])
 
     def both(side, first, last):
@@ -321,6 +324,10 @@
 
 def shape(dims, dtype=BF16):
     return jax.ShapeDtypeStruct(dims, dtype)
+
+
+def to_each(rows, axis, order):
+    return lax.all_to_all(rows, axis, 0, 0, tiled=True, axis_index_groups=[order])
 
 
 def local(
@@ -349,7 +356,7 @@
     spread = jnp.broadcast_to(
         jnp.concatenate([inputs, cotangent], axis=1), (Z_COUNT, block, 2 * width)
     ).reshape(-1, 2 * width)
-    both = lax.all_to_all(spread, "z", 0, 0, tiled=True)
+    both = to_each(spread, "z", ALONG_Z)
 
     by_kind = jnp.transpose(qkv_weight, (1, 0, 2))
     own_weights = (norm_gain.reshape(1, width), up_weight, by_kind, down_weight, out_weight)
@@ -368,10 +375,8 @@
     sum_rows = jnp.concatenate([p.reshape(-1, 128) for p in pieces(sums, 3)])
     sum_rows = jnp.pad(sum_rows, ((0, own - sum_rows.shape[0]), (0, 0)))
 
-    low, high = both[:half], both[half:]
-    pair = lax.all_to_all(
-        jnp.concatenate([low, high, low, high]), ("y_lo", "core"), 0, 0, tiled=True
-    ).reshape(4, half, 2 * width)
+    pair = to_each(jnp.concatenate([both, both]), ("y_lo", "core"), WITHIN)
+    pair = pair.reshape(4, half, 2 * width)
     weight_pairs = [w for two in zip(own_weights, other_weights) for w in two]
     (sent,) = call(
         forward_kernel,
@@ -381,13 +386,13 @@
         flops=4 * image * width * edge,
         scalars=1,
     )
-    got = lax.all_to_all(sent, ("y_hi", "x"), 0, 0, tiled=True).reshape(CHIPS, own, -1)
+    got = to_each(sent, ("y_hi", "x"), ACROSS).reshape(CHIPS, own, -1)
     share, totals = call(
         functools.partial(middle_kernel, hidden_size, 2 * width),
         [shape((CHIPS, own, edge + 128)), shape((8, 128), F32)],
         (got,),
     )
-    shared = lax.all_to_all(share.reshape(image, -1), ("y_hi", "x"), 0, 0, tiled=True)
+    shared = to_each(share.reshape(image, -1), ("y_hi", "x"), ACROSS)
     parts, own_normed, bundle = call(
         functools.partial(backward_kernel, total),
         [
@@ -407,11 +412,10 @@
         flops=4 * image * width * (hidden_size + heads3) + 14 * image * image * head_size,
         scalars=1,
     )
-    parts = lax.all_to_all(
-        parts.reshape(4 * half, width), ("y_lo", "core"), 0, 0, tiled=True
-    ).reshape(2, image, width)
+    parts = to_each(parts.reshape(4 * half, width), ("y_lo", "core"), WITHIN)
+    parts = parts.reshape(2, image, width)
     parts = jnp.sum(parts.astype(F32), axis=0).astype(BF16)
-    last = lax.all_to_all(parts, "z", 0, 0, tiled=True).reshape(Z_COUNT, -1, width)
+    last = to_each(parts, "z", ALONG_Z).reshape(Z_COUNT, -1, width)
 
     theirs = lax.ppermute(bundle, "core", swap)
     theirs, _ = lax.optimization_barrier((theirs, parts))

time: 135 us -> 128 us (0.948)
  the two profiles are of different devices: /device:TPU:2 before, /device:TPU:1 now
where the time goes in v5:
time: 128 us; the launch traced here: 127 us
  starting transfers between devices  50.5 us (39%)
  blocking collectives  42.4 us (33%)
  waiting for transfers between devices  22 us (17%)
  Pallas kernels  5.57 us (4%)
  other arithmetic  3.19 us (2%)
    all_to_all x3, blocking collectives, to_each(): lax.all_to_all(rows, axis, 0, 0, tiled=True, axis_index_groups=[order])  42.4 us
    all_to_all x3, starting transfers between devices, to_each(): lax.all_to_all(rows, axis, 0, 0, tiled=True, axis_index_groups=[order])  34.1 us
    all_to_all x3, waiting for transfers between devices, to_each(): lax.all_to_all(rows, axis, 0, 0, tiled=True, axis_index_groups=[order])  22 us
    ppermute x5, starting transfers between devices, local(): other_weights = tuple((lax.ppermute(w, 'core', swap) for w in own_weights))  11.8 us
    pallas_call x4, Pallas kernels, call(): pl.pallas_call(kernel, out_shape=outs, in_specs=[pl.BlockSpec(memory_spac...  5.57 us
    ppermute x1, starting transfers between devices, local(): theirs = lax.ppermute(bundle, 'core', swap)  4.65 us
  transfers between devices with their start and end apart: 9, of which 3 were waited for; matrix products, arithmetic and copies ran while one was open for 2% of the time, Pallas kernels for 1%

profile of v5, /device:TPU:1, one launch (start us, length us, event | category | flops | bytes accessed | tf_op | source)
XLA Modules:
  0.0 126.8 jit_solution(1178823906472196544)
XLA Ops:
  0.6 0.0 copy-start.6
  0.6 0.0 copy-start.3
  0.7 0.0 copy-start.1
  0.7 0.0 copy-start.2
  0.7 0.0 copy-start
  0.7 0.8 pad_maximum_fusion.1
  1.5 0.8 broadcast_in_dim.3
  2.3 19.1 %all-to-all-start = ((bf16[16,16,768]{2,1,0:T(8,128)(2,1)}), bf16[16,16,768]{2,1,0:T(8,128)(2,1)S(1)}, u32[]{:S(2)}, u32[]{:S(2)}) async-start(bf16[16,16,768]{2,1,0:T(8,128)(2,1)} %broadcast_in_dim.3), calls=%async_computation | async-start | bytes 786432 | tf_op jit(solution)/shard_map/all_to_all | solution.py:330
  21.4 0.0 copy-done.6
  21.4 3.1 %collective-permute-start = (f32[1,384]{1,0:T(1,128)S(1)}, f32[1,384]{1,0:T(1,128)S(1)}, u32[]{:S(2)}, u32[]{:S(2)}) collective-permute-start(f32[1,384]{1,0:T(1,128)S(1)} %reshape.66.own_gain), channel_id=1, source_target_pairs={{0,1},{1,0},{2,3},{3,2},{4,5},{5,4},{6,7},{7,6},{8,9},{9,8},{10,11... | collective-permute-start | bytes 4616 | tf_op jit(solution)/shard_map/ppermute | solution.py:363
  24.6 0.0 copy-done.3
  24.6 1.9 %collective-permute-start.4 = (bf16[128,384]{1,0:T(8,128)(2,1)S(1)}, bf16[128,384]{1,0:T(8,128)(2,1)S(1)}, u32[]{:S(2)}, u32[]{:S(2)}) collective-permute-start(bf16[128,384]{1,0:T(8,128)(2,1)S(1)} %copy-done.3), channel_id=1, source_target_pairs={{0,1},{1,0},{2,3},{3,2},{4,5},{5,4},{6,7},{7,6},{8,9},{9,8},{10,11... | collective-permute-start | bytes 294920 | tf_op jit(solution)/shard_map/ppermute | solution.py:363
  26.5 0.0 copy-done.1
  26.5 2.4 %collective-permute-start.2 = (bf16[3,384,128]{2,1,0:T(8,128)(2,1)S(1)}, bf16[3,384,128]{2,1,0:T(8,128)(2,1)S(1)}, u32[]{:S(2)}, u32[]{:S(2)}) collective-permute-start(bf16[3,384,128]{2,1,0:T(8,128)(2,1)S(1)} %bitcast.45), channel_id=1, source_target_pairs={{0,1},{1,0},{2,3},{3,2},{4,5},{5,4},{6,7},{7,6},{8,9},{9,8},{10,11... | collective-permute-start | bytes 884744 | tf_op jit(solution)/shard_map/ppermute | solution.py:363
  28.9 0.0 copy-done.2
  28.9 1.9 %collective-permute-start.3 = (bf16[512,384]{1,0:T(8,128)(2,1)S(1)}, bf16[512,384]{1,0:T(8,128)(2,1)S(1)}, u32[]{:S(2)}, u32[]{:S(2)}) collective-permute-start(bf16[512,384]{1,0:T(8,128)(2,1)S(1)} %copy-done.2), channel_id=1, source_target_pairs={{0,1},{1,0},{2,3},{3,2},{4,5},{5,4},{6,7},{7,6},{8,9},{9,8},{10,11... | collective-permute-start | bytes 1179656 | tf_op jit(solution)/shard_map/ppermute | solution.py:363
  30.9 0.0 copy-done
  30.9 2.4 %collective-permute-start.1 = (bf16[384,512]{1,0:T(8,128)(2,1)S(1)}, bf16[384,512]{1,0:T(8,128)(2,1)S(1)}, u32[]{:S(2)}, u32[]{:S(2)}) collective-permute-start(bf16[384,512]{1,0:T(8,128)(2,1)S(1)} %copy-done), channel_id=1, source_target_pairs={{0,1},{1,0},{2,3},{3,2},{4,5},{5,4},{6,7},{7,6},{8,9},{9,8},{10,11... | collective-permute-start | bytes 1179656 | tf_op jit(solution)/shard_map/ppermute | solution.py:363
  33.3 0.3 fusion.13
  33.6 5.8 %all-to-all-done = bf16[16,16,768]{2,1,0:T(8,128)(2,1)S(1)} async-done(((bf16[16,16,768]{2,1,0:T(8,128)(2,1)}), bf16[16,16,768]{2,1,0:T(8,128)(2,1)S(1)}, u32[]{:S(2)}, u32[]{:S(2)}) %all-to-all-start) | async-done | bytes 393248 | tf_op jit(solution)/shard_map/all_to_all | solution.py:330
  39.4 1.0 pad_maximum_fusion
  40.4 3.5 %all-to-all-start.1 = ((bf16[4,128,768]{2,1,0:T(8,128)(2,1)}), bf16[4,128,768]{2,1,0:T(8,128)(2,1)S(1)}, u32[]{:S(2)}, u32[]{:S(2)}) async-start(bf16[4,128,768]{2,1,0:T(8,128)(2,1)} %bitcast.51), calls=%async_computation.1 | async-start | bytes 1572864 | tf_op jit(solution)/shard_map/all_to_all | solution.py:330
  43.9 0.2 fusion.11
  44.1 0.0 collective-permute-done.2.other_qkv
  44.1 0.2 copy.14
  44.4 0.0 collective-permute-done.other_gain
  44.4 0.4 convolution_reduce_fusion
  44.8 0.0 collective-permute-done.1.other_up
  44.8 0.3 fusion.9
  45.1 0.0 collective-permute-done.4.other_out
  45.1 0.0 collective-permute-done.3.other_down
  45.1 9.1 %all-to-all-done.1.pair = bf16[4,128,768]{2,1,0:T(8,128)(2,1)S(1)} async-done(((bf16[4,128,768]{2,1,0:T(8,128)(2,1)}), bf16[4,128,768]{2,1,0:T(8,128)(2,1)S(1)}, u32[]{:S(2)}, u32[]{:S(2)}) %all-to-all-start.1) | async-done | bytes 786464 | tf_op jit(solution)/shard_map/all_to_all | solution.py:330
  54.2 1.3 %shard_map.128 = bf16[256,1792]{1,0:T(8,128)(2,1)S(1)} custom-call(s32[1]{0:T(128)} %bitcast.2.core, bf16[4,128,768]{2,1,0:T(8,128)(2,1)S(1)} %all-to-all-done.1.pair, f32[1,384]{1,0:T(1,128)S(1)} %reshape.66.own_gain, f32[1,384]{1,0:T(1,128)S(1)} %collective-permute-done.other_gain, bf16[384,512]{1,0:T(8,128)(2,1)S(1)} %copy-done, ...), custom_call_target="tpu_custom_call" | custom-call | flops 603979776 | bytes 4074500 | tf_op jit(solution)/shard_map/pallas_call | solution.py:313
  55.5 18.5 %all_to_all.50.got = bf16[8,32,1792]{2,1,0:T(8,128)(2,1)S(1)} all-to-all(bf16[8,32,1792]{2,1,0:T(8,128)(2,1)S(1)} %bitcast.43), channel_id=1, replica_groups={{12,14,8,10,4,6,0,2},{13,15,9,11,5,7,1,3},{28,30,24,26,20,22,16,18},{29..., dimensions={0} | all-to-all | bytes 1835008 | tf_op jit(solution)/shard_map/all_to_all | solution.py:330
  74.0 0.0 copy-start.4
  74.0 0.5 shard_map.129
  74.5 15.0 %all_to_all.51 = bf16[8,32,1664]{2,1,0:T(8,128)(2,1)S(1)} all-to-all(bf16[8,32,1664]{2,1,0:T(8,128)(2,1)S(1)} %get-tuple-element.20), channel_id=1, replica_groups={{12,14,8,10,4,6,0,2},{13,15,9,11,5,7,1,3},{28,30,24,26,20,22,16,18},{29..., dimensions={0} | all-to-all | bytes 1703936 | tf_op jit(solution)/shard_map/all_to_all | solution.py:330
  89.5 0.0 copy-done.4
  89.5 0.0 copy-done.5
  89.5 2.1 %shard_map.130 = (bf16[4,128,384]{2,1,0:T(8,128)(2,1)S(1)}, bf16[256,384]{1,0:T(8,128)(2,1)S(1)}, bf16[256,2304]{1,0:T(8,128)(2,1)S(1)}) custom-call(s32[1]{0:T(128)} %bitcast.2.core, bf16[256,1664]{1,0:T(8,128)(2,1)S(1)} %bitcast.44, bf16[4,128,768]{2,1,0:T(8,128)(2,1)S(1)} %all-to-all-done.1.pair, f32[1,384]{1,0:T(1,128)S(1)} %reshape.66.own_gain, ...), custom_call_target="tpu_custom_call" | custom-call | flops 469762048 | bytes 4792324 | tf_op jit(solution)/shard_map/pallas_call | solution.py:313
  91.5 4.7 %collective-permute-start.5 = (bf16[256,2304]{1,0:T(8,128)(2,1)S(1)}, bf16[256,2304]{1,0:T(8,128)(2,1)S(1)}, u32[]{:S(2)}, u32[]{:S(2)}) collective-permute-start(bf16[256,2304]{1,0:T(8,128)(2,1)S(1)} %get-tuple-element.22.bundle), channel_id=1, source_target_pairs={{0,1},{1,0},{2,3},{3,2},{4,5},{5,4},{6,7},{7,6},{8,9},{9,8},{10,11... | collective-permute-start | bytes 3538952 | tf_op jit(solution)/shard_map/ppermute | solution.py:420
  96.2 8.9 %all_to_all.52 = bf16[4,128,384]{2,1,0:T(8,128)(2,1)S(1)} all-to-all(bf16[4,128,384]{2,1,0:T(8,128)(2,1)S(1)} %get-tuple-element.23), channel_id=1, replica_groups={{1,0,17,16},{3,2,19,18},{5,4,21,20},{7,6,23,22},{9,8,25,24},{11,10,27,2..., dimensions={0} | all-to-all | bytes 786432 | tf_op jit(solution)/shard_map/all_to_all | solution.py:330
  105.1 0.7 bitcast_reduce_fusion
  105.8 11.5 %all-to-all-start.5 = ((bf16[16,16,384]{2,1,0:T(8,128)(2,1)}), bf16[16,16,384]{2,1,0:T(8,128)(2,1)S(1)}, u32[]{:S(2)}, u32[]{:S(2)}) async-start(bf16[16,16,384]{2,1,0:T(8,128)(2,1)} %bitcast.55), calls=%async_computation.5 | async-start | bytes 393216 | tf_op jit(solution)/shard_map/all_to_all | solution.py:330
  117.3 0.0 collective-permute-done.5.theirs
  117.3 1.8 %shard_map.131 = (bf16[3,384,128]{2,1,0:T(8,128)(2,1)}, bf16[128,384]{1,0:T(8,128)(2,1)}, bf16[384,512]{1,0:T(8,128)(2,1)}, bf16[512,384]{1,0:T(8,128)(2,1)}) custom-call(s32[1]{0:T(128)} %bitcast.2.core, bf16[256,2304]{1,0:T(8,128)(2,1)S(1)} %get-tuple-element.22.bundle, bf16[256,2304]{1,0:T(8,128)(2,1)S(1)} %collective-permute-done.5.theirs, ...), custom_call_target="tpu_custom_call" | custom-call | flops 603979776 | bytes 4521988 | tf_op jit(solution)/shard_map/pallas_call | solution.py:313
  119.1 7.1 %all-to-all-done.5 = bf16[16,16,384]{2,1,0:T(8,128)(2,1)S(1)} async-done(((bf16[16,16,384]{2,1,0:T(8,128)(2,1)}), bf16[16,16,384]{2,1,0:T(8,128)(2,1)S(1)}, u32[]{:S(2)}, u32[]{:S(2)}) %all-to-all-start.5) | async-done | bytes 196640 | tf_op jit(solution)/shard_map/all_to_all | solution.py:330
  126.2 0.6 reduce_sum.25
  (7 shorter events, 0.0 us)
Async XLA Ops:
  0.6 20.8 %copy-start.6 = (f32[384]{0:T(512)S(1)}, f32[384]{0:T(512)}, u32[]{:S(2)}) copy-start(f32[384]{0:T(512)} %param.11) | copy-start | bytes 4612
  0.6 23.9 %copy-start.3 = (bf16[128,384]{1,0:T(8,128)(2,1)S(1)}, bf16[128,384]{1,0:T(8,128)(2,1)}, u32[]{:S(2)}) copy-start(bf16[128,384]{1,0:T(8,128)(2,1)} %own_out.1) | copy-start | bytes 294916
  0.7 25.9 %copy-start.1 = (bf16[384,3,128]{2,0,1:T(8,128)(2,1)S(1)}, bf16[384,3,128]{2,0,1:T(8,128)(2,1)}, u32[]{:S(2)}) copy-start(bf16[384,3,128]{2,0,1:T(8,128)(2,1)} %param.12) | copy-start | bytes 884740
  0.7 28.3 %copy-start.2 = (bf16[512,384]{1,0:T(8,128)(2,1)S(1)}, bf16[512,384]{1,0:T(8,128)(2,1)}, u32[]{:S(2)}) copy-start(bf16[512,384]{1,0:T(8,128)(2,1)} %own_down.1) | copy-start | bytes 1179652
  0.7 30.2 %copy-start = (bf16[384,512]{1,0:T(8,128)(2,1)S(1)}, bf16[384,512]{1,0:T(8,128)(2,1)}, u32[]{:S(2)}) copy-start(bf16[384,512]{1,0:T(8,128)(2,1)} %own_up.3) | copy-start | bytes 1179652
  2.3 37.1 %all-to-all-start = ((bf16[16,16,768]{2,1,0:T(8,128)(2,1)}), bf16[16,16,768]{2,1,0:T(8,128)(2,1)S(1)}, u32[]{:S(2)}, u32[]{:S(2)}) async-start(bf16[16,16,768]{2,1,0:T(8,128)(2,1)} %broadcast_in_dim.3), calls=%async_computation | async-start | bytes 786432 | tf_op jit(solution)/shard_map/all_to_all | solution.py:330
  21.4 22.9 %collective-permute-start = (f32[1,384]{1,0:T(1,128)S(1)}, f32[1,384]{1,0:T(1,128)S(1)}, u32[]{:S(2)}, u32[]{:S(2)}) collective-permute-start(f32[1,384]{1,0:T(1,128)S(1)} %reshape.66.own_gain), channel_id=1, source_target_pairs={{0,1},{1,0},{2,3},{3,2},{4,5},{5,4},{6,7},{7,6},{8,9},{9,8},{10,11... | collective-permute-start | bytes 4616 | tf_op jit(solution)/shard_map/ppermute | solution.py:363
  24.6 20.5 %collective-permute-start.4 = (bf16[128,384]{1,0:T(8,128)(2,1)S(1)}, bf16[128,384]{1,0:T(8,128)(2,1)S(1)}, u32[]{:S(2)}, u32[]{:S(2)}) collective-permute-start(bf16[128,384]{1,0:T(8,128)(2,1)S(1)} %copy-done.3), channel_id=1, source_target_pairs={{0,1},{1,0},{2,3},{3,2},{4,5},{5,4},{6,7},{7,6},{8,9},{9,8},{10,11... | collective-permute-start | bytes 294920 | tf_op jit(solution)/shard_map/ppermute | solution.py:363
  26.5 17.6 %collective-permute-start.2 = (bf16[3,384,128]{2,1,0:T(8,128)(2,1)S(1)}, bf16[3,384,128]{2,1,0:T(8,128)(2,1)S(1)}, u32[]{:S(2)}, u32[]{:S(2)}) collective-permute-start(bf16[3,384,128]{2,1,0:T(8,128)(2,1)S(1)} %bitcast.45), channel_id=1, source_target_pairs={{0,1},{1,0},{2,3},{3,2},{4,5},{5,4},{6,7},{7,6},{8,9},{9,8},{10,11... | collective-permute-start | bytes 884744 | tf_op jit(solution)/shard_map/ppermute | solution.py:363
  28.9 16.1 %collective-permute-start.3 = (bf16[512,384]{1,0:T(8,128)(2,1)S(1)}, bf16[512,384]{1,0:T(8,128)(2,1)S(1)}, u32[]{:S(2)}, u32[]{:S(2)}) collective-permute-start(bf16[512,384]{1,0:T(8,128)(2,1)S(1)} %copy-done.2), channel_id=1, source_target_pairs={{0,1},{1,0},{2,3},{3,2},{4,5},{5,4},{6,7},{7,6},{8,9},{9,8},{10,11... | collective-permute-start | bytes 1179656 | tf_op jit(solution)/shard_map/ppermute | solution.py:363
  30.9 13.9 %collective-permute-start.1 = (bf16[384,512]{1,0:T(8,128)(2,1)S(1)}, bf16[384,512]{1,0:T(8,128)(2,1)S(1)}, u32[]{:S(2)}, u32[]{:S(2)}) collective-permute-start(bf16[384,512]{1,0:T(8,128)(2,1)S(1)} %copy-done), channel_id=1, source_target_pairs={{0,1},{1,0},{2,3},{3,2},{4,5},{5,4},{6,7},{7,6},{8,9},{9,8},{10,11... | collective-permute-start | bytes 1179656 | tf_op jit(solution)/shard_map/ppermute | solution.py:363
  40.4 13.8 %all-to-all-start.1 = ((bf16[4,128,768]{2,1,0:T(8,128)(2,1)}), bf16[4,128,768]{2,1,0:T(8,128)(2,1)S(1)}, u32[]{:S(2)}, u32[]{:S(2)}) async-start(bf16[4,128,768]{2,1,0:T(8,128)(2,1)} %bitcast.51), calls=%async_computation.1 | async-start | bytes 1572864 | tf_op jit(solution)/shard_map/all_to_all | solution.py:330
  74.0 15.4 %copy-start.4 = (f32[128]{0:T(128)S(1)}, f32[128]{0:T(128)}, u32[]{:S(2)}) copy-start(f32[128]{0:T(128)} %param.16) | copy-start | bytes 1540
  74.0 15.4 %copy-start.5 = (f32[128]{0:T(128)S(1)}, f32[128]{0:T(128)}, u32[]{:S(2)}) copy-start(f32[128]{0:T(128)} %param.17) | copy-start | bytes 1540
  91.5 25.8 %collective-permute-start.5 = (bf16[256,2304]{1,0:T(8,128)(2,1)S(1)}, bf16[256,2304]{1,0:T(8,128)(2,1)S(1)}, u32[]{:S(2)}, u32[]{:S(2)}) collective-permute-start(bf16[256,2304]{1,0:T(8,128)(2,1)S(1)} %get-tuple-element.22.bundle), channel_id=1, source_target_pairs={{0,1},{1,0},{2,3},{3,2},{4,5},{5,4},{6,7},{7,6},{8,9},{9,8},{10,11... | collective-permute-start | bytes 3538952 | tf_op jit(solution)/shard_map/ppermute | solution.py:420
  105.8 20.3 %all-to-all-start.5 = ((bf16[16,16,384]{2,1,0:T(8,128)(2,1)}), bf16[16,16,384]{2,1,0:T(8,128)(2,1)S(1)}, u32[]{:S(2)}, u32[]{:S(2)}) async-start(bf16[16,16,384]{2,1,0:T(8,128)(2,1)} %bitcast.55), calls=%async_computation.5 | async-start | bytes 393216 | tf_op jit(solution)/shard_map/all_to_all | solution.py:330

commit v6 on v5

--- a/solution.py
+++ b/solution.py
@@ -14,8 +14,8 @@
 EPSILON = 1e-06
 Z_COUNT = 16
 CHIPS = 8
-ALONG_Z = [8, 9, 10, 11, 12, 13, 14, 15, 0, 1, 2, 3, 4, 5, 6, 7]
-WITHIN = [1, 0, 3, 2]
+PAIRS = [4, 5, 6, 7, 0, 1, 2, 3]
+NEAR = [1, 0, 3, 2, 5, 4, 7, 6]
 ACROSS = [6, 7, 4, 5, 2, 3, 0, 1]
 VMEM_BYTES = 24 * 1024 * 1024
 F32 = jnp.float32
@@ -83,13 +83,13 @@
     other_rows,
 ):
     own_index, other_index = 1 - core[0], core[0]
-    half, width = pair.shape[1], own_gain.shape[1]
+    part, width = pair.shape[1], own_gain.shape[1]
     hidden_size, heads3 = own_up.shape[1], 3 * HEAD_DIM
     edge = 2 * hidden_size + heads3 + own_out.shape[0]
-    for y in range(2):
-        at = slice(y * half, (y + 1) * half)
-        own = pair[2 * y + own_index]
-        other = pair[2 * y + other_index]
+    for i in range(4):
+        at = slice(i * part, (i + 1) * part)
+        own = pair[2 * i + own_index]
+        other = pair[2 * i + other_index]
         own_rows[at, width:] = own[:, width:]
         other_rows[at, width:] = other[:, width:]
         own, other = own[:, :width].astype(F32), other[:, :width].astype(F32)
@@ -102,7 +102,7 @@
         )
         own_rows[at, :width] = (own * own_gain[...]).astype(BF16)
         other_rows[at, :width] = (other * other_gain[...]).astype(BF16)
-        sent[at, edge : edge + 128] = lanes(split(part_mean, 3) + split(part_square, 3), half)
+        sent[at, edge : edge + 128] = lanes(split(part_mean, 3) + split(part_square, 3), part)
     for i in range(sent.shape[0] // sum_rows.shape[0]):
         sent[i * sum_rows.shape[0] : (i + 1) * sum_rows.shape[0], edge + 128 :] = sum_rows[...]
     start = 0
@@ -113,9 +113,10 @@
         (own_out, other_out, width, 1),
     ):
         size = own_weight.shape[1 - dim]
+        last = own_weight.shape[0]
         sent[:, start : start + size] = (
             dot(own_rows[:, first : first + width], own_weight[...], 1, dim)
-            + dot(other_rows[:, first : first + width], other_weight[...], 1, dim)
+            + dot(other_rows[:, first : first + width], other_weight[:last], 1, dim)
         ).astype(BF16)
         start += size
 
@@ -220,15 +221,15 @@
     own_normed,
     bundle,
 ):
-    half, width = pair.shape[1], own_gain.shape[1]
+    part, width = pair.shape[1], own_gain.shape[1]
     hidden_size = own_up.shape[1]
     start = 2 * hidden_size
     edge = start + 4 * HEAD_DIM
     other_normed = bundle.at[:, edge : edge + width]
     attention = bundle.at[:, start:edge]
     bundle[:, :start] = shared[:, :start]
-    for y in range(2):
-        bundle[y * half : (y + 1) * half, edge + width :] = pair[2 * y + core[0], :, width:]
+    for i in range(4):
+        bundle[i * part : (i + 1) * part, edge + width :] = pair[2 * i + core[0], :, width:]
     score_scale = 1.0 / math.sqrt(HEAD_DIM)
 
     stats = shared[:, edge:].astype(F32)
@@ -275,11 +276,11 @@
                 for i in range(3)
             )
         )
-        for y in range(2):
-            at = slice(y * half, (y + 1) * half)
-            unit_rows = (pair[2 * y + index, :, :width].astype(F32) - mean[at]) * inverse[at]
+        for i in range(4):
+            at = slice(i * part, (i + 1) * part)
+            unit_rows = (pair[2 * i + index, :, :width].astype(F32) - mean[at]) * inverse[at]
             normed[at, :] = (unit_rows * gain[...]).astype(BF16)
-            parts[2 * y + index] = (
+            parts[2 * i + index] = (
                 inverse[at] * (unit_grad[at] - grad_sum[at] - unit_rows * grad_project[at])
             ).astype(BF16)
 
@@ -290,7 +291,7 @@
     width = normed.shape[1]
     start = 2 * hidden_size
     edge = start + 4 * HEAD_DIM
-    mine = (normed[...], jnp.concatenate([pair[2 * y + 1 - core[0], :, width:] for y in range(2)]))
+    mine = (normed[...], jnp.concatenate([pair[2 * i + 1 - core[0], :, width:] for i in range(4)]))
     other = (theirs[:, edge : edge + width], theirs[:, edge + width :])
 
     def both(side, first, last):
@@ -306,6 +307,10 @@
     qkv = both(0, start + HEAD_DIM, edge)
     for i in range(3):
         qkv_out[i] = qkv[:, i * HEAD_DIM : (i + 1) * HEAD_DIM]
+
+
+def add_kernel(parts, out):
+    out[...] = sum(parts[i].astype(F32) for i in range(parts.shape[0])).astype(BF16)
 
 
 def call(kernel, outs, args, scratch=(), flops=0, scalars=0):
@@ -345,7 +350,6 @@
     total = float(width * CHIPS * 2)
     image = block * Z_COUNT
     own = image // CHIPS
-    half = image // 2
     hidden_size = up_weight.shape[1]
     head_size = out_weight.shape[0]
     heads3 = 3 * head_size
@@ -354,13 +358,19 @@
     swap = [(0, 1), (1, 0)]
 
     spread = jnp.broadcast_to(
-        jnp.concatenate([inputs, cotangent], axis=1), (Z_COUNT, block, 2 * width)
+        jnp.concatenate([inputs, cotangent], axis=1), (len(PAIRS), block, 2 * width)
     ).reshape(-1, 2 * width)
-    both = to_each(spread, "z", ALONG_Z)
+    both = to_each(spread, "z_pair", PAIRS)
 
     by_kind = jnp.transpose(qkv_weight, (1, 0, 2))
     own_weights = (norm_gain.reshape(1, width), up_weight, by_kind, down_weight, out_weight)
-    other_weights = tuple(lax.ppermute(w, "core", swap) for w in own_weights)
+    gain_rows = jnp.stack(pieces(norm_gain, 3) + [jnp.zeros((width,), BF16)] * 13)
+    rows = jnp.concatenate([out_weight, gain_rows])
+    other_up, other_kinds, other_down, rows = (
+        lax.ppermute(w, "core", swap) for w in (up_weight, by_kind, down_weight, rows)
+    )
+    other_gain = jnp.sum(rows[head_size:].astype(F32), axis=0, keepdims=True)
+    other_weights = (other_gain, other_up, other_kinds, other_down, rows)
 
     def column_sums(weights):
         gain, up, qkv = weights[:3]
@@ -375,8 +385,8 @@
     sum_rows = jnp.concatenate([p.reshape(-1, 128) for p in pieces(sums, 3)])
     sum_rows = jnp.pad(sum_rows, ((0, own - sum_rows.shape[0]), (0, 0)))
 
-    pair = to_each(jnp.concatenate([both, both]), ("y_lo", "core"), WITHIN)
-    pair = pair.reshape(4, half, 2 * width)
+    pair = to_each(jnp.concatenate([both] * 4), ("z_lo", "y_lo", "core"), NEAR)
+    pair = pair.reshape(8, image // 4, 2 * width)
     weight_pairs = [w for two in zip(own_weights, other_weights) for w in two]
     (sent,) = call(
         forward_kernel,
@@ -396,7 +406,7 @@
     parts, own_normed, bundle = call(
         functools.partial(backward_kernel, total),
         [
-            shape((4, half, width)),
+            shape((8, image // 4, width)),
             shape((image, width)),
             shape((image, edge + 2 * width)),
         ],
@@ -412,10 +422,11 @@
         flops=4 * image * width * (hidden_size + heads3) + 14 * image * image * head_size,
         scalars=1,
     )
-    parts = to_each(parts.reshape(4 * half, width), ("y_lo", "core"), WITHIN)
-    parts = parts.reshape(2, image, width)
-    parts = jnp.sum(parts.astype(F32), axis=0).astype(BF16)
-    last = to_each(parts, "z", ALONG_Z).reshape(Z_COUNT, -1, width)
+    parts = to_each(parts.reshape(2 * image, width), ("z_lo", "y_lo", "core"), NEAR)
+    (parts,) = call(
+        add_kernel, [shape((image // 2, width))], (parts.reshape(4, image // 2, width),)
+    )
+    last = to_each(parts, "z_pair", PAIRS).reshape(len(PAIRS), -1, width)
 
     theirs = lax.ppermute(bundle, "core", swap)
     theirs, _ = lax.optimization_barrier((theirs, parts))
@@ -438,8 +449,9 @@
 
 
 def solution(mesh):
-    mesh = Mesh(mesh.devices.reshape(Z_COUNT, 2, 2, 4, 2), ("z", "y_lo", "y_hi", "x", "core"))
-    hid, wid = ("z", "y_lo"), ("y_hi", "x", "core")
+    names = ("z_pair", "z_lo", "y_lo", "y_hi", "x", "core")
+    mesh = Mesh(mesh.devices.reshape(Z_COUNT // 2, 2, 2, 2, 4, 2), names)
+    hid, wid = names[:3], names[3:]
     return jax.shard_map(
         local,
         mesh=mesh,

time: 128 us -> 116 us (0.906)
  blocking collectives: 42.4 us -> 63.8 us
  starting transfers between devices: 50.5 us -> 31 us
  waiting for transfers between devices: 22 us -> 7.39 us
  Pallas kernels: 5.57 us -> 7.52 us
    all_to_all x3, blocking collectives: 42.4 us -> 63.8 us  [to_each(): lax.all_to_all(rows, axis, 0, 0, tiled=True, axis_index_groups=[order])]
    all_to_all x3, waiting for transfers between devices: 22 us -> 6.92 us  [to_each(): lax.all_to_all(rows, axis, 0, 0, tiled=True, axis_index_groups=[order])]
    all_to_all x3, starting transfers between devices: 34.1 us -> 19.7 us  [to_each(): lax.all_to_all(rows, axis, 0, 0, tiled=True, axis_index_groups=[order])]
    ppermute x5 -> x4, starting transfers between devices: 11.8 us -> 8.64 us  [local(): lax.ppermute(w, 'core', swap)]
    ppermute x1, starting transfers between devices: 4.65 us -> 2.66 us  [local(): theirs = lax.ppermute(bundle, 'core', swap)]
    pallas_call x4 -> x5, Pallas kernels: 5.57 us -> 7.52 us  [call(): pl.pallas_call(kernel, out_shape=outs, in_specs=[pl.BlockSpec(memory_spac...]
  transfers between devices with their start and end apart: 9 -> 8, of which waited for: 3 -> 4; matrix products, arithmetic and copies ran while one was open for 2% -> 1% of each run, Pallas kernels for 1% -> 3%
where the time goes in v6:
time: 116 us; the launch traced here: 115 us
  blocking collectives  63.8 us (55%)
  starting transfers between devices  31 us (27%)
  Pallas kernels  7.52 us (6%)
  waiting for transfers between devices  7.39 us (6%)
  other arithmetic  2.36 us (2%)
  matrix products  1.17 us (1%)
    all_to_all x3, blocking collectives, to_each(): lax.all_to_all(rows, axis, 0, 0, tiled=True, axis_index_groups=[order])  63.8 us
    all_to_all x3, starting transfers between devices, to_each(): lax.all_to_all(rows, axis, 0, 0, tiled=True, axis_index_groups=[order])  19.7 us
    ppermute x4, starting transfers between devices, local(): lax.ppermute(w, 'core', swap)  8.64 us
    pallas_call x5, Pallas kernels, call(): pl.pallas_call(kernel, out_shape=outs, in_specs=[pl.BlockSpec(memory_spac...  7.52 us
    all_to_all x3, waiting for transfers between devices, to_each(): lax.all_to_all(rows, axis, 0, 0, tiled=True, axis_index_groups=[order])  6.92 us
    ppermute x1, starting transfers between devices, local(): theirs = lax.ppermute(bundle, 'core', swap)  2.66 us
  transfers between devices with their start and end apart: 8, of which 4 were waited for; matrix products, arithmetic and copies ran while one was open for 1% of the time, Pallas kernels for 3%

profile of v6, /device:TPU:1, one launch (start us, length us, event | category | flops | bytes accessed | tf_op | source)
XLA Modules:
  0.0 115.2 jit_solution(5911016830019588021)
XLA Ops:
  0.6 0.7 pad_maximum_fusion.1
  1.4 28.1 %all_to_all.50 = bf16[8,16,768]{2,1,0:T(8,128)(2,1)S(1)} all-to-all(bf16[8,16,768]{2,1,0:T(8,128)(2,1)S(1)} %broadcast_in_dim.6), channel_id=1, replica_groups={{256,320,384,448,0,64,128,192},{257,321,385,449,1,65,129,193},{258,322,..., dimensions={0} | all-to-all | bytes 393216 | tf_op jit(solution)/shard_map/all_to_all | solution.py:335
  29.5 0.0 copy-start.7
  29.5 0.0 copy-start.4
  29.5 0.0 copy-start.1
  29.5 0.0 copy-start.3
  29.5 0.0 copy-start
  29.5 1.0 pad_maximum_fusion
  30.5 3.8 %all-to-all-start.1 = ((bf16[8,64,768]{2,1,0:T(8,128)(2,1)}), bf16[8,64,768]{2,1,0:T(8,128)(2,1)S(1)}, u32[]{:S(2)}, u32[]{:S(2)}) async-start(bf16[8,64,768]{2,1,0:T(8,128)(2,1)} %bitcast.47), calls=%async_computation.1 | async-start | bytes 1572864 | tf_op jit(solution)/shard_map/all_to_all | solution.py:335
  34.3 0.0 copy-done.7
  34.4 0.0 copy-done.4
  34.4 0.1 concatenate.28
  34.5 2.4 %collective-permute-start = (bf16[144,384]{1,0:T(8,128)(2,1)S(1)}, bf16[144,384]{1,0:T(8,128)(2,1)S(1)}, u32[]{:S(2)}, u32[]{:S(2)}) collective-permute-start(bf16[144,384]{1,0:T(8,128)(2,1)S(1)} %concatenate.28), channel_id=1, source_target_pairs={{0,1},{1,0},{2,3},{3,2},{4,5},{5,4},{6,7},{7,6},{8,9},{9,8},{10,11... | collective-permute-start | bytes 331784 | tf_op jit(solution)/shard_map/ppermute | solution.py:370
  36.9 0.0 copy-done.1
  36.9 1.9 %collective-permute-start.2 = (bf16[3,384,128]{2,1,0:T(8,128)(2,1)S(1)}, bf16[3,384,128]{2,1,0:T(8,128)(2,1)S(1)}, u32[]{:S(2)}, u32[]{:S(2)}) collective-permute-start(bf16[3,384,128]{2,1,0:T(8,128)(2,1)S(1)} %bitcast.40), channel_id=1, source_target_pairs={{0,1},{1,0},{2,3},{3,2},{4,5},{5,4},{6,7},{7,6},{8,9},{9,8},{10,11... | collective-permute-start | bytes 884744 | tf_op jit(solution)/shard_map/ppermute | solution.py:370
  38.8 0.0 copy-done.3
  38.8 2.4 %collective-permute-start.3 = (bf16[512,384]{1,0:T(8,128)(2,1)S(1)}, bf16[512,384]{1,0:T(8,128)(2,1)S(1)}, u32[]{:S(2)}, u32[]{:S(2)}) collective-permute-start(bf16[512,384]{1,0:T(8,128)(2,1)S(1)} %copy-done.3), channel_id=1, source_target_pairs={{0,1},{1,0},{2,3},{3,2},{4,5},{5,4},{6,7},{7,6},{8,9},{9,8},{10,11... | collective-permute-start | bytes 1179656 | tf_op jit(solution)/shard_map/ppermute | solution.py:370
  41.2 0.0 copy-done
  41.2 1.9 %collective-permute-start.1 = (bf16[384,512]{1,0:T(8,128)(2,1)S(1)}, bf16[384,512]{1,0:T(8,128)(2,1)S(1)}, u32[]{:S(2)}, u32[]{:S(2)}) collective-permute-start(bf16[384,512]{1,0:T(8,128)(2,1)S(1)} %copy-done), channel_id=1, source_target_pairs={{0,1},{1,0},{2,3},{3,2},{4,5},{5,4},{6,7},{7,6},{8,9},{9,8},{10,11... | collective-permute-start | bytes 1179656 | tf_op jit(solution)/shard_map/ppermute | solution.py:370
  43.2 0.3 fusion.12
  43.4 0.3 fusion.10
  43.7 0.0 collective-permute-done.other_out
  43.8 0.0 collective-permute-done.2.other_qkv
  43.8 0.2 copy.14
  44.0 0.4 convolution_reduce_fusion
  44.4 0.5 collective-permute-done.1.other_up
  44.8 0.3 fusion.13
  45.1 0.0 collective-permute-done.3.other_down
  45.2 0.5 all-to-all-done.1.pair
  45.6 1.3 %shard_map.128 = bf16[256,1792]{1,0:T(8,128)(2,1)S(1)} custom-call(s32[1]{0:T(128)} %bitcast.2.core, bf16[8,64,768]{2,1,0:T(8,128)(2,1)S(1)} %all-to-all-done.1.pair, f32[1,384]{1,0:T(1,128)S(1)} %reshape.66.own_gain, f32[1,384]{1,0:T(1,128)S(1)} %broadcast_in_dim.7.other_gain, bf16[384,512]{1,0:T(8,128)(2,1)S(1)} %copy-done, ...), custom_call_target="tpu_custom_call" | custom-call | flops 603979776 | bytes 4086788 | tf_op jit(solution)/shard_map/pallas_call | solution.py:318
  46.9 18.9 %all_to_all.51.got = bf16[8,32,1792]{2,1,0:T(8,128)(2,1)S(1)} all-to-all(bf16[8,32,1792]{2,1,0:T(8,128)(2,1)S(1)} %bitcast.38), channel_id=1, replica_groups={{12,14,8,10,4,6,0,2},{13,15,9,11,5,7,1,3},{28,30,24,26,20,22,16,18},{29..., dimensions={0} | all-to-all | bytes 1835008 | tf_op jit(solution)/shard_map/all_to_all | solution.py:335
  65.8 0.0 copy-start.6
  65.8 0.5 shard_map.129
  66.3 16.7 %all_to_all.52 = bf16[8,32,1664]{2,1,0:T(8,128)(2,1)S(1)} all-to-all(bf16[8,32,1664]{2,1,0:T(8,128)(2,1)S(1)} %get-tuple-element.20), channel_id=1, replica_groups={{12,14,8,10,4,6,0,2},{13,15,9,11,5,7,1,3},{28,30,24,26,20,22,16,18},{29..., dimensions={0} | all-to-all | bytes 1703936 | tf_op jit(solution)/shard_map/all_to_all | solution.py:335
  83.0 0.0 copy-done.5
  83.0 0.0 copy-done.6
  83.0 2.1 %shard_map.130 = (bf16[8,64,384]{2,1,0:T(8,128)(2,1)S(1)}, bf16[256,384]{1,0:T(8,128)(2,1)S(1)}, bf16[256,2304]{1,0:T(8,128)(2,1)S(1)}) custom-call(s32[1]{0:T(128)} %bitcast.2.core, bf16[256,1664]{1,0:T(8,128)(2,1)S(1)} %bitcast.39, bf16[8,64,768]{2,1,0:T(8,128)(2,1)S(1)} %all-to-all-done.1.pair, f32[1,384]{1,0:T(1,128)S(1)} %reshape.66.own_gain, ...), custom_call_target="tpu_custom_call" | custom-call | flops 469762048 | bytes 4792324 | tf_op jit(solution)/shard_map/pallas_call | solution.py:318
  85.1 0.0 copy-start.2
  85.1 0.7 copy-done.2
  85.8 4.0 %all-to-all-start.4 = ((bf16[8,64,384]{2,1,0:T(8,128)(2,1)}), bf16[8,64,384]{2,1,0:T(8,128)(2,1)S(1)}, u32[]{:S(2)}, u32[]{:S(2)}) async-start(bf16[8,64,384]{2,1,0:T(8,128)(2,1)} %copy-done.2), calls=%async_computation.4 | async-start | bytes 786432 | tf_op jit(solution)/shard_map/all_to_all | solution.py:335
  89.8 2.7 %collective-permute-start.4 = (bf16[256,2304]{1,0:T(8,128)(2,1)S(1)}, bf16[256,2304]{1,0:T(8,128)(2,1)}, u32[]{:S(2)}, u32[]{:S(2)}) collective-permute-start(bf16[256,2304]{1,0:T(8,128)(2,1)S(1)} %get-tuple-element.22.bundle), channel_id=1, source_target_pairs={{0,1},{1,0},{2,3},{3,2},{4,5},{5,4},{6,7},{7,6},{8,9},{9,8},{10,11... | collective-permute-start | bytes 3538952 | tf_op jit(solution)/shard_map/ppermute | solution.py:431
  92.5 4.5 %all-to-all-done.4 = bf16[8,64,384]{2,1,0:T(8,128)(2,1)S(1)} async-done(((bf16[8,64,384]{2,1,0:T(8,128)(2,1)}), bf16[8,64,384]{2,1,0:T(8,128)(2,1)S(1)}, u32[]{:S(2)}, u32[]{:S(2)}) %all-to-all-start.4) | async-done | bytes 393248 | tf_op jit(solution)/shard_map/all_to_all | solution.py:335
  97.0 0.7 shard_map.131
  97.7 11.9 %all-to-all-start.5 = ((bf16[8,16,384]{2,1,0:T(8,128)(2,1)}), bf16[8,16,384]{2,1,0:T(8,128)(2,1)S(1)}, u32[]{:S(2)}, u32[]{:S(2)}) async-start(bf16[8,16,384]{2,1,0:T(8,128)(2,1)} %bitcast.17), calls=%async_computation.5 | async-start | bytes 196608 | tf_op jit(solution)/shard_map/all_to_all | solution.py:335
  109.6 0.0 collective-permute-done.4.theirs
  109.6 3.0 %shard_map.132 = (bf16[3,384,128]{2,1,0:T(8,128)(2,1)}, bf16[128,384]{1,0:T(8,128)(2,1)}, bf16[384,512]{1,0:T(8,128)(2,1)}, bf16[512,384]{1,0:T(8,128)(2,1)}) custom-call(s32[1]{0:T(128)} %bitcast.2.core, bf16[256,2304]{1,0:T(8,128)(2,1)S(1)} %get-tuple-element.22.bundle, bf16[256,2304]{1,0:T(8,128)(2,1)} %collective-permute-done.4.theirs, ...), custom_call_target="tpu_custom_call" | custom-call | flops 603979776 | bytes 4521988 | tf_op jit(solution)/shard_map/pallas_call | solution.py:318
  112.6 1.9 %all-to-all-done.5 = bf16[8,16,384]{2,1,0:T(8,128)(2,1)S(1)} async-done(((bf16[8,16,384]{2,1,0:T(8,128)(2,1)}), bf16[8,16,384]{2,1,0:T(8,128)(2,1)S(1)}, u32[]{:S(2)}, u32[]{:S(2)}) %all-to-all-start.5) | async-done | bytes 98336 | tf_op jit(solution)/shard_map/all_to_all | solution.py:335
  114.6 0.6 reduce_sum.22
  (18 shorter events, 0.1 us)
Async XLA Ops:
  29.5 4.8 %copy-start.7 = (f32[384]{0:T(512)S(1)}, f32[384]{0:T(512)}, u32[]{:S(2)}) copy-start(f32[384]{0:T(512)} %param.11) | copy-start | bytes 4612
  29.5 4.8 %copy-start.4 = (bf16[128,384]{1,0:T(8,128)(2,1)S(1)}, bf16[128,384]{1,0:T(8,128)(2,1)}, u32[]{:S(2)}) copy-start(bf16[128,384]{1,0:T(8,128)(2,1)} %own_out.1) | copy-start | bytes 294916
  29.5 7.3 %copy-start.1 = (bf16[384,3,128]{2,0,1:T(8,128)(2,1)S(1)}, bf16[384,3,128]{2,0,1:T(8,128)(2,1)}, u32[]{:S(2)}) copy-start(bf16[384,3,128]{2,0,1:T(8,128)(2,1)} %param.12) | copy-start | bytes 884740
  29.5 9.3 %copy-start.3 = (bf16[512,384]{1,0:T(8,128)(2,1)S(1)}, bf16[512,384]{1,0:T(8,128)(2,1)}, u32[]{:S(2)}) copy-start(bf16[512,384]{1,0:T(8,128)(2,1)} %own_down.1) | copy-start | bytes 1179652
  29.5 11.7 %copy-start = (bf16[384,512]{1,0:T(8,128)(2,1)S(1)}, bf16[384,512]{1,0:T(8,128)(2,1)}, u32[]{:S(2)}) copy-start(bf16[384,512]{1,0:T(8,128)(2,1)} %own_up.3) | copy-start | bytes 1179652
  30.5 15.1 %all-to-all-start.1 = ((bf16[8,64,768]{2,1,0:T(8,128)(2,1)}), bf16[8,64,768]{2,1,0:T(8,128)(2,1)S(1)}, u32[]{:S(2)}, u32[]{:S(2)}) async-start(bf16[8,64,768]{2,1,0:T(8,128)(2,1)} %bitcast.47), calls=%async_computation.1 | async-start | bytes 1572864 | tf_op jit(solution)/shard_map/all_to_all | solution.py:335
  34.5 9.2 %collective-permute-start = (bf16[144,384]{1,0:T(8,128)(2,1)S(1)}, bf16[144,384]{1,0:T(8,128)(2,1)S(1)}, u32[]{:S(2)}, u32[]{:S(2)}) collective-permute-start(bf16[144,384]{1,0:T(8,128)(2,1)S(1)} %concatenate.28), channel_id=1, source_target_pairs={{0,1},{1,0},{2,3},{3,2},{4,5},{5,4},{6,7},{7,6},{8,9},{9,8},{10,11... | collective-permute-start | bytes 331784 | tf_op jit(solution)/shard_map/ppermute | solution.py:370
  36.9 6.9 %collective-permute-start.2 = (bf16[3,384,128]{2,1,0:T(8,128)(2,1)S(1)}, bf16[3,384,128]{2,1,0:T(8,128)(2,1)S(1)}, u32[]{:S(2)}, u32[]{:S(2)}) collective-permute-start(bf16[3,384,128]{2,1,0:T(8,128)(2,1)S(1)} %bitcast.40), channel_id=1, source_target_pairs={{0,1},{1,0},{2,3},{3,2},{4,5},{5,4},{6,7},{7,6},{8,9},{9,8},{10,11... | collective-permute-start | bytes 884744 | tf_op jit(solution)/shard_map/ppermute | solution.py:370
  38.8 6.3 %collective-permute-start.3 = (bf16[512,384]{1,0:T(8,128)(2,1)S(1)}, bf16[512,384]{1,0:T(8,128)(2,1)S(1)}, u32[]{:S(2)}, u32[]{:S(2)}) collective-permute-start(bf16[512,384]{1,0:T(8,128)(2,1)S(1)} %copy-done.3), channel_id=1, source_target_pairs={{0,1},{1,0},{2,3},{3,2},{4,5},{5,4},{6,7},{7,6},{8,9},{9,8},{10,11... | collective-permute-start | bytes 1179656 | tf_op jit(solution)/shard_map/ppermute | solution.py:370
  41.2 3.6 %collective-permute-start.1 = (bf16[384,512]{1,0:T(8,128)(2,1)S(1)}, bf16[384,512]{1,0:T(8,128)(2,1)S(1)}, u32[]{:S(2)}, u32[]{:S(2)}) collective-permute-start(bf16[384,512]{1,0:T(8,128)(2,1)S(1)} %copy-done), channel_id=1, source_target_pairs={{0,1},{1,0},{2,3},{3,2},{4,5},{5,4},{6,7},{7,6},{8,9},{9,8},{10,11... | collective-permute-start | bytes 1179656 | tf_op jit(solution)/shard_map/ppermute | solution.py:370
  65.8 17.2 %copy-start.5 = (f32[128]{0:T(128)S(1)}, f32[128]{0:T(128)}, u32[]{:S(2)}) copy-start(f32[128]{0:T(128)} %param.16) | copy-start | bytes 1540
  65.8 17.2 %copy-start.6 = (f32[128]{0:T(128)S(1)}, f32[128]{0:T(128)}, u32[]{:S(2)}) copy-start(f32[128]{0:T(128)} %param.17) | copy-start | bytes 1540
  85.1 0.7 copy-start.2
  85.8 11.2 %all-to-all-start.4 = ((bf16[8,64,384]{2,1,0:T(8,128)(2,1)}), bf16[8,64,384]{2,1,0:T(8,128)(2,1)S(1)}, u32[]{:S(2)}, u32[]{:S(2)}) async-start(bf16[8,64,384]{2,1,0:T(8,128)(2,1)} %copy-done.2), calls=%async_computation.4 | async-start | bytes 786432 | tf_op jit(solution)/shard_map/all_to_all | solution.py:335
  89.8 19.8 %collective-permute-start.4 = (bf16[256,2304]{1,0:T(8,128)(2,1)S(1)}, bf16[256,2304]{1,0:T(8,128)(2,1)}, u32[]{:S(2)}, u32[]{:S(2)}) collective-permute-start(bf16[256,2304]{1,0:T(8,128)(2,1)S(1)} %get-tuple-element.22.bundle), channel_id=1, source_target_pairs={{0,1},{1,0},{2,3},{3,2},{4,5},{5,4},{6,7},{7,6},{8,9},{9,8},{10,11... | collective-permute-start | bytes 3538952 | tf_op jit(solution)/shard_map/ppermute | solution.py:431
  97.7 16.9 %all-to-all-start.5 = ((bf16[8,16,384]{2,1,0:T(8,128)(2,1)}), bf16[8,16,384]{2,1,0:T(8,128)(2,1)S(1)}, u32[]{:S(2)}, u32[]{:S(2)}) async-start(bf16[8,16,384]{2,1,0:T(8,128)(2,1)} %bitcast.17), calls=%async_computation.5 | async-start | bytes 196608 | tf_op jit(solution)/shard_map/all_to_all | solution.py:335

commit v7 on v6

--- a/solution.py
+++ b/solution.py
@@ -14,7 +14,8 @@
 EPSILON = 1e-06
 Z_COUNT = 16
 CHIPS = 8
-PAIRS = [4, 5, 6, 7, 0, 1, 2, 3]
+PAIRS = [5, 6, 7, 4, 0, 1, 2, 3]
+LAST = [5, 6, 7, 4, 0, 1, 2, 3]
 NEAR = [1, 0, 3, 2, 5, 4, 7, 6]
 ACROSS = [6, 7, 4, 5, 2, 3, 0, 1]
 VMEM_BYTES = 24 * 1024 * 1024
@@ -310,7 +311,11 @@
 
 
 def add_kernel(parts, out):
-    out[...] = sum(parts[i].astype(F32) for i in range(parts.shape[0])).astype(BF16)
+    rows = out.shape[0] // len(LAST)
+    for i, place in enumerate(PAIRS):
+        to = LAST.index(place) * rows
+        added = sum(parts[j, i * rows : (i + 1) * rows].astype(F32) for j in range(parts.shape[0]))
+        out[to : to + rows] = added.astype(BF16)
 
 
 def call(kernel, outs, args, scratch=(), flops=0, scalars=0):
@@ -426,7 +431,7 @@
     (parts,) = call(
         add_kernel, [shape((image // 2, width))], (parts.reshape(4, image // 2, width),)
     )
-    last = to_each(parts, "z_pair", PAIRS).reshape(len(PAIRS), -1, width)
+    last = to_each(parts, "z_pair", LAST).reshape(len(PAIRS), -1, width)
 
     theirs = lax.ppermute(bundle, "core", swap)
     theirs, _ = lax.optimization_barrier((theirs, parts))

time: 116 us -> 115 us (level)
  starting transfers between devices: 31 us -> 28.8 us
    all_to_all x3, starting transfers between devices: 19.7 us -> 17.2 us  [to_each(): lax.all_to_all(rows, axis, 0, 0, tiled=True, axis_index_groups=[order])]
where the time goes in v7:
time: 115 us; the launch traced here: 114 us
  blocking collectives  64.1 us (56%)
  starting transfers between devices  28.8 us (25%)
  waiting for transfers between devices  8.08 us (7%)
  Pallas kernels  7.51 us (7%)
  other arithmetic  2.36 us (2%)
  matrix products  1.17 us (1%)
    all_to_all x3, blocking collectives, to_each(): lax.all_to_all(rows, axis, 0, 0, tiled=True, axis_index_groups=[order])  64.1 us
    all_to_all x3, starting transfers between devices, to_each(): lax.all_to_all(rows, axis, 0, 0, tiled=True, axis_index_groups=[order])  17.2 us
    ppermute x4, starting transfers between devices, local(): lax.ppermute(w, 'core', swap)  8.7 us
    all_to_all x3, waiting for transfers between devices, to_each(): lax.all_to_all(rows, axis, 0, 0, tiled=True, axis_index_groups=[order])  7.61 us
    pallas_call x5, Pallas kernels, call(): pl.pallas_call(kernel, out_shape=outs, in_specs=[pl.BlockSpec(memory_spac...  7.51 us
    ppermute x1, starting transfers between devices, local(): theirs = lax.ppermute(bundle, 'core', swap)  2.89 us
  transfers between devices with their start and end apart: 8, of which 4 were waited for; matrix products, arithmetic and copies ran while one was open for 1% of the time, Pallas kernels for 3%

profile of v7, /device:TPU:1, one launch (start us, length us, event | category | flops | bytes accessed | tf_op | source)
XLA Modules:
  0.0 114.0 jit_solution(3519196929667010092)
XLA Ops:
  0.6 0.7 pad_maximum_fusion.1
  1.4 28.1 %all_to_all.50 = bf16[8,16,768]{2,1,0:T(8,128)(2,1)S(1)} all-to-all(bf16[8,16,768]{2,1,0:T(8,128)(2,1)S(1)} %broadcast_in_dim.6), channel_id=1, replica_groups={{320,384,448,256,0,64,128,192},{321,385,449,257,1,65,129,193},{322,386,..., dimensions={0} | all-to-all | bytes 393216 | tf_op jit(solution)/shard_map/all_to_all | solution.py:340
  29.5 0.0 copy-start.7
  29.5 0.0 copy-start.4
  29.5 0.0 copy-start.1
  29.5 0.0 copy-start.3
  29.5 0.0 copy-start
  29.5 1.0 pad_maximum_fusion
  30.5 3.5 %all-to-all-start.1 = ((bf16[8,64,768]{2,1,0:T(8,128)(2,1)}), bf16[8,64,768]{2,1,0:T(8,128)(2,1)S(1)}, u32[]{:S(2)}, u32[]{:S(2)}) async-start(bf16[8,64,768]{2,1,0:T(8,128)(2,1)} %bitcast.47), calls=%async_computation.1 | async-start | bytes 1572864 | tf_op jit(solution)/shard_map/all_to_all | solution.py:340
  34.1 0.0 copy-done.7
  34.1 0.0 copy-done.4
  34.2 0.1 concatenate.28
  34.2 2.5 %collective-permute-start = (bf16[144,384]{1,0:T(8,128)(2,1)S(1)}, bf16[144,384]{1,0:T(8,128)(2,1)S(1)}, u32[]{:S(2)}, u32[]{:S(2)}) collective-permute-start(bf16[144,384]{1,0:T(8,128)(2,1)S(1)} %concatenate.28), channel_id=1, source_target_pairs={{0,1},{1,0},{2,3},{3,2},{4,5},{5,4},{6,7},{7,6},{8,9},{9,8},{10,11... | collective-permute-start | bytes 331784 | tf_op jit(solution)/shard_map/ppermute | solution.py:375
  36.7 0.0 copy-done.1
  36.7 1.9 %collective-permute-start.2 = (bf16[3,384,128]{2,1,0:T(8,128)(2,1)S(1)}, bf16[3,384,128]{2,1,0:T(8,128)(2,1)S(1)}, u32[]{:S(2)}, u32[]{:S(2)}) collective-permute-start(bf16[3,384,128]{2,1,0:T(8,128)(2,1)S(1)} %bitcast.40), channel_id=1, source_target_pairs={{0,1},{1,0},{2,3},{3,2},{4,5},{5,4},{6,7},{7,6},{8,9},{9,8},{10,11... | collective-permute-start | bytes 884744 | tf_op jit(solution)/shard_map/ppermute | solution.py:375
  38.6 0.0 copy-done.3
  38.6 2.4 %collective-permute-start.3 = (bf16[512,384]{1,0:T(8,128)(2,1)S(1)}, bf16[512,384]{1,0:T(8,128)(2,1)S(1)}, u32[]{:S(2)}, u32[]{:S(2)}) collective-permute-start(bf16[512,384]{1,0:T(8,128)(2,1)S(1)} %copy-done.3), channel_id=1, source_target_pairs={{0,1},{1,0},{2,3},{3,2},{4,5},{5,4},{6,7},{7,6},{8,9},{9,8},{10,11... | collective-permute-start | bytes 1179656 | tf_op jit(solution)/shard_map/ppermute | solution.py:375
  41.1 0.0 copy-done
  41.1 1.9 %collective-permute-start.1 = (bf16[384,512]{1,0:T(8,128)(2,1)S(1)}, bf16[384,512]{1,0:T(8,128)(2,1)S(1)}, u32[]{:S(2)}, u32[]{:S(2)}) collective-permute-start(bf16[384,512]{1,0:T(8,128)(2,1)S(1)} %copy-done), channel_id=1, source_target_pairs={{0,1},{1,0},{2,3},{3,2},{4,5},{5,4},{6,7},{7,6},{8,9},{9,8},{10,11... | collective-permute-start | bytes 1179656 | tf_op jit(solution)/shard_map/ppermute | solution.py:375
  43.0 0.3 fusion.12
  43.3 0.3 fusion.10
  43.5 0.0 collective-permute-done.other_out
  43.6 0.0 collective-permute-done.2.other_qkv
  43.6 0.2 copy.14
  43.8 0.4 convolution_reduce_fusion
  44.2 0.5 collective-permute-done.1.other_up
  44.7 0.3 fusion.13
  45.0 0.0 collective-permute-done.3.other_down
  45.0 0.3 all-to-all-done.1.pair
  45.3 1.3 %shard_map.128 = bf16[256,1792]{1,0:T(8,128)(2,1)S(1)} custom-call(s32[1]{0:T(128)} %bitcast.2.core, bf16[8,64,768]{2,1,0:T(8,128)(2,1)S(1)} %all-to-all-done.1.pair, f32[1,384]{1,0:T(1,128)S(1)} %reshape.66.own_gain, f32[1,384]{1,0:T(1,128)S(1)} %broadcast_in_dim.7.other_gain, bf16[384,512]{1,0:T(8,128)(2,1)S(1)} %copy-done, ...), custom_call_target="tpu_custom_call" | custom-call | flops 603979776 | bytes 4086788 | tf_op jit(solution)/shard_map/pallas_call | solution.py:323
  46.6 19.2 %all_to_all.51.got = bf16[8,32,1792]{2,1,0:T(8,128)(2,1)S(1)} all-to-all(bf16[8,32,1792]{2,1,0:T(8,128)(2,1)S(1)} %bitcast.38), channel_id=1, replica_groups={{12,14,8,10,4,6,0,2},{13,15,9,11,5,7,1,3},{28,30,24,26,20,22,16,18},{29..., dimensions={0} | all-to-all | bytes 1835008 | tf_op jit(solution)/shard_map/all_to_all | solution.py:340
  65.7 0.0 copy-start.5
  65.8 0.5 shard_map.129
  66.2 16.7 %all_to_all.52 = bf16[8,32,1664]{2,1,0:T(8,128)(2,1)S(1)} all-to-all(bf16[8,32,1664]{2,1,0:T(8,128)(2,1)S(1)} %get-tuple-element.20), channel_id=1, replica_groups={{12,14,8,10,4,6,0,2},{13,15,9,11,5,7,1,3},{28,30,24,26,20,22,16,18},{29..., dimensions={0} | all-to-all | bytes 1703936 | tf_op jit(solution)/shard_map/all_to_all | solution.py:340
  83.0 0.0 copy-done.5
  83.0 0.0 copy-done.6
  83.0 2.1 %shard_map.130 = (bf16[8,64,384]{2,1,0:T(8,128)(2,1)S(1)}, bf16[256,384]{1,0:T(8,128)(2,1)S(1)}, bf16[256,2304]{1,0:T(8,128)(2,1)S(1)}) custom-call(s32[1]{0:T(128)} %bitcast.2.core, bf16[256,1664]{1,0:T(8,128)(2,1)S(1)} %bitcast.39, bf16[8,64,768]{2,1,0:T(8,128)(2,1)S(1)} %all-to-all-done.1.pair, f32[1,384]{1,0:T(1,128)S(1)} %reshape.66.own_gain, ...), custom_call_target="tpu_custom_call" | custom-call | flops 469762048 | bytes 4792324 | tf_op jit(solution)/shard_map/pallas_call | solution.py:323
  85.0 0.0 copy-start.2
  85.1 0.7 copy-done.2
  85.8 3.8 %all-to-all-start.4 = ((bf16[8,64,384]{2,1,0:T(8,128)(2,1)}), bf16[8,64,384]{2,1,0:T(8,128)(2,1)S(1)}, u32[]{:S(2)}, u32[]{:S(2)}) async-start(bf16[8,64,384]{2,1,0:T(8,128)(2,1)} %copy-done.2), calls=%async_computation.4 | async-start | bytes 786432 | tf_op jit(solution)/shard_map/all_to_all | solution.py:340
  89.6 2.9 %collective-permute-start.4 = (bf16[256,2304]{1,0:T(8,128)(2,1)S(1)}, bf16[256,2304]{1,0:T(8,128)(2,1)}, u32[]{:S(2)}, u32[]{:S(2)}) collective-permute-start(bf16[256,2304]{1,0:T(8,128)(2,1)S(1)} %get-tuple-element.22.bundle), channel_id=1, source_target_pairs={{0,1},{1,0},{2,3},{3,2},{4,5},{5,4},{6,7},{7,6},{8,9},{9,8},{10,11... | collective-permute-start | bytes 3538952 | tf_op jit(solution)/shard_map/ppermute | solution.py:436
  92.5 4.3 %all-to-all-done.4 = bf16[8,64,384]{2,1,0:T(8,128)(2,1)S(1)} async-done(((bf16[8,64,384]{2,1,0:T(8,128)(2,1)}), bf16[8,64,384]{2,1,0:T(8,128)(2,1)S(1)}, u32[]{:S(2)}, u32[]{:S(2)}) %all-to-all-start.4) | async-done | bytes 393248 | tf_op jit(solution)/shard_map/all_to_all | solution.py:340
  96.8 0.7 shard_map.131
  97.5 9.9 %all-to-all-start.5 = ((bf16[8,16,384]{2,1,0:T(8,128)(2,1)}), bf16[8,16,384]{2,1,0:T(8,128)(2,1)S(1)}, u32[]{:S(2)}, u32[]{:S(2)}) async-start(bf16[8,16,384]{2,1,0:T(8,128)(2,1)} %bitcast.17), calls=%async_computation.5 | async-start | bytes 196608 | tf_op jit(solution)/shard_map/all_to_all | solution.py:340
  107.4 0.0 collective-permute-done.4.theirs
  107.4 3.0 %shard_map.132 = (bf16[3,384,128]{2,1,0:T(8,128)(2,1)}, bf16[128,384]{1,0:T(8,128)(2,1)}, bf16[384,512]{1,0:T(8,128)(2,1)}, bf16[512,384]{1,0:T(8,128)(2,1)}) custom-call(s32[1]{0:T(128)} %bitcast.2.core, bf16[256,2304]{1,0:T(8,128)(2,1)S(1)} %get-tuple-element.22.bundle, bf16[256,2304]{1,0:T(8,128)(2,1)} %collective-permute-done.4.theirs, ...), custom_call_target="tpu_custom_call" | custom-call | flops 603979776 | bytes 4521988 | tf_op jit(solution)/shard_map/pallas_call | solution.py:323
  110.4 3.0 %all-to-all-done.5 = bf16[8,16,384]{2,1,0:T(8,128)(2,1)S(1)} async-done(((bf16[8,16,384]{2,1,0:T(8,128)(2,1)}), bf16[8,16,384]{2,1,0:T(8,128)(2,1)S(1)}, u32[]{:S(2)}, u32[]{:S(2)}) %all-to-all-start.5) | async-done | bytes 98336 | tf_op jit(solution)/shard_map/all_to_all | solution.py:340
  113.4 0.6 reduce_sum.22
  (18 shorter events, 0.1 us)
Async XLA Ops:
  29.5 4.5 %copy-start.7 = (f32[384]{0:T(512)S(1)}, f32[384]{0:T(512)}, u32[]{:S(2)}) copy-start(f32[384]{0:T(512)} %param.11) | copy-start | bytes 4612
  29.5 4.6 %copy-start.4 = (bf16[128,384]{1,0:T(8,128)(2,1)S(1)}, bf16[128,384]{1,0:T(8,128)(2,1)}, u32[]{:S(2)}) copy-start(bf16[128,384]{1,0:T(8,128)(2,1)} %own_out.1) | copy-start | bytes 294916
  29.5 7.2 %copy-start.1 = (bf16[384,3,128]{2,0,1:T(8,128)(2,1)S(1)}, bf16[384,3,128]{2,0,1:T(8,128)(2,1)}, u32[]{:S(2)}) copy-start(bf16[384,3,128]{2,0,1:T(8,128)(2,1)} %param.12) | copy-start | bytes 884740
  29.5 9.1 %copy-start.3 = (bf16[512,384]{1,0:T(8,128)(2,1)S(1)}, bf16[512,384]{1,0:T(8,128)(2,1)}, u32[]{:S(2)}) copy-start(bf16[512,384]{1,0:T(8,128)(2,1)} %own_down.1) | copy-start | bytes 1179652
  29.5 11.5 %copy-start = (bf16[384,512]{1,0:T(8,128)(2,1)S(1)}, bf16[384,512]{1,0:T(8,128)(2,1)}, u32[]{:S(2)}) copy-start(bf16[384,512]{1,0:T(8,128)(2,1)} %own_up.3) | copy-start | bytes 1179652
  30.5 14.8 %all-to-all-start.1 = ((bf16[8,64,768]{2,1,0:T(8,128)(2,1)}), bf16[8,64,768]{2,1,0:T(8,128)(2,1)S(1)}, u32[]{:S(2)}, u32[]{:S(2)}) async-start(bf16[8,64,768]{2,1,0:T(8,128)(2,1)} %bitcast.47), calls=%async_computation.1 | async-start | bytes 1572864 | tf_op jit(solution)/shard_map/all_to_all | solution.py:340
  34.2 9.3 %collective-permute-start = (bf16[144,384]{1,0:T(8,128)(2,1)S(1)}, bf16[144,384]{1,0:T(8,128)(2,1)S(1)}, u32[]{:S(2)}, u32[]{:S(2)}) collective-permute-start(bf16[144,384]{1,0:T(8,128)(2,1)S(1)} %concatenate.28), channel_id=1, source_target_pairs={{0,1},{1,0},{2,3},{3,2},{4,5},{5,4},{6,7},{7,6},{8,9},{9,8},{10,11... | collective-permute-start | bytes 331784 | tf_op jit(solution)/shard_map/ppermute | solution.py:375
  36.7 6.9 %collective-permute-start.2 = (bf16[3,384,128]{2,1,0:T(8,128)(2,1)S(1)}, bf16[3,384,128]{2,1,0:T(8,128)(2,1)S(1)}, u32[]{:S(2)}, u32[]{:S(2)}) collective-permute-start(bf16[3,384,128]{2,1,0:T(8,128)(2,1)S(1)} %bitcast.40), channel_id=1, source_target_pairs={{0,1},{1,0},{2,3},{3,2},{4,5},{5,4},{6,7},{7,6},{8,9},{9,8},{10,11... | collective-permute-start | bytes 884744 | tf_op jit(solution)/shard_map/ppermute | solution.py:375
  38.6 6.3 %collective-permute-start.3 = (bf16[512,384]{1,0:T(8,128)(2,1)S(1)}, bf16[512,384]{1,0:T(8,128)(2,1)S(1)}, u32[]{:S(2)}, u32[]{:S(2)}) collective-permute-start(bf16[512,384]{1,0:T(8,128)(2,1)S(1)} %copy-done.3), channel_id=1, source_target_pairs={{0,1},{1,0},{2,3},{3,2},{4,5},{5,4},{6,7},{7,6},{8,9},{9,8},{10,11... | collective-permute-start | bytes 1179656 | tf_op jit(solution)/shard_map/ppermute | solution.py:375
  41.1 3.6 %collective-permute-start.1 = (bf16[384,512]{1,0:T(8,128)(2,1)S(1)}, bf16[384,512]{1,0:T(8,128)(2,1)S(1)}, u32[]{:S(2)}, u32[]{:S(2)}) collective-permute-start(bf16[384,512]{1,0:T(8,128)(2,1)S(1)} %copy-done), channel_id=1, source_target_pairs={{0,1},{1,0},{2,3},{3,2},{4,5},{5,4},{6,7},{7,6},{8,9},{9,8},{10,11... | collective-permute-start | bytes 1179656 | tf_op jit(solution)/shard_map/ppermute | solution.py:375
  65.7 17.2 %copy-start.5 = (f32[128]{0:T(128)S(1)}, f32[128]{0:T(128)}, u32[]{:S(2)}) copy-start(f32[128]{0:T(128)} %param.16) | copy-start | bytes 1540
  65.8 17.2 %copy-start.6 = (f32[128]{0:T(128)S(1)}, f32[128]{0:T(128)}, u32[]{:S(2)}) copy-start(f32[128]{0:T(128)} %param.17) | copy-start | bytes 1540
  85.0 0.7 copy-start.2
  85.8 11.0 %all-to-all-start.4 = ((bf16[8,64,384]{2,1,0:T(8,128)(2,1)}), bf16[8,64,384]{2,1,0:T(8,128)(2,1)S(1)}, u32[]{:S(2)}, u32[]{:S(2)}) async-start(bf16[8,64,384]{2,1,0:T(8,128)(2,1)} %copy-done.2), calls=%async_computation.4 | async-start | bytes 786432 | tf_op jit(solution)/shard_map/all_to_all | solution.py:340
  89.6 17.8 %collective-permute-start.4 = (bf16[256,2304]{1,0:T(8,128)(2,1)S(1)}, bf16[256,2304]{1,0:T(8,128)(2,1)}, u32[]{:S(2)}, u32[]{:S(2)}) collective-permute-start(bf16[256,2304]{1,0:T(8,128)(2,1)S(1)} %get-tuple-element.22.bundle), channel_id=1, source_target_pairs={{0,1},{1,0},{2,3},{3,2},{4,5},{5,4},{6,7},{7,6},{8,9},{9,8},{10,11... | collective-permute-start | bytes 3538952 | tf_op jit(solution)/shard_map/ppermute | solution.py:436
  97.5 15.9 %all-to-all-start.5 = ((bf16[8,16,384]{2,1,0:T(8,128)(2,1)}), bf16[8,16,384]{2,1,0:T(8,128)(2,1)S(1)}, u32[]{:S(2)}, u32[]{:S(2)}) async-start(bf16[8,16,384]{2,1,0:T(8,128)(2,1)} %bitcast.17), calls=%async_computation.5 | async-start | bytes 196608 | tf_op jit(solution)/shard_map/all_to_all | solution.py:340

commit v8 on v7

--- a/solution.py
+++ b/solution.py
@@ -16,7 +16,7 @@
 CHIPS = 8
 PAIRS = [5, 6, 7, 4, 0, 1, 2, 3]
 LAST = [5, 6, 7, 4, 0, 1, 2, 3]
-NEAR = [1, 0, 3, 2, 5, 4, 7, 6]
+NEAR = [3, 2, 1, 0, 7, 6, 5, 4]
 ACROSS = [6, 7, 4, 5, 2, 3, 0, 1]
 VMEM_BYTES = 24 * 1024 * 1024
 F32 = jnp.float32

time: 115 us -> 115 us (level)
  starting transfers between devices: 28.8 us -> 30.3 us
    all_to_all x3, starting transfers between devices: 17.2 us -> 19.4 us  [to_each(): lax.all_to_all(rows, axis, 0, 0, tiled=True, axis_index_groups=[order])]
  transfers between devices with their start and end apart: 8 -> 8, of which waited for: 4 -> 3; matrix products, arithmetic and copies ran while one was open for 1% -> 1% of each run, Pallas kernels for 3% -> 3%
where the time goes in v8:
time: 115 us; the launch traced here: 114 us
  blocking collectives  63.7 us (55%)
  starting transfers between devices  30.3 us (26%)
  Pallas kernels  7.52 us (7%)
  waiting for transfers between devices  7.36 us (6%)
  other arithmetic  2.36 us (2%)
  matrix products  1.17 us (1%)
    all_to_all x3, blocking collectives, to_each(): lax.all_to_all(rows, axis, 0, 0, tiled=True, axis_index_groups=[order])  63.7 us
    all_to_all x3, starting transfers between devices, to_each(): lax.all_to_all(rows, axis, 0, 0, tiled=True, axis_index_groups=[order])  19.4 us
    ppermute x4, starting transfers between devices, local(): lax.ppermute(w, 'core', swap)  8.64 us
    pallas_call x5, Pallas kernels, call(): pl.pallas_call(kernel, out_shape=outs, in_specs=[pl.BlockSpec(memory_spac...  7.52 us
    all_to_all x3, waiting for transfers between devices, to_each(): lax.all_to_all(rows, axis, 0, 0, tiled=True, axis_index_groups=[order])  6.96 us
    ppermute x1, starting transfers between devices, local(): theirs = lax.ppermute(bundle, 'core', swap)  2.33 us
  transfers between devices with their start and end apart: 8, of which 3 were waited for; matrix products, arithmetic and copies ran while one was open for 1% of the time, Pallas kernels for 3%

profile of v8, /device:TPU:1, one launch (start us, length us, event | category | flops | bytes accessed | tf_op | source)
XLA Modules:
  0.0 114.5 jit_solution(7006801064140557455)
XLA Ops:
  0.6 0.7 pad_maximum_fusion.1
  1.4 28.1 %all_to_all.50 = bf16[8,16,768]{2,1,0:T(8,128)(2,1)S(1)} all-to-all(bf16[8,16,768]{2,1,0:T(8,128)(2,1)S(1)} %broadcast_in_dim.6), channel_id=1, replica_groups={{320,384,448,256,0,64,128,192},{321,385,449,257,1,65,129,193},{322,386,..., dimensions={0} | all-to-all | bytes 393216 | tf_op jit(solution)/shard_map/all_to_all | solution.py:340
  29.5 0.0 copy-start.7
  29.5 0.0 copy-start.4
  29.5 0.0 copy-start.1
  29.5 0.0 copy-start.3
  29.5 0.0 copy-start
  29.5 1.0 pad_maximum_fusion
  30.5 4.8 %all-to-all-start.1 = ((bf16[8,64,768]{2,1,0:T(8,128)(2,1)}), bf16[8,64,768]{2,1,0:T(8,128)(2,1)S(1)}, u32[]{:S(2)}, u32[]{:S(2)}) async-start(bf16[8,64,768]{2,1,0:T(8,128)(2,1)} %bitcast.47), calls=%async_computation.1 | async-start | bytes 1572864 | tf_op jit(solution)/shard_map/all_to_all | solution.py:340
  35.3 0.0 copy-done.7
  35.3 0.0 copy-done.4
  35.3 0.1 concatenate.28
  35.4 2.3 %collective-permute-start = (bf16[144,384]{1,0:T(8,128)(2,1)S(1)}, bf16[144,384]{1,0:T(8,128)(2,1)S(1)}, u32[]{:S(2)}, u32[]{:S(2)}) collective-permute-start(bf16[144,384]{1,0:T(8,128)(2,1)S(1)} %concatenate.28), channel_id=1, source_target_pairs={{0,1},{1,0},{2,3},{3,2},{4,5},{5,4},{6,7},{7,6},{8,9},{9,8},{10,11... | collective-permute-start | bytes 331784 | tf_op jit(solution)/shard_map/ppermute | solution.py:375
  37.8 0.0 copy-done.1
  37.8 2.0 %collective-permute-start.2 = (bf16[3,384,128]{2,1,0:T(8,128)(2,1)S(1)}, bf16[3,384,128]{2,1,0:T(8,128)(2,1)S(1)}, u32[]{:S(2)}, u32[]{:S(2)}) collective-permute-start(bf16[3,384,128]{2,1,0:T(8,128)(2,1)S(1)} %bitcast.40), channel_id=1, source_target_pairs={{0,1},{1,0},{2,3},{3,2},{4,5},{5,4},{6,7},{7,6},{8,9},{9,8},{10,11... | collective-permute-start | bytes 884744 | tf_op jit(solution)/shard_map/ppermute | solution.py:375
  39.8 0.0 copy-done.3
  39.8 2.3 %collective-permute-start.3 = (bf16[512,384]{1,0:T(8,128)(2,1)S(1)}, bf16[512,384]{1,0:T(8,128)(2,1)S(1)}, u32[]{:S(2)}, u32[]{:S(2)}) collective-permute-start(bf16[512,384]{1,0:T(8,128)(2,1)S(1)} %copy-done.3), channel_id=1, source_target_pairs={{0,1},{1,0},{2,3},{3,2},{4,5},{5,4},{6,7},{7,6},{8,9},{9,8},{10,11... | collective-permute-start | bytes 1179656 | tf_op jit(solution)/shard_map/ppermute | solution.py:375
  42.1 0.0 copy-done
  42.1 2.0 %collective-permute-start.1 = (bf16[384,512]{1,0:T(8,128)(2,1)S(1)}, bf16[384,512]{1,0:T(8,128)(2,1)S(1)}, u32[]{:S(2)}, u32[]{:S(2)}) collective-permute-start(bf16[384,512]{1,0:T(8,128)(2,1)S(1)} %copy-done), channel_id=1, source_target_pairs={{0,1},{1,0},{2,3},{3,2},{4,5},{5,4},{6,7},{7,6},{8,9},{9,8},{10,11... | collective-permute-start | bytes 1179656 | tf_op jit(solution)/shard_map/ppermute | solution.py:375
  44.1 0.3 fusion.12
  44.4 0.3 fusion.10
  44.7 0.0 collective-permute-done.other_out
  44.7 0.0 collective-permute-done.2.other_qkv
  44.7 0.2 copy.14
  45.0 0.4 convolution_reduce_fusion
  45.4 0.4 collective-permute-done.1.other_up
  45.7 0.3 fusion.13
  46.0 0.0 collective-permute-done.3.other_down
  46.1 0.0 all-to-all-done.1.pair
  46.1 1.3 %shard_map.128 = bf16[256,1792]{1,0:T(8,128)(2,1)S(1)} custom-call(s32[1]{0:T(128)} %bitcast.2.core, bf16[8,64,768]{2,1,0:T(8,128)(2,1)S(1)} %all-to-all-done.1.pair, f32[1,384]{1,0:T(1,128)S(1)} %reshape.66.own_gain, f32[1,384]{1,0:T(1,128)S(1)} %broadcast_in_dim.7.other_gain, bf16[384,512]{1,0:T(8,128)(2,1)S(1)} %copy-done, ...), custom_call_target="tpu_custom_call" | custom-call | flops 603979776 | bytes 4086788 | tf_op jit(solution)/shard_map/pallas_call | solution.py:323
  47.4 18.7 %all_to_all.51.got = bf16[8,32,1792]{2,1,0:T(8,128)(2,1)S(1)} all-to-all(bf16[8,32,1792]{2,1,0:T(8,128)(2,1)S(1)} %bitcast.38), channel_id=1, replica_groups={{12,14,8,10,4,6,0,2},{13,15,9,11,5,7,1,3},{28,30,24,26,20,22,16,18},{29..., dimensions={0} | all-to-all | bytes 1835008 | tf_op jit(solution)/shard_map/all_to_all | solution.py:340
  66.0 0.0 copy-start.5
  66.0 0.5 shard_map.129
  66.5 16.9 %all_to_all.52 = bf16[8,32,1664]{2,1,0:T(8,128)(2,1)S(1)} all-to-all(bf16[8,32,1664]{2,1,0:T(8,128)(2,1)S(1)} %get-tuple-element.20), channel_id=1, replica_groups={{12,14,8,10,4,6,0,2},{13,15,9,11,5,7,1,3},{28,30,24,26,20,22,16,18},{29..., dimensions={0} | all-to-all | bytes 1703936 | tf_op jit(solution)/shard_map/all_to_all | solution.py:340
  83.4 0.0 copy-done.5
  83.4 0.0 copy-done.6
  83.4 2.1 %shard_map.130 = (bf16[8,64,384]{2,1,0:T(8,128)(2,1)S(1)}, bf16[256,384]{1,0:T(8,128)(2,1)S(1)}, bf16[256,2304]{1,0:T(8,128)(2,1)S(1)}) custom-call(s32[1]{0:T(128)} %bitcast.2.core, bf16[256,1664]{1,0:T(8,128)(2,1)S(1)} %bitcast.39, bf16[8,64,768]{2,1,0:T(8,128)(2,1)S(1)} %all-to-all-done.1.pair, f32[1,384]{1,0:T(1,128)S(1)} %reshape.66.own_gain, ...), custom_call_target="tpu_custom_call" | custom-call | flops 469762048 | bytes 4792324 | tf_op jit(solution)/shard_map/pallas_call | solution.py:323
  85.5 0.0 copy-start.2
  85.5 0.7 copy-done.2
  86.2 4.9 %all-to-all-start.4 = ((bf16[8,64,384]{2,1,0:T(8,128)(2,1)}), bf16[8,64,384]{2,1,0:T(8,128)(2,1)S(1)}, u32[]{:S(2)}, u32[]{:S(2)}) async-start(bf16[8,64,384]{2,1,0:T(8,128)(2,1)} %copy-done.2), calls=%async_computation.4 | async-start | bytes 786432 | tf_op jit(solution)/shard_map/all_to_all | solution.py:340
  91.2 2.3 %collective-permute-start.4 = (bf16[256,2304]{1,0:T(8,128)(2,1)S(1)}, bf16[256,2304]{1,0:T(8,128)(2,1)}, u32[]{:S(2)}, u32[]{:S(2)}) collective-permute-start(bf16[256,2304]{1,0:T(8,128)(2,1)S(1)} %get-tuple-element.22.bundle), channel_id=1, source_target_pairs={{0,1},{1,0},{2,3},{3,2},{4,5},{5,4},{6,7},{7,6},{8,9},{9,8},{10,11... | collective-permute-start | bytes 3538952 | tf_op jit(solution)/shard_map/ppermute | solution.py:436
  93.5 3.7 %all-to-all-done.4 = bf16[8,64,384]{2,1,0:T(8,128)(2,1)S(1)} async-done(((bf16[8,64,384]{2,1,0:T(8,128)(2,1)}), bf16[8,64,384]{2,1,0:T(8,128)(2,1)S(1)}, u32[]{:S(2)}, u32[]{:S(2)}) %all-to-all-start.4) | async-done | bytes 393248 | tf_op jit(solution)/shard_map/all_to_all | solution.py:340
  97.2 0.7 shard_map.131
  97.9 9.7 %all-to-all-start.5 = ((bf16[8,16,384]{2,1,0:T(8,128)(2,1)}), bf16[8,16,384]{2,1,0:T(8,128)(2,1)S(1)}, u32[]{:S(2)}, u32[]{:S(2)}) async-start(bf16[8,16,384]{2,1,0:T(8,128)(2,1)} %bitcast.17), calls=%async_computation.5 | async-start | bytes 196608 | tf_op jit(solution)/shard_map/all_to_all | solution.py:340
  107.6 0.0 collective-permute-done.4.theirs
  107.6 3.0 %shard_map.132 = (bf16[3,384,128]{2,1,0:T(8,128)(2,1)}, bf16[128,384]{1,0:T(8,128)(2,1)}, bf16[384,512]{1,0:T(8,128)(2,1)}, bf16[512,384]{1,0:T(8,128)(2,1)}) custom-call(s32[1]{0:T(128)} %bitcast.2.core, bf16[256,2304]{1,0:T(8,128)(2,1)S(1)} %get-tuple-element.22.bundle, bf16[256,2304]{1,0:T(8,128)(2,1)} %collective-permute-done.4.theirs, ...), custom_call_target="tpu_custom_call" | custom-call | flops 603979776 | bytes 4521988 | tf_op jit(solution)/shard_map/pallas_call | solution.py:323
  110.6 3.3 %all-to-all-done.5 = bf16[8,16,384]{2,1,0:T(8,128)(2,1)S(1)} async-done(((bf16[8,16,384]{2,1,0:T(8,128)(2,1)}), bf16[8,16,384]{2,1,0:T(8,128)(2,1)S(1)}, u32[]{:S(2)}, u32[]{:S(2)}) %all-to-all-start.5) | async-done | bytes 98336 | tf_op jit(solution)/shard_map/all_to_all | solution.py:340
  113.8 0.6 reduce_sum.22
  (18 shorter events, 0.1 us)
Async XLA Ops:
  29.5 5.7 %copy-start.7 = (f32[384]{0:T(512)S(1)}, f32[384]{0:T(512)}, u32[]{:S(2)}) copy-start(f32[384]{0:T(512)} %param.11) | copy-start | bytes 4612
  29.5 5.8 %copy-start.4 = (bf16[128,384]{1,0:T(8,128)(2,1)S(1)}, bf16[128,384]{1,0:T(8,128)(2,1)}, u32[]{:S(2)}) copy-start(bf16[128,384]{1,0:T(8,128)(2,1)} %own_out.1) | copy-start | bytes 294916
  29.5 8.2 %copy-start.1 = (bf16[384,3,128]{2,0,1:T(8,128)(2,1)S(1)}, bf16[384,3,128]{2,0,1:T(8,128)(2,1)}, u32[]{:S(2)}) copy-start(bf16[384,3,128]{2,0,1:T(8,128)(2,1)} %param.12) | copy-start | bytes 884740
  29.5 10.2 %copy-start.3 = (bf16[512,384]{1,0:T(8,128)(2,1)S(1)}, bf16[512,384]{1,0:T(8,128)(2,1)}, u32[]{:S(2)}) copy-start(bf16[512,384]{1,0:T(8,128)(2,1)} %own_down.1) | copy-start | bytes 1179652
  29.5 12.6 %copy-start = (bf16[384,512]{1,0:T(8,128)(2,1)S(1)}, bf16[384,512]{1,0:T(8,128)(2,1)}, u32[]{:S(2)}) copy-start(bf16[384,512]{1,0:T(8,128)(2,1)} %own_up.3) | copy-start | bytes 1179652
  30.5 15.6 %all-to-all-start.1 = ((bf16[8,64,768]{2,1,0:T(8,128)(2,1)}), bf16[8,64,768]{2,1,0:T(8,128)(2,1)S(1)}, u32[]{:S(2)}, u32[]{:S(2)}) async-start(bf16[8,64,768]{2,1,0:T(8,128)(2,1)} %bitcast.47), calls=%async_computation.1 | async-start | bytes 1572864 | tf_op jit(solution)/shard_map/all_to_all | solution.py:340
  35.4 9.2 %collective-permute-start = (bf16[144,384]{1,0:T(8,128)(2,1)S(1)}, bf16[144,384]{1,0:T(8,128)(2,1)S(1)}, u32[]{:S(2)}, u32[]{:S(2)}) collective-permute-start(bf16[144,384]{1,0:T(8,128)(2,1)S(1)} %concatenate.28), channel_id=1, source_target_pairs={{0,1},{1,0},{2,3},{3,2},{4,5},{5,4},{6,7},{7,6},{8,9},{9,8},{10,11... | collective-permute-start | bytes 331784 | tf_op jit(solution)/shard_map/ppermute | solution.py:375
  37.8 7.0 %collective-permute-start.2 = (bf16[3,384,128]{2,1,0:T(8,128)(2,1)S(1)}, bf16[3,384,128]{2,1,0:T(8,128)(2,1)S(1)}, u32[]{:S(2)}, u32[]{:S(2)}) collective-permute-start(bf16[3,384,128]{2,1,0:T(8,128)(2,1)S(1)} %bitcast.40), channel_id=1, source_target_pairs={{0,1},{1,0},{2,3},{3,2},{4,5},{5,4},{6,7},{7,6},{8,9},{9,8},{10,11... | collective-permute-start | bytes 884744 | tf_op jit(solution)/shard_map/ppermute | solution.py:375
  39.8 6.3 %collective-permute-start.3 = (bf16[512,384]{1,0:T(8,128)(2,1)S(1)}, bf16[512,384]{1,0:T(8,128)(2,1)S(1)}, u32[]{:S(2)}, u32[]{:S(2)}) collective-permute-start(bf16[512,384]{1,0:T(8,128)(2,1)S(1)} %copy-done.3), channel_id=1, source_target_pairs={{0,1},{1,0},{2,3},{3,2},{4,5},{5,4},{6,7},{7,6},{8,9},{9,8},{10,11... | collective-permute-start | bytes 1179656 | tf_op jit(solution)/shard_map/ppermute | solution.py:375
  42.1 3.6 %collective-permute-start.1 = (bf16[384,512]{1,0:T(8,128)(2,1)S(1)}, bf16[384,512]{1,0:T(8,128)(2,1)S(1)}, u32[]{:S(2)}, u32[]{:S(2)}) collective-permute-start(bf16[384,512]{1,0:T(8,128)(2,1)S(1)} %copy-done), channel_id=1, source_target_pairs={{0,1},{1,0},{2,3},{3,2},{4,5},{5,4},{6,7},{7,6},{8,9},{9,8},{10,11... | collective-permute-start | bytes 1179656 | tf_op jit(solution)/shard_map/ppermute | solution.py:375
  66.0 17.4 %copy-start.5 = (f32[128]{0:T(128)S(1)}, f32[128]{0:T(128)}, u32[]{:S(2)}) copy-start(f32[128]{0:T(128)} %param.16) | copy-start | bytes 1540
  66.0 17.4 %copy-start.6 = (f32[128]{0:T(128)S(1)}, f32[128]{0:T(128)}, u32[]{:S(2)}) copy-start(f32[128]{0:T(128)} %param.17) | copy-start | bytes 1540
  85.5 0.7 copy-start.2
  86.2 11.0 %all-to-all-start.4 = ((bf16[8,64,384]{2,1,0:T(8,128)(2,1)}), bf16[8,64,384]{2,1,0:T(8,128)(2,1)S(1)}, u32[]{:S(2)}, u32[]{:S(2)}) async-start(bf16[8,64,384]{2,1,0:T(8,128)(2,1)} %copy-done.2), calls=%async_computation.4 | async-start | bytes 786432 | tf_op jit(solution)/shard_map/all_to_all | solution.py:340
  91.2 16.4 %collective-permute-start.4 = (bf16[256,2304]{1,0:T(8,128)(2,1)S(1)}, bf16[256,2304]{1,0:T(8,128)(2,1)}, u32[]{:S(2)}, u32[]{:S(2)}) collective-permute-start(bf16[256,2304]{1,0:T(8,128)(2,1)S(1)} %get-tuple-element.22.bundle), channel_id=1, source_target_pairs={{0,1},{1,0},{2,3},{3,2},{4,5},{5,4},{6,7},{7,6},{8,9},{9,8},{10,11... | collective-permute-start | bytes 3538952 | tf_op jit(solution)/shard_map/ppermute | solution.py:436
  97.9 15.9 %all-to-all-start.5 = ((bf16[8,16,384]{2,1,0:T(8,128)(2,1)}), bf16[8,16,384]{2,1,0:T(8,128)(2,1)S(1)}, u32[]{:S(2)}, u32[]{:S(2)}) async-start(bf16[8,16,384]{2,1,0:T(8,128)(2,1)} %bitcast.17), calls=%async_computation.5 | async-start | bytes 196608 | tf_op jit(solution)/shard_map/all_to_all | solution.py:340
